TPU v7x, 32 devices: a whole 2x2x4 slice. The times are simulated.
32 devices in a mesh: seq: 32 (over z, y, x, core).
Axes of the slice: x: 2, y: 2, z: 4, core: 2. Of those that a mesh axis runs over, the one named last changes fastest.
Arguments:
- hidden: bfloat16 [8192, 1024], P('seq'), may hold values from -6 to 6
- segment_ids: int32 [8192], P('seq'), may hold values from 0 to 2, as said below
- in_weight: bfloat16 [2, 1024, 4384], P(None, 'seq'), may hold values from -0.1875 to 0.1875
- out_weight: bfloat16 [2, 2048, 1024], P(None, 'seq'), may hold values from -0.125 to 0.125
- conv_weight: bfloat16 [2, 4, 2304], P(None, None, 'seq'), may hold values from -3 to 3
- conv_bias: bfloat16 [2, 2304], P(None, 'seq'), may hold values from -3 to 3
- norm_gain: bfloat16 [2, 1024], P(None, 'seq'), may hold values from 0.099609375 to 1.8984375
- gate_gain: bfloat16 [2, 2048], P(None, 'seq'), may hold values from 0.099609375 to 1.8984375
- dt_bias: float32 [2, 32], replicated, may hold values from -6.9 to -2.3
- a_log: float32 [2, 32], replicated, may hold values from -5 to 1
- skip_param: float32 [2, 32], replicated, may hold values from 0.5 to 1.5
- cotangent: float32 [8192, 1024], P('seq'), may hold values from -6 to 6
Outputs:
- final_hidden: float32 [8192, 1024], P('seq')
- hidden_grad: float32 [8192, 1024], P('seq')
- in_weight_grad: float32 [2, 1024, 4384], P(None, 'seq')
- out_weight_grad: float32 [2, 2048, 1024], P(None, 'seq')
- conv_weight_grad: float32 [2, 4, 2304], P(None, None, 'seq')
- conv_bias_grad: float32 [2, 2304], P(None, 'seq')
- norm_gain_grad: float32 [2, 1024], P(None, 'seq')
- gate_gain_grad: float32 [2, 2048], P(None, 'seq')
- dt_bias_grad: float32 [2, 32], replicated
- a_log_grad: float32 [2, 32], replicated
- skip_grad: float32 [2, 32], replicated
Inputs may be any that keep to these rules, and one draw needn't show every extreme that they name: `segment_ids`: ids never fall along the tokens and every id from 0 to 2 is used; document 0 ends within the first 256 tokens and document 2 begins within the last 256 tokens.
All inputs are finite; a program needn't handle non-finite values.
Results may differ from a plain program's by a relative error of at most 0.015.
Values may be sent and summed in bfloat16 or wider, within the bound.
No kernel may reach another device: no remote copies, remote signals or barrier semaphores. Data moves between devices by JAX's collectives and lax.ppermute only.
A program may use at most 512 MiB of HBM per device.

v0:
```python
from functools import partial

import jax
import jax.numpy as jnp
from jax import lax
from jax.sharding import PartitionSpec as P

HEADS = 32
HEAD_DIM = 64
STATE = 128
CONV_K = 4
INNER = 2048
CONV_CH = 2304


EPS = 1e-05
PRECISE = lax.Precision.HIGHEST


def shifted(shard, axis, by):
    length = lax.axis_size(axis)
    pairs = [(i, i + by) for i in range(length) if 0 <= i + by < length]
    return lax.ppermute(shard, axis, pairs)


def prefix(value, axis, join, neutral):
    count, mine = (lax.axis_size(axis), lax.axis_index(axis))
    pieces = jax.tree.map(lambda part: lax.all_gather(part, axis), value)
    so_far = jax.tree.map(
        lambda part, zero: jnp.full_like(part, 0) + jnp.asarray(zero, part.dtype), value, neutral
    )

    def lap(position, so_far):
        longer = join(so_far, jax.tree.map(lambda part: part[position], pieces))
        return jax.tree.map(lambda new, old: jnp.where(position < mine, new, old), longer, so_far)

    return lax.fori_loop(0, count - 1, lap, so_far)


def carried_in(shard, axis, join, neutral):
    count = lax.axis_size(axis)
    place = lax.axis_index(axis)
    ahead = count - 1 - place
    gathered = jax.tree.map(
        lambda a, kind: lax.all_gather(a.astype(kind), axis),
        shard,
        jax.tree.map(lambda a: jnp.bfloat16 if a.dtype == jnp.float32 else a.dtype, shard),
    )
    state = jax.tree.map(lambda a, e: jnp.zeros_like(a) + jnp.asarray(e, a.dtype), shard, neutral)

    def one(lap, state):
        source = count - 1 - lap
        return join(
            state,
            jax.tree.map(
                lambda a, own: lax.dynamic_index_in_dim(a, source, 0, False).astype(own.dtype),
                gathered,
                shard,
            ),
        )

    return lax.fori_loop(0, ahead, one, state)


def norm_input(residual, norm_g):
    inv_rms = lax.rsqrt(jnp.mean(residual * residual, axis=-1, keepdims=True) + EPS)
    return residual * inv_rms * norm_g


def conv_mix(padded, dt_raw, conv_w, conv_b, dt_b, a_lg, seg_pad):
    tokens_n = dt_raw.shape[0]
    own_segs = seg_pad[CONV_K - 1 :]
    conv_out = jnp.zeros((tokens_n, conv_w.shape[1]), jnp.float32) + conv_b
    for offset in range(CONV_K):
        same_doc = (seg_pad[offset : offset + tokens_n] == own_segs).astype(jnp.float32)
        conv_out = (
            conv_out + conv_w[offset] * padded[offset : offset + tokens_n] * same_doc[:, None]
        )
    activated = jax.nn.silu(conv_out)
    head_in = activated[:, :INNER].reshape(tokens_n, HEADS, HEAD_DIM)
    b_rows = activated[:, INNER : INNER + STATE]
    c_rows = activated[:, INNER + STATE :]
    step_size = jax.nn.softplus(dt_raw + dt_b)
    return (head_in, b_rows, c_rows, step_size, -jnp.exp(a_lg))


def ssd_local(head_in, b_rows, c_rows, step_size, decay_rate, state_in, segments, before):
    log_decay = jnp.cumsum(step_size * decay_rate, axis=0)
    length = segments.shape[0]
    positions = jnp.arange(length)
    allowed = (positions[:, None] >= positions[None, :]) & (segments[:, None] == segments[None, :])
    allowed_cube = allowed[:, :, None]
    spread = jnp.where(allowed_cube, log_decay[:, None, :] - log_decay[None, :, :], 0.0)
    decayed = jnp.where(allowed_cube, jnp.exp(spread), 0.0)
    scores = jnp.einsum("tn,sn->ts", c_rows, b_rows, precision=PRECISE)
    mixing = scores[:, :, None] * decayed * step_size[None, :, :]
    within = jnp.einsum("tsh,shp->thp", mixing, head_in, precision=PRECISE)
    carry_on = (segments == before).astype(jnp.float32)
    inflow = jnp.exp(log_decay) * carry_on[:, None]
    return within + inflow[:, :, None] * jnp.einsum(
        "tn,hpn->thp", c_rows, state_in, precision=PRECISE
    )


def state_local(head_in, b_rows, step_size, decay_rate, segments, before):
    log_decay = jnp.cumsum(step_size * decay_rate, axis=0)
    tail_doc = (segments == segments[-1]).astype(jnp.float32)
    weight_last = tail_doc[:, None] * jnp.exp(log_decay[-1][None, :] - log_decay) * step_size
    keep_all = jnp.exp(log_decay[-1]) * (segments[-1] == before).astype(jnp.float32)
    local_state = jnp.einsum("sh,shp,sn->hpn", weight_last, head_in, b_rows, precision=PRECISE)
    return (keep_all, local_state)


def post_mix(y_out, head_in, gate_z, skip_d, gate_g):
    tokens_n = gate_z.shape[0]
    y_full = (y_out + skip_d[:, None] * head_in).reshape(tokens_n, INNER)
    gated = y_full * jax.nn.silu(gate_z)
    inv_rms = lax.rsqrt(jnp.mean(gated * gated, axis=-1, keepdims=True) + EPS)
    return gated * inv_rms * gate_g


def combine_state(earlier, later):
    return (earlier[0] * later[0], later[0][:, None, None] * earlier[1] + later[1])


def stack_kind(entries, kind_pos):
    return jnp.stack([entry[kind_pos] for entry in entries])


def per_device(
    hidden,
    segment_ids,
    in_weight,
    out_weight,
    conv_weight,
    conv_bias,
    norm_gain,
    gate_gain,
    dt_bias,
    a_log,
    skip_param,
    cotangent,
):
    layers_n = in_weight.shape[0]
    tokens_n = hidden.shape[0]
    halo_n = CONV_K - 1
    seg_tail = (segment_ids[tokens_n - halo_n :] + 1).astype(jnp.bfloat16)
    residual = hidden.astype(jnp.float32)
    saved = []
    saved_weights = []
    for layer_idx in range(layers_n):
        shards = (
            in_weight[layer_idx],
            out_weight[layer_idx],
            conv_weight[layer_idx],
            conv_bias[layer_idx],
            norm_gain[layer_idx],
            gate_gain[layer_idx],
        )
        gathered = (
            lax.all_gather(shards[0], "seq", axis=0, tiled=True),
            lax.all_gather(shards[1], "seq", axis=0, tiled=True),
            lax.all_gather(shards[2], "seq", axis=1, tiled=True),
            lax.all_gather(shards[3], "seq", axis=0, tiled=True),
            lax.all_gather(shards[4], "seq", axis=0, tiled=True),
            lax.all_gather(shards[5], "seq", axis=0, tiled=True),
        )
        in_w, out_w, conv_w, conv_b, norm_g, gate_g = gathered
        normed_pre, pull_norm = jax.vjp(norm_input, residual, norm_g.astype(jnp.float32))
        normed = normed_pre.astype(jnp.bfloat16)
        projected = jnp.dot(normed, in_w, preferred_element_type=jnp.float32).astype(jnp.bfloat16)
        conv_in = projected[:, INNER : INNER + CONV_CH]
        edge_rows, edge_segs = shifted((conv_in[tokens_n - halo_n :], seg_tail), "seq", 1)
        seg_before = edge_segs.astype(jnp.int32) - 1
        seg_pad = jnp.concatenate([seg_before, segment_ids])
        before = seg_before[halo_n - 1]
        padded = jnp.concatenate([edge_rows, conv_in], axis=0).astype(jnp.float32)
        mix_fn = partial(conv_mix, seg_pad=seg_pad)
        mixed, pull_mix = jax.vjp(
            mix_fn,
            padded,
            projected[:, INNER + CONV_CH :].astype(jnp.float32),
            conv_w.astype(jnp.float32),
            conv_b.astype(jnp.float32),
            dt_bias[layer_idx],
            a_log[layer_idx],
        )
        head_in, b_rows, c_rows, step_size, decay_rate = mixed
        state_fn = partial(state_local, segments=segment_ids, before=before)
        (keep_all, local_state), pull_state = jax.vjp(
            state_fn, head_in, b_rows, step_size, decay_rate
        )
        identity = (jnp.ones_like(keep_all), jnp.zeros_like(local_state))
        state_in = prefix((keep_all, local_state), "seq", combine_state, identity)[1]
        ssd_fn = jax.checkpoint(partial(ssd_local, segments=segment_ids, before=before))
        y_out, pull_ssd = jax.vjp(ssd_fn, head_in, b_rows, c_rows, step_size, decay_rate, state_in)
        gated_pre, pull_post = jax.vjp(
            post_mix,
            y_out,
            head_in,
            projected[:, :INNER].astype(jnp.float32),
            skip_param[layer_idx],
            gate_g.astype(jnp.float32),
        )
        gnormed = gated_pre.astype(jnp.bfloat16)
        residual = residual + jnp.dot(gnormed, out_w, preferred_element_type=jnp.float32)
        saved.append(
            (
                normed,
                gnormed,
                keep_all,
                state_in,
                identity,
                pull_norm,
                pull_mix,
                pull_state,
                pull_ssd,
                pull_post,
            )
        )
        saved_weights.append((in_w, out_w))
    grad_resid = cotangent
    head_terms = [None] * layers_n
    shares = [None] * layers_n
    for layer_idx in range(layers_n - 1, -1, -1):
        (
            normed,
            gnormed,
            keep_all,
            state_in,
            identity,
            pull_norm,
            pull_mix,
            pull_state,
            pull_ssd,
            pull_post,
        ) = saved[layer_idx]
        in_w, out_w = saved_weights[layer_idx]
        grad_mixed = grad_resid.astype(jnp.bfloat16)
        out_term = jnp.einsum("ti,td->id", gnormed, grad_mixed, preferred_element_type=jnp.float32)
        grad_gnormed = jnp.einsum(
            "td,id->ti", grad_mixed, out_w, preferred_element_type=jnp.float32
        )
        grad_y, grad_head_post, grad_gate_z, grad_skip, grad_gate_g = pull_post(grad_gnormed)
        grad_head_ssd, grad_b_ssd, grad_c, grad_step_ssd, grad_rate_ssd, grad_state_in = pull_ssd(
            grad_y
        )
        grad_after = carried_in((keep_all, grad_state_in), "seq", combine_state, identity)[1]
        grad_keep = jnp.sum(grad_after * state_in, axis=(1, 2))
        grad_head_st, grad_b_st, grad_step_st, grad_rate_st = pull_state((grad_keep, grad_after))
        grad_pad, grad_dt_raw, grad_conv_w, grad_conv_b, grad_dt_bias, grad_a_log = pull_mix(
            (
                grad_head_post + grad_head_ssd + grad_head_st,
                grad_b_ssd + grad_b_st,
                grad_c,
                grad_step_ssd + grad_step_st,
                grad_rate_ssd + grad_rate_st,
            )
        )
        spilled = shifted(grad_pad[:halo_n], "seq", -1)
        grad_conv_in = grad_pad[halo_n:].at[tokens_n - halo_n :].add(spilled)
        grad_proj = jnp.concatenate([grad_gate_z, grad_conv_in, grad_dt_raw], axis=1).astype(
            jnp.bfloat16
        )
        in_term = jnp.einsum("td,tk->dk", normed, grad_proj, preferred_element_type=jnp.float32)
        grad_normed = jnp.einsum("tk,dk->td", grad_proj, in_w, preferred_element_type=jnp.float32)
        grad_resid_in, grad_norm_g = pull_norm(grad_normed)
        grad_resid = grad_resid + grad_resid_in
        head_terms[layer_idx] = (grad_dt_bias, grad_a_log, grad_skip)
        shares[layer_idx] = (
            lax.psum_scatter(in_term, "seq", scatter_dimension=0, tiled=True),
            lax.psum_scatter(out_term, "seq", scatter_dimension=0, tiled=True),
            lax.psum_scatter(grad_conv_w, "seq", scatter_dimension=1, tiled=True),
            lax.psum_scatter(grad_conv_b, "seq", scatter_dimension=0, tiled=True),
            lax.psum_scatter(grad_norm_g, "seq", scatter_dimension=0, tiled=True),
            lax.psum_scatter(grad_gate_g, "seq", scatter_dimension=0, tiled=True),
        )
    stacked = (
        stack_kind(shares, 0),
        stack_kind(shares, 1),
        stack_kind(shares, 2),
        stack_kind(shares, 3),
        stack_kind(shares, 4),
        stack_kind(shares, 5),
    )
    head_sums = lax.psum(
        (stack_kind(head_terms, 0), stack_kind(head_terms, 1), stack_kind(head_terms, 2)), "seq"
    )
    return (
        residual,
        grad_resid,
        stacked[0],
        stacked[1],
        stacked[2],
        stacked[3],
        stacked[4],
        stacked[5],
        head_sums[0],
        head_sums[1],
        head_sums[2],
    )


def solution(mesh):
    return jax.shard_map(
        per_device,
        mesh=mesh,
        in_specs=(
            P("seq", None),
            P("seq"),
            P(None, "seq", None),
            P(None, "seq", None),
            P(None, None, "seq"),
            P(None, "seq"),
            P(None, "seq"),
            P(None, "seq"),
            P(),
            P(),
            P(),
            P("seq", None),
        ),
        out_specs=(
            P("seq", None),
            P("seq", None),
            P(None, "seq", None),
            P(None, "seq", None),
            P(None, None, "seq"),
            P(None, "seq"),
            P(None, "seq"),
            P(None, "seq"),
            P(),
            P(),
            P(),
        ),
        check_vma=False,
    )
```

profile of v0, /device:TPU:0, one launch (start us, length us, event | category | flops | bytes accessed | tf_op | source)
XLA Modules:
  0.0 2185.0 jit_solution(9949622248275633545)
XLA Ops:
  17.2 42.6 %all-reduce.41 = (bf16[1024]{0:T(1024)(128)(2,1)S(1)}, bf16[2304]{0:T(1024)(128)(2,1)S(1)}, bf16[2048]{0:T(1024)(128)(2,1)}, bf16[1024]{0:T(1024)(128)(2,1)}, bf...) all-reduce(bf16[1024]{0:T(1024)(128)(2,1)S(1)} %dynamic-update-slice.7, ...), channel_id=4, replica_groups=mesh['seq'=32] {'seq'}, use_global_device_ids=true, to_apply=%add.27 | all-reduce | flops 10752 | bytes 43008
  61.7 49.1 %all-gather.1 = bf16[1,4,2304]{1,0,2:T(2,128)(2,1)S(1)} all-gather(bf16[1,4,72]{1,0,2:T(2,128)(2,1)S(1)} %copy.307), channel_id=3, replica_groups=mesh['seq'=32] {'seq'}, dimensions={2}, use_global_device_ids=true | all-gather | bytes 19008 | tf_op jit(solution)/shard_map/all_gather | solution.py:163
  113.4 49.1 %slice_reduce_fusion.7 = (f32[2304]{0:T(1024)S(1)}, f32[2304]{0:T(1024)}, f32[2304]{0:T(1024)}, f32[2304]{0:T(1024)}) fusion(f32[1,4,2304]{1,0,2:T(1,128)S(1)} %convert_element_type.212), kind=kLoop, calls=%fused_computation.213 | loop fusion | bytes 73728 | tf_op jit(solution)/shard_map/jvp()/slice | solution.py:77
  166.3 7.4 fusion.36
  184.4 4.9 fusion.83
  200.0 45.0 %all-gather.8 = bf16[1,4,2304]{1,0,2:T(2,128)(2,1)S(1)} all-gather(bf16[1,4,72]{1,0,2:T(2,128)(2,1)} %copy.308), channel_id=10, replica_groups=mesh['seq'=32] {'seq'}, dimensions={2}, use_global_device_ids=true | all-gather | bytes 19008 | tf_op jit(solution)/shard_map/all_gather | solution.py:163
  248.8 48.5 %slice_reduce_fusion.3 = (f32[2304]{0:T(1024)}, f32[2304]{0:T(1024)}, f32[2304]{0:T(1024)}, f32[2304]{0:T(1024)}) fusion(f32[1,4,2304]{1,0,2:T(1,128)S(1)} %convert_element_type.216), kind=kLoop, calls=%fused_computation.209 | loop fusion | bytes 73728 | tf_op jit(solution)/shard_map/jvp()/slice | solution.py:77
  297.3 40.4 %all-gather.16 = f32[32,1,32]{2,1,0:T(1,128)} all-gather(f32[1,1,32]{2,1,0:T(1,128)S(1)} %bitcast.636), channel_id=1, replica_groups=mesh['seq'=32] {'seq'}, dimensions={0}, use_global_device_ids=true | all-gather | bytes 4224 | tf_op jit(solution)/shard_map/all_gather | solution.py:28
  339.8 51.1 %all-gather.31.cloned.1.call-done = f32[1024,64,128]{2,1,0:T(8,128)} async-done(((f32[32,64,128]{2,1,0:T(8,128)}), f32[1024,64,128]{2,1,0:T(8,128)}) %all-gather.31.cloned.1.call-update) | async-done | bytes 33554448 | tf_op jit(solution)/shard_map/all_gather | solution.py:28
  390.9 105.1 %while.60 = (s32[]{:T(128)}, f32[32,64,128]{2,1,0:T(8,128)}, s32[]{:T(128)}, f32[32,32]{1,0:T(8,128)}, f32[32,32,64,128]{3,2,1,0:T(8,128)}, /*index=5*/s32[]{:T(128)}, s32[]{:T(128)}) while((s32[]{:T(128)}, f32[32,64,128]{2,1,0:T(8,128)}, s32[]{:T(128)}, f32[32,32]{1,0:T(8,128)}, f32[32,32,64,128]{3,2,1,0:T(8,128)}, ...), condition=%wide.region_4.6_spmd.clone, body=%wide.region_3.5_spmd.clone.sunk | while | flops 1048580 | bytes 3146217 | solution.py:37
  499.4 9.6 fusion.105
  509.0 4.0 multiply_reduce_fusion.21
  513.6 5.5 multiply_reduce_fusion.26
  519.7 16.8 all-gather.35.cloned.1.call-done
  536.5 7.7 fusion.39
  566.1 5.3 fusion.82
  577.0 40.9 %all-gather.17 = f32[32,1,32]{2,1,0:T(1,128)} all-gather(f32[1,1,32]{2,1,0:T(1,128)} %bitcast.637), channel_id=1, replica_groups=mesh['seq'=32] {'seq'}, dimensions={0}, use_global_device_ids=true | all-gather | bytes 4224 | tf_op jit(solution)/shard_map/all_gather | solution.py:28
  621.7 148.7 %all-gather.37.cloned.1.call-done = f32[1024,64,128]{2,1,0:T(8,128)} async-done(((f32[32,64,128]{2,1,0:T(8,128)}), f32[1024,64,128]{2,1,0:T(8,128)}) %all-gather.37.cloned.1.call-update) | async-done | bytes 33554448 | tf_op jit(solution)/shard_map/all_gather | solution.py:28
  770.4 105.3 %while.61 = (s32[]{:T(128)}, f32[32,64,128]{2,1,0:T(8,128)}, s32[]{:T(128)}, f32[32,32]{1,0:T(8,128)}, f32[32,32,64,128]{3,2,1,0:T(8,128)}, /*index=5*/s32[]{:T(128)}, s32[]{:T(128)}) while((s32[]{:T(128)}, f32[32,64,128]{2,1,0:T(8,128)}, s32[]{:T(128)}, f32[32,32]{1,0:T(8,128)}, f32[32,32,64,128]{3,2,1,0:T(8,128)}, ...), condition=%wide.region_10.12_spmd.clone, body=%wide.region_9.11_spmd.clone.sunk | while | flops 1048580 | bytes 3146217 | solution.py:37
  879.1 9.6 fusion.104
  888.7 4.2 multiply_reduce_fusion.20
  893.5 5.7 multiply_reduce_fusion.14
  899.3 4.8 multiply_reduce_fusion.12
  912.7 4.2 fusion.139
  919.8 38.6 %all-gather.18 = bf16[32,1,32]{2,1,0:T(2,128)(2,1)S(1)} all-gather(bf16[1,1,32]{2,1,0:T(2,128)(2,1)S(1)} %bitcast.638), channel_id=1, replica_groups=mesh['seq'=32] {'seq'}, dimensions={0}, use_global_device_ids=true | all-gather | bytes 2112 | tf_op jit(solution)/shard_map/all_gather | solution.py:45
  959.9 3.8 multiply_reduce_fusion.18
  965.1 14.1 fusion.43
  980.0 3.8 reduce-window.64
  987.8 3.9 fusion.153
  992.8 37.8 %all-gather.41.cloned.1.call-done = bf16[1024,64,128]{2,1,0:T(8,128)(2,1)} async-done(((bf16[32,64,128]{2,1,0:T(8,128)(2,1)}), bf16[1024,64,128]{2,1,0:T(8,128)(2,1)}) %all-gather.41.cloned.1.call-update) | async-done | bytes 16777232 | tf_op jit(solution)/shard_map/all_gather | solution.py:45
  1031.8 99.9 %while.58 = (s32[]{:T(128)}, f32[32,64,128]{2,1,0:T(8,128)}, s32[]{:T(128)}, bf16[32,32]{1,0:T(8,128)(2,1)}, bf16[32,32,64,128]{3,2,1,0:T(8,128)(2,1)}, /*index=5*/s32[]{:T(128)}, s32[]{:T(128)}, s32[]{:T(128)}, s32[]{:T(128)}) while((s32[]{:T(128)}, f32[32,64,128]{2,1,0:T(8,128)}, s32[]{:T(128)}, bf16[32,32]{1,0:T(8,128)(2,1)}, ...), condition=%wide.region_17.19_spmd, body=%wide.region_16.18_spmd.sunk | while | flops 786470 | bytes 2621907 | solution.py:62
  1131.7 3.9 fusion.150
  1135.7 4.2 multiply_reduce_fusion.11
  1141.2 7.5 fusion.100
  1148.9 5.0 multiply_reduce_fusion.5
  1173.7 3.8 reduce-window.66
  1184.0 3.5 slice.400
  1192.2 7.4 scatter-add.6
  1199.6 8.0 multiply_reduce_fusion.22
  1211.9 4.7 multiply_reduce_fusion.13
  1225.2 4.2 fusion.142
  1229.5 6.5 fusion.180
  1236.5 6.4 fusion.177
  1243.9 37.4 %all-gather.19 = bf16[32,1,32]{2,1,0:T(2,128)(2,1)S(1)} all-gather(bf16[1,1,32]{2,1,0:T(2,128)(2,1)S(1)} %bitcast.639), channel_id=1, replica_groups=mesh['seq'=32] {'seq'}, dimensions={0}, use_global_device_ids=true | all-gather | bytes 2112 | tf_op jit(solution)/shard_map/all_gather | solution.py:45
  1289.3 4.0 multiply_reduce_fusion.16
  1293.9 16.1 fusion.45
  1310.7 3.8 reduce-window.74
  1320.7 4.3 fusion.156
  1326.0 15.4 all-gather.43.cloned.1.call-done
  1342.6 99.0 %while.59 = (s32[]{:T(128)}, f32[32,64,128]{2,1,0:T(8,128)}, s32[]{:T(128)}, bf16[32,32]{1,0:T(8,128)(2,1)}, bf16[32,32,64,128]{3,2,1,0:T(8,128)(2,1)}, /*index=5*/s32[]{:T(128)}, s32[]{:T(128)}, s32[]{:T(128)}, s32[]{:T(128)}) while((s32[]{:T(128)}, f32[32,64,128]{2,1,0:T(8,128)}, s32[]{:T(128)}, bf16[32,32]{1,0:T(8,128)(2,1)}, ...), condition=%wide.region_34.36_spmd, body=%wide.region_33.35_spmd.sunk | while | flops 786470 | bytes 2621907 | solution.py:62
  1445.3 5.2 multiply_reduce_fusion.10
  1456.1 3.8 reduce-window.76
  1462.7 4.2 fusion.147
  1467.4 9.4 fusion.96
  1476.9 4.9 multiply_reduce_fusion.9
  1505.2 7.4 scatter-add.9
  1512.6 8.8 fusion.160
  1521.5 10.3 fusion.176
  1533.3 10.3 fusion.175
  1545.2 4.6 fusion.136
  1549.7 87.8 %reduce-scatter.11.cloned.1.call-done = f32[64,1024]{1,0:T(8,128)} async-done(((f32[2048,1024]{1,0:T(8,128)}), f32[64,1024]{1,0:T(8,128)}) %reduce-scatter.11.cloned.1.call-update) | async-done | bytes 262160 | tf_op jit(solution)/shard_map/reduce_scatter | solution.py:272
  1642.3 126.8 %all-reduce.44.cloned.1.call-done = (f32[4,2304]{1,0:T(4,128)}, f32[4,2304]{1,0:T(4,128)}, f32[2304]{0:T(1024)}, f32[2304]{0:T(1024)}, f32[1024]{0:T(1024)}, /*i...) async-done(((f32[4,2304]{1,0:T(4,128)}, f32[4,2304]{1,0:T(4,128)}, f32[2304]{0:T(1024)}, ...) | async-done | bytes 117520
  1777.5 192.5 %reduce-scatter.9.cloned.1.call-done = f32[32,4384]{1,0:T(8,128)} async-done(((f32[1024,4384]{1,0:T(8,128)}), f32[32,4384]{1,0:T(8,128)}) %reduce-scatter.9.cloned.1.call-update) | async-done | bytes 561168 | tf_op jit(solution)/shard_map/reduce_scatter | solution.py:271
  1970.0 202.3 %reduce-scatter.7.cloned.1.call-done = f32[32,4384]{1,0:T(8,128)} async-done(((f32[1024,4384]{1,0:T(8,128)}), f32[32,4384]{1,0:T(8,128)}) %reduce-scatter.7.cloned.1.call-update) | async-done | bytes 561168 | tf_op jit(solution)/shard_map/reduce_scatter | solution.py:271
  (839 shorter events, 634.9 us)
Async XLA Ops:
  7.2 104.9 %copy-start.34 = (bf16[256,1024]{1,0:T(8,128)(2,1)S(1)}, bf16[256,1024]{1,0:T(8,128)(2,1)}, u32[]{:S(2)}) copy-start(bf16[256,1024]{1,0:T(8,128)(2,1)} %param.25) | copy-start | bytes 1572868
  7.2 159.1 %all-gather.29.cloned.1.call-start = ((), (), s32[]{:S(2)}) async-start(), calls=%async_computation.8 | async-start | bytes 9461760 | tf_op jit(solution)/shard_map/all_gather | solution.py:161
  9.2 103.1 %copy-start.171 = (f32[2,32]{1,0:T(2,128)S(1)}, f32[2,32]{1,0:T(2,128)}, u32[]{:S(2)}) copy-start(f32[2,32]{1,0:T(2,128)} %param.33) | copy-start | bytes 772
  9.2 103.7 %copy-start.169 = (f32[2,32]{1,0:T(2,128)S(1)}, f32[2,32]{1,0:T(2,128)}, u32[]{:S(2)}) copy-start(f32[2,32]{1,0:T(2,128)} %param.34) | copy-start | bytes 772
  9.2 381.7 %all-gather.31.cloned.1.call-start = ((), (), s32[]{:S(2)}) async-start(), calls=%async_computation.9 | async-start | bytes 34603008 | tf_op jit(solution)/shard_map/all_gather | solution.py:28
  10.0 152.5 %collective-permute-start.1 = (bf16[3]{0:T(256)(128)(2,1)S(1)}, bf16[3]{0:T(256)(128)(2,1)S(1)}, u32[]{:S(2)}, u32[]{:S(2)}) collective-permute-start(bf16[3]{0:T(256)(128)(2,1)S(1)} %add_convert_fusion), channel_id=1, source_target_pairs={{0,1},{1,2},{2,3},{3,4},{4,5},{5,6},{6,7},{7,8},{8,9},{9,10},{10,1... | collective-permute-start | bytes 26 | tf_op jit(solution)/shard_map/ppermute | solution.py:23
  59.8 106.5 %copy-start.53 = (f32[1024]{0:T(1024)}, f32[1024]{0:T(1024)S(1)}, u32[]{:S(2)}) copy-start(f32[1024]{0:T(1024)S(1)} %convert_element_type.220) | copy-start | bytes 12292
  112.3 50.3 %copy-start.153 = (f32[256]{0:T(256)}, f32[256]{0:T(256)S(1)}, u32[]{:S(2)}) copy-start(f32[256]{0:T(256)S(1)} %fusion.163) | copy-start | bytes 3076
  112.3 54.0 %copy-start.129 = (f32[256]{0:T(256)}, f32[256]{0:T(256)S(1)}, u32[]{:S(2)}) copy-start(f32[256]{0:T(256)S(1)} %fusion.238) | copy-start | bytes 3076
  112.8 66.3 %copy-start.149 = (f32[32]{0:T(128)}, f32[32]{0:T(128)S(1)}, u32[]{:S(2)}) copy-start(f32[32]{0:T(128)S(1)} %get-tuple-element.632) | copy-start | bytes 388
  113.4 60.5 %copy-start.151 = (f32[32]{0:T(128)}, f32[32]{0:T(128)S(1)}, u32[]{:S(2)}) copy-start(f32[32]{0:T(128)S(1)} %get-tuple-element.429) | copy-start | bytes 388
  113.4 50.9 %copy-start.98 = (s32[256]{0:T(256)S(1)}, s32[256]{0:T(256)}, u32[]{:S(2)}) copy-start(s32[256]{0:T(256)} %param.26) | copy-start | bytes 3076
  162.6 21.8 copy-start.82
  166.3 12.8 copy-start.120
  166.3 12.8 copy-start.159
  176.1 4.9 collective-permute-start
  194.2 319.4 %all-gather.33.cloned.1.call-start = ((), (), s32[]{:S(2)}) async-start(), calls=%async_computation.10 | async-start | bytes 4325376 | tf_op jit(solution)/shard_map/all_gather | solution.py:162
  196.0 340.5 %all-gather.35.cloned.1.call-start = ((), (), s32[]{:S(2)}) async-start(), calls=%async_computation.11 | async-start | bytes 9461760 | tf_op jit(solution)/shard_map/all_gather | solution.py:161
  196.6 573.8 %all-gather.37.cloned.1.call-start = ((), (), s32[]{:S(2)}) async-start(), calls=%async_computation.12 | async-start | bytes 34603008 | tf_op jit(solution)/shard_map/all_gather | solution.py:28
  196.6 317.0 %copy-start.80 = (f32[2048]{0:T(1024)}, f32[2048]{0:T(1024)S(1)}, u32[]{:S(2)}) copy-start(f32[2048]{0:T(1024)S(1)} %convert_element_type.221) | copy-start | bytes 24580
  248.8 48.5 %copy-start.170 = (f32[32]{0:T(128)S(1)}, f32[32]{0:T(128)}, u32[]{:S(2)}) copy-start(f32[32]{0:T(128)} %get-tuple-element.512) | copy-start | bytes 388
  519.7 24.6 %copy-start.126 = (f32[256]{0:T(256)}, f32[256]{0:T(256)S(1)}, u32[]{:S(2)}) copy-start(f32[256]{0:T(256)S(1)} %fusion.240) | copy-start | bytes 3076
  536.5 9.3 copy-start.147
  536.5 9.3 copy-start.150
  536.5 21.5 copy-start.121
  551.2 14.9 copy-start.137
  555.3 6.7 collective-permute-start.2
  576.4 317.1 %all-gather.39.cloned.1.call-start = ((), (), s32[]{:S(2)}) async-start(), calls=%async_computation.13 | async-start | bytes 4325376 | tf_op jit(solution)/shard_map/all_gather | solution.py:162
  576.9 453.7 %all-gather.41.cloned.1.call-start = ((), (), s32[]{:S(2)}) async-start(), calls=%async_computation.14 | async-start | bytes 17301504 | tf_op jit(solution)/shard_map/all_gather | solution.py:45
  899.3 10.8 copy-start.99
  916.9 424.5 %all-gather.43.cloned.1.call-start = ((), (), s32[]{:S(2)}) async-start(), calls=%async_computation.15 | async-start | bytes 17301504 | tf_op jit(solution)/shard_map/all_gather | solution.py:45
  917.0 48.1 %copy-start.8 = (f32[256,2048]{0,1:T(8,128)S(1)}, f32[256,2048]{0,1:T(8,128)}, u32[]{:S(2)}) copy-start(f32[256,2048]{0,1:T(8,128)} %get-tuple-element.573) | copy-start | bytes 6291460
  917.0 48.1 %copy-start.19 = (f32[256,2048]{0,1:T(8,128)S(1)}, f32[256,2048]{0,1:T(8,128)}, u32[]{:S(2)}) copy-start(f32[256,2048]{0,1:T(8,128)} %copy-done.17) | copy-start | bytes 6291460
  917.0 48.1 %copy-start.64 = (f32[256,32]{0,1:T(8,128)S(1)}, f32[256,32]{0,1:T(8,128)}, u32[]{:S(2)}) copy-start(f32[256,32]{0,1:T(8,128)} %get-tuple-element.417) | copy-start | bytes 98308
  959.7 19.5 copy-start.133
  959.9 19.4 copy-start.106
  965.1 14.2 copy-start.72
  965.1 14.2 copy-start.50
  965.1 14.2 copy-start.144
  965.1 14.2 copy-start.158
  1163.6 23.9 %collective-permute-start.3 = (f32[3,2304]{1,0:T(4,128)}, f32[3,2304]{1,0:T(4,128)}, u32[]{:S(2)}, u32[]{:S(2)}) collective-permute-start(f32[3,2304]{1,0:T(4,128)} %copy.230), channel_id=1, source_target_pairs={{1,0},{2,1},{3,2},{4,3},{5,4},{6,5},{7,6},{8,7},{9,8},{10,9},{11,1... | collective-permute-start | bytes 82952 | tf_op jit(solution)/shard_map/ppermute | solution.py:23
  1229.5 320.3 %reduce-scatter.13.cloned.1.call-start = ((), (), s32[]{:S(2)}) async-start(), calls=%async_computation.7 | async-start | bytes 8650752 | tf_op jit(solution)/shard_map/reduce_scatter | solution.py:272
  1236.0 401.5 %reduce-scatter.11.cloned.1.call-start = ((), (), s32[]{:S(2)}) async-start(), calls=%async_computation.6 | async-start | bytes 8650752 | tf_op jit(solution)/shard_map/reduce_scatter | solution.py:272
  1242.9 526.2 %all-reduce.44.cloned.1.call-start = ((), (), s32[]{:S(2)}) async-start(), calls=%async_computation.16 | async-start | bytes 251904
  1284.7 9.1 copy-start.6
  1284.7 9.1 copy-start.68
  1289.2 20.7 copy-start.131
  1289.3 20.6 copy-start.104
  1293.8 16.1 copy-start.70
  1293.8 16.1 copy-start.49
  1293.8 16.1 copy-start.142
  1293.8 16.1 copy-start.156
  1441.6 8.9 copy-start.122
  1467.3 9.5 copy-start.24
  1467.3 9.5 copy-start.51
  1467.3 9.5 copy-start.111
  1467.3 9.5 copy-start.115
  1467.3 9.5 copy-start.119
  1492.1 8.7 collective-permute-start.4
  1503.0 9.6 copy-start.54
  1512.6 8.9 copy-start.33
  1521.4 448.6 %reduce-scatter.9.cloned.1.call-start = ((), (), s32[]{:S(2)}) async-start(), calls=%async_computation.5 | async-start | bytes 18923520 | tf_op jit(solution)/shard_map/reduce_scatter | solution.py:271
  1531.9 640.4 %reduce-scatter.7.cloned.1.call-start = ((), (), s32[]{:S(2)}) async-start(), calls=%async_computation.4 | async-start | bytes 18923520 | tf_op jit(solution)/shard_map/reduce_scatter | solution.py:271
  1545.2 94.2 %copy-start.154 = (f32[256]{0:T(256)S(1)}, f32[256]{0:T(256)}, u32[]{:S(2)}) copy-start(f32[256]{0:T(256)} %copy-done.153) | copy-start | bytes 3076
  (130 other events, 537.7 us)
Sparse Core Ops, SparseCore 0:
  11.5 92.2 all-gather.28
  194.3 196.4 all-gather.30
  393.7 60.2 all-gather.32
  457.3 79.2 all-gather.34
  576.5 193.8 all-gather.36
  773.1 60.1 all-gather.38
  917.1 113.5 all-gather.40
  1229.6 111.8 all-gather.42
  1343.8 146.8 reduce-scatter.12
  1492.8 144.6 reduce-scatter.10
  1645.1 124.0 all-reduce.43
  1771.4 198.5 reduce-scatter.8
  1972.3 199.9 reduce-scatter.6
where the time goes:
time: 2200 us; the launch traced here: 2190 us
  waiting for transfers between devices  881 us (40%)
  other arithmetic  512 us (23%)
  blocking collectives  294 us (13%)
  local copies, waits for them, and re-layouts  256 us (12%)
  matrix products  213 us (10%)
    reduce_scatter x2, waiting for transfers between devices, per_device(): lax.psum_scatter(in_term, 'seq', scatter_dimension=0, tiled=True)  395 us
    all_gather x2, waiting for transfers between devices, prefix(): pieces = jax.tree.map(lambda part: lax.all_gather(part, axis), value)  200 us
    select_n x62, other arithmetic, lap(): jnp.where(position < mine, new, old)  167 us
    add x62, other arithmetic, combine_state(): later[0][:, None, None] * earlier[1] + later[1]  157 us
    unnamed x14, waiting for transfers between devices  128 us
    slice x2, local copies, waits for them, and re-layouts, conv_mix(): conv_w[offset] * padded[offset:offset + tokens_n] * same_doc[:, None]  97.6 us
    all_gather x2, blocking collectives, per_device(): lax.all_gather(shards[2], 'seq', axis=1, tiled=True)  94.1 us
    reduce_scatter x2, waiting for transfers between devices, per_device(): lax.psum_scatter(out_term, 'seq', scatter_dimension=0, tiled=True)  87.8 us
  transfers between devices with their start and end apart: 18, of which 9 were waited for; matrix products, arithmetic and copies ran while one was open for 33% of the time, Pallas kernels for 0%

commit v1 on v0

v1 whole, which is shorter than its diff:
```python
from functools import partial

import jax
import jax.numpy as jnp
import numpy as np
from jax import lax
from jax.experimental import pallas as pl
from jax.experimental.pallas import tpu as pltpu
from jax.sharding import PartitionSpec as P

HEADS = 32
HEAD_DIM = 64
STATE = 128
CONV_K = 4
INNER = 2048
CONV_CH = 2304
SIDE = CONV_CH + HEADS
WIDE = 2432
CUT = 1280
LANES = 128
PAIRS = HEADS // 2
HALO = 16
LEAD = HALO - (CONV_K - 1)
FAR = -1e30

EPS = 1e-05
F32 = jnp.float32
BF16 = jnp.bfloat16
EXACT = lax.Precision.HIGHEST
MB = 1024 * 1024


def axes_of(count):
    side = 4 if count >= 128 else 2
    plane = 2 * side * side
    return {"c": (2, 1), "x": (side, 2), "y": (side, 2 * side), "z": (count // plane, plane)}


def swap(value, flip):
    count = lax.axis_size("seq")
    return lax.ppermute(value, "seq", [(i, i ^ flip) for i in range(count)])


def shifted(shard, by):
    count = lax.axis_size("seq")
    return lax.ppermute(shard, "seq", [(i, i + by) for i in range(count) if 0 <= i + by < count])


def relative_places(count):
    axes = axes_of(count)
    places = np.zeros((1,), np.int32)
    for name in ("c", "y", "x", "z"):
        size, shift = axes[name]
        places = (places[:, None] + np.arange(size, dtype=np.int32)[None, :] * shift).reshape(-1)
    return places


def relative_order(count, me, block):
    places = jnp.asarray(np.repeat(relative_places(count), block))
    inner = jnp.asarray(np.tile(np.arange(block, dtype=np.int32), count))
    source = (places ^ me) * block + inner
    return (jnp.arange(count * block)[:, None] == source[None, :]).astype(BF16)


def gather_side(shard):
    axes = axes_of(lax.axis_size("seq"))

    def grow(value, name, axis):
        size, shift = axes[name]
        return jnp.stack([value] + [swap(value, d * shift) for d in range(1, size)], axis)

    line = grow(shard, "z", 0)
    left = grow(grow(line[:, :, :CUT], "x", 0), "y", 0)
    right = grow(grow(line[:, :, CUT:], "y", 0), "x", 1)
    left = left.reshape(-1, left.shape[-1])
    right = right.reshape(-1, right.shape[-1])
    return (left, swap(left, 1)), (right, swap(right, 1))


def reduce_shares(grad, order):
    axes = axes_of(lax.axis_size("seq"))
    sizes = tuple(axes[name][0] for name in ("c", "y", "x", "z"))
    rows = grad.shape[0] // int(np.prod(sizes))
    parts = grad.reshape(sizes + (rows, grad.shape[1]))
    names = ["c", "y", "x", "z"]
    terms = [parts]
    for name in ("c",) + order + ("z",):
        size, shift = axes[name]
        axis = names.index(name)
        names.remove(name)

        def total(index, terms=terms, axis=axis):
            picked = [lax.index_in_dim(t, index, axis, False).astype(F32) for t in terms]
            return sum(picked[1:], picked[0])

        if len(terms) == 1:
            pieces = [lax.index_in_dim(terms[0], d, axis, False) for d in range(size)]
        else:
            pieces = [total(d).astype(BF16) for d in range(size)]
        terms = [pieces[0]] + [swap(pieces[d], d * shift) for d in range(1, size)]
    picked = [t.astype(F32) for t in terms]
    return sum(picked[1:], picked[0])


def sum_all(value):
    flip = lax.axis_size("seq") // 2
    while flip:
        value = value + swap(value, flip)
        flip //= 2
    return value


def kernel_call(body, outs, args, scratch=(), limit=40, flops=0, moved=None):
    in_specs = [
        pl.BlockSpec(memory_space=pltpu.SMEM if a.dtype == jnp.int32 else pltpu.VMEM) for a in args
    ]
    size = sum(int(np.prod(a.shape)) * a.dtype.itemsize for a in args) + sum(
        int(np.prod(o[0])) * jnp.dtype(o[1]).itemsize for o in outs
    )
    return pl.pallas_call(
        body,
        out_shape=tuple(jax.ShapeDtypeStruct(*o) for o in outs),
        in_specs=in_specs,
        out_specs=tuple(pl.BlockSpec(memory_space=pltpu.VMEM) for _ in outs),
        scratch_shapes=list(scratch),
        compiler_params=pltpu.CompilerParams(vmem_limit_bytes=limit * MB),
        cost_estimate=pl.CostEstimate(flops=flops, bytes_accessed=size, transcendentals=0),
    )(*args)


def dot(left, right, precision=None):
    return jnp.dot(left, right, precision=precision, preferred_element_type=F32)


def dot_t(left, right):
    return lax.dot_general(left, right, (((1,), (1,)), ((), ())), preferred_element_type=F32)


def halves(value):
    high = value.astype(BF16)
    return high, (value - high.astype(F32)).astype(BF16)


def fine(form, left, right):
    (lh, ll), (rh, rl) = halves(left), halves(right)
    return form(lh, rh) + (form(ll, rh) + form(lh, rl))


def lanes_of(rows):
    return lax.broadcasted_iota(jnp.int32, (rows, LANES), 1)


def spread(values, pair):
    low = lanes_of(values.shape[0]) < HEAD_DIM
    return jnp.where(low, values[:, 2 * pair : 2 * pair + 1], values[:, 2 * pair + 1 : 2 * pair + 2])


def spread_row(row):
    return jnp.concatenate([spread(row, pair) for pair in range(PAIRS)], axis=1)


def head_sums(product, pair):
    rows = lax.broadcasted_iota(jnp.int32, (LANES, LANES), 0)
    cols = lax.broadcasted_iota(jnp.int32, (LANES, LANES), 1)
    pick = (cols == 2 * pair + (rows >= HEAD_DIM).astype(jnp.int32)).astype(BF16)
    high = product.astype(BF16)
    low = (product - high.astype(F32)).astype(BF16)
    return dot(high, pick) + dot(low, pick)


def sigmoid(v):
    return 1.0 / (1.0 + jnp.exp(-v))


def silu(v):
    return v * sigmoid(v)


def tile(pair):
    return slice(pair * LANES, (pair + 1) * LANES)


def pack_row(row):
    first = row.astype(BF16).astype(F32)
    second = (row - first).astype(BF16).astype(F32)
    third = row - first - second
    place = lax.broadcasted_iota(jnp.int32, (16, row.shape[1]), 0)
    packed = jnp.where(place == 0, first, jnp.where(place == 1, second, third))
    return jnp.where(place < 3, packed, 0.0).astype(BF16)


def unpack_row(rows):
    return jnp.sum(rows.astype(F32), axis=0, keepdims=True)


def emit_msg(total, keep, msg_o):
    msg_o[0:STATE, :] = total.astype(msg_o.dtype)
    if msg_o.dtype == F32:
        msg_o[STATE:, :] = jnp.broadcast_to(keep, (msg_o.shape[0] - STATE, keep.shape[1]))
    else:
        msg_o[STATE:, :] = pack_row(keep)


def read_msg(recv):
    if recv.dtype == F32:
        return recv[0:STATE, :], recv[STATE : STATE + 1, :]
    return recv[0:STATE, :].astype(F32), unpack_row(recv[STATE:, :])


def emit_full(total, keep, total_o, keep_o, msg_o):
    total_o[...] = total
    keep_o[...] = jnp.broadcast_to(keep, keep_o.shape)
    emit_msg(total, keep, msg_o)


def emit_halves(total, keep, upper, total_o, keep_o, msg_o):
    half = total.shape[1] // 2
    low, high = total[:, :half], total[:, half:]
    klow, khigh = keep[:, :half], keep[:, half:]
    total_o[...] = jnp.where(upper, high, low)
    keep_o[...] = jnp.broadcast_to(jnp.where(upper, khigh, klow), keep_o.shape)
    emit_msg(jnp.where(upper, low, high), jnp.where(upper, klow, khigh), msg_o)


def bit_of(me, flip):
    return (me[0] & flip) != 0


def state_outs(width, kind):
    tail = 8 if kind == F32 else 16
    return [((STATE, width), F32), ((8, width), F32), ((STATE + tail, width), kind)]


def halve_kernel(total, keep, recv, me, first_o, kfirst_o, total_o, keep_o, msg_o, *, flip, after, back):
    other, kother = read_msg(recv)
    mine, kmine = total[...], keep[0:1, :]
    first = jnp.logical_xor(bit_of(me, flip), not back)
    t_first = jnp.where(first, mine, other)
    t_second = jnp.where(first, other, mine)
    k_first = jnp.where(first, kmine, kother)
    k_second = jnp.where(first, kother, kmine)
    first_o[...] = t_first
    kfirst_o[...] = jnp.broadcast_to(k_first, kfirst_o.shape)
    joined = k_second * t_first + t_second
    if after:
        emit_halves(joined, k_first * k_second, bit_of(me, after), total_o, keep_o, msg_o)
    else:
        emit_full(joined, k_first * k_second, total_o, keep_o, msg_o)


def whole_kernel(total, keep, state, kstate, recv, me, state_o, kstate_o, total_o, keep_o, msg_o, *, flip, back):
    other, kother = read_msg(recv)
    mine, kmine = total[...], keep[0:1, :]
    later = jnp.logical_xor(bit_of(me, flip), back)
    kpre = kstate[0:1, :]
    state_o[...] = state[...] + jnp.where(later, kpre * other, 0.0)
    kstate_o[...] = jnp.broadcast_to(jnp.where(later, kpre * kother, kpre), kstate_o.shape)
    joined = jnp.where(later, kmine * other + mine, kother * mine + other)
    emit_full(joined, kmine * kother, total_o, keep_o, msg_o)


def last_kernel(state, kstate, recv, first, kfirst, me, mine_o, msg_o, *, flip, down, back):
    later = jnp.logical_xor(bit_of(me, flip), back)
    into = state[...] + jnp.where(later, kstate[0:1, :] * recv[0:STATE, :].astype(F32), 0.0)
    split_block(into, first, kfirst, me, mine_o, msg_o, down, back)


def split_block(into, first, kfirst, me, mine_o, msg_o, down, back):
    beyond = kfirst[0:1, :] * into + first[...]
    second = jnp.logical_xor(bit_of(me, down), back)
    mine_o[...] = jnp.where(second, beyond, into)
    msg_o[...] = jnp.where(second, into, beyond).astype(msg_o.dtype)


def join_halves(mine, recv, upper):
    theirs = recv[...].astype(F32)
    own = mine[...]
    return jnp.where(upper, theirs, own), jnp.where(upper, own, theirs)


def down_kernel(mine, recv, first, kfirst, me, mine_o, msg_o, *, up, down, back):
    low, high = join_halves(mine, recv, bit_of(me, up))
    split_block(jnp.concatenate([low, high], axis=1), first, kfirst, me, mine_o, msg_o, down, back)


def exchange(total, keep, msg, me, back):
    count = lax.axis_size("seq")
    kind = msg.dtype
    halving = (1, 2, 4)
    rest = [1 << k for k in range(3, count.bit_length() - 1)]
    saved = []
    recv = swap(msg, halving[0])
    for i, flip in enumerate(halving):
        width = total.shape[1]
        after = halving[i + 1] if i + 1 < len(halving) else 0
        outs = state_outs(width, kind)[:2] + state_outs(width // 2 if after else width, kind)
        first, kfirst, total, keep, msg = kernel_call(
            partial(halve_kernel, flip=flip, after=after, back=back),
            outs, (total, keep, recv, me), limit=12,
        )
        saved.append((first, kfirst))
        recv = swap(msg, after or rest[0])
    width = total.shape[1]
    state, kstate = jnp.zeros((STATE, width), F32), jnp.ones((8, width), F32)
    for i, flip in enumerate(rest[:-1]):
        state, kstate, total, keep, msg = kernel_call(
            partial(whole_kernel, flip=flip, back=back),
            state_outs(width, kind)[:2] + state_outs(width, kind),
            (total, keep, state, kstate, recv, me), limit=12,
        )
        recv = swap(msg, rest[i + 1])
    mine, msg = kernel_call(
        partial(last_kernel, flip=rest[-1], down=halving[2], back=back),
        [((STATE, width), F32), ((STATE, width), kind)],
        (state, kstate, recv) + saved[2] + (me,), limit=12,
    )
    for up in (2, 1):
        recv = swap(msg, halving[up])
        width *= 2
        mine, msg = kernel_call(
            partial(down_kernel, up=halving[up], down=halving[up - 1], back=back),
            [((STATE, width), F32), ((STATE, width), kind)],
            (mine, recv) + saved[up - 1] + (me,), limit=12,
        )
    return mine, swap(msg, 1)


def norm_kernel(h, halo, gain, out):
    for ref, at in ((halo, slice(0, HALO)), (h, slice(HALO, HALO + h.shape[0]))):
        v = ref[...].astype(F32)
        inv = lax.rsqrt(jnp.mean(v * v, axis=-1, keepdims=True) + EPS)
        out[at, :] = (v * inv * gain[0:1, :]).astype(BF16)


def norm_back_kernel(gn, h, g, gain, out, gain_o):
    v = h[...].astype(F32)
    grad = gn[...]
    inv = lax.rsqrt(jnp.mean(v * v, axis=-1, keepdims=True) + EPS)
    n = v * inv
    q = grad * gain[0:1, :]
    out[...] = g[...] + inv * (q - n * jnp.mean(q * n, axis=-1, keepdims=True))
    gain_o[...] = jnp.broadcast_to(jnp.sum(grad * n, axis=0, keepdims=True), gain_o.shape)


def triangle(rows, lower):
    r = lax.broadcasted_iota(jnp.int32, (rows, rows), 0)
    c = lax.broadcasted_iota(jnp.int32, (rows, rows), 1)
    return r >= c if lower else r <= c


def conv_state_kernel(pc, cw, hp, mk, me, conv_o, dt_o, log_o, total_o, keep_o, msg_o, xw, *low, precise):
    rows = mk.shape[0]
    marks = mk[...]
    raw = pc[HALO:, CONV_CH:WIDE].astype(F32) + hp[0:1, :]
    soft = jnp.maximum(raw, 0.0) + jnp.log1p(jnp.exp(-jnp.abs(raw)))
    dt = jnp.where(lanes_of(rows) < HEADS, soft, 0.0)
    log = dot(triangle(rows, True).astype(F32), dt * hp[1:2, :], EXACT)
    last = log[rows - 1 : rows, :]
    weight = marks[:, 4:5] * jnp.exp(last - log) * dt
    dt_o[...] = dt
    log_o[...] = log
    b_cols = None
    for j in range(CONV_CH // LANES):
        ext = pc[:, tile(j)].astype(F32)
        out = cw[4:5, tile(j)] + cw[3:4, tile(j)] * ext[HALO:, :]
        for k in range(CONV_K - 1):
            out = out + cw[k : k + 1, tile(j)] * ext[LEAD + k : LEAD + k + rows, :] * marks[:, k : k + 1]
        conv_o[:, tile(j)] = out
        if j < PAIRS:
            high, rest = halves(silu(out) * spread(weight, j))
            xw[:, tile(j)] = high
            if precise:
                low[0][:, tile(j)] = rest
        elif j == PAIRS:
            b_cols, b_rest = halves(silu(out).T)
    total = dot(b_cols, xw[...])
    if precise:
        total = total + (dot(b_rest, xw[...]) + dot(b_cols, low[0][...]))
    keep = spread_row(jnp.exp(last) * marks[rows - 1 : rows, 3:4])
    emit_halves(total, keep, bit_of(me, 1), total_o, keep_o, msg_o)


def mask_bias(mk, sr, rows):
    same = mk[:, 5:6] == sr[0:1, :]
    return jnp.where(jnp.logical_and(triangle(rows, True), same), 0.0, FAR)


def within_kernel(conv, dt, log, hp, mk, sr, y_o, xdt, lcol, lrow, *lower, precise):
    rows = mk.shape[0]
    b = silu(conv[:, tile(PAIRS)])
    c = silu(conv[:, tile(PAIRS + 1)])
    scores = fine(dot_t, c, b)
    bias = mask_bias(mk, sr, rows)
    dtv, logv = dt[...], log[...]
    lrow[...] = logv.T
    for j in range(PAIRS):
        x = silu(conv[:, tile(j)])
        high, rest = halves(x * spread(dtv, j))
        xdt[:, tile(j)] = high
        if precise:
            lower[0][:, tile(j)] = rest
        y_o[:, tile(j)] = x * spread(hp[2:3, :], j)
    for h in range(HEADS):
        lcol[h] = jnp.broadcast_to(logv[:, h : h + 1], (rows, LANES))
    low = lanes_of(rows) < HEAD_DIM

    def pair(j, _):
        at = pl.ds(pl.multiple_of(j * LANES, LANES), LANES)
        xp = xdt[:, at]
        res = []
        for q in range(2):
            col = lcol[2 * j + q]
            span = jnp.concatenate([col] * (rows // LANES), axis=1) - lrow[pl.ds(2 * j + q, 1), :]
            mix = scores * jnp.exp(span + bias)
            if precise:
                high, rest = halves(mix)
                res.append(dot(high, xp) + (dot(rest, xp) + dot(high, lower[0][:, at])))
            else:
                res.append(dot(mix.astype(BF16), xp))
        y_o[:, at] += jnp.where(low, res[0], res[1])
        return 0

    lax.fori_loop(0, PAIRS, pair, 0)


def post_kernel(yw, mine, recv, conv, log, mk, z, gg, me, y_o, gn_o, st_o, gated):
    rows = mk.shape[0]
    low, high = join_halves(mine, recv, bit_of(me, 1))
    st_o[:, : INNER // 2] = low.astype(BF16)
    st_o[:, INNER // 2 :] = high.astype(BF16)
    c = silu(conv[:, tile(PAIRS + 1)])
    inflow = jnp.exp(log[...]) * mk[:, 3:4]
    total = jnp.zeros((rows, LANES), F32)
    for j in range(PAIRS):
        state = (low if j < PAIRS // 2 else high)[:, tile(j % (PAIRS // 2))]
        y = yw[:, tile(j)] + fine(dot, c, state) * spread(inflow, j)
        y_o[:, tile(j)] = y
        v = y * silu(z[:, tile(j)].astype(F32))
        gated[:, tile(j)] = v
        total = total + v * v
    inv = lax.rsqrt(jnp.sum(total, axis=-1, keepdims=True) / INNER + EPS)
    for j in range(PAIRS):
        gn_o[:, tile(j)] = (gated[:, tile(j)] * inv * gg[0:1, tile(j)]).astype(BF16)


def post_back_kernel(ggn, y, z, gg, conv, log, mk, me, gy_o, gz_o, rows_o, total_o, keep_o, msg_o, ge):
    rows = mk.shape[0]
    logv = log[...]
    inflow = jnp.exp(logv) * mk[:, 3:4]
    total = jnp.zeros((rows, LANES), F32)
    cross = jnp.zeros((rows, LANES), F32)
    for j in range(PAIRS):
        v = y[:, tile(j)] * silu(z[:, tile(j)].astype(F32))
        total = total + v * v
        cross = cross + v * ggn[:, tile(j)] * gg[0:1, tile(j)]
    inv = lax.rsqrt(jnp.sum(total, axis=-1, keepdims=True) / INNER + EPS)
    mean = jnp.sum(cross, axis=-1, keepdims=True) * inv / INNER
    for j in range(PAIRS):
        zf = z[:, tile(j)].astype(F32)
        s = sigmoid(zf)
        sz = zf * s
        yv = y[:, tile(j)]
        n = yv * sz * inv
        up = ggn[:, tile(j)]
        gga = inv * (up * gg[0:1, tile(j)] - n * mean)
        gy = gga * sz
        gz_o[:, tile(j)] = (gga * yv * (s * (1.0 + zf * (1.0 - s)))).astype(BF16)
        gy_o[:, tile(j)] = gy.astype(BF16)
        ge[:, tile(j)] = (gy * spread(inflow, j)).astype(BF16)
        rows_o[0:1, tile(j)] = jnp.sum(up * n, axis=0, keepdims=True)
        rows_o[1:2, tile(j)] = jnp.sum(gy * silu(conv[:, tile(j)]), axis=0, keepdims=True)
    rows_o[2:8, :] = jnp.zeros((6, INNER), F32)
    c_cols = silu(conv[:, tile(PAIRS + 1)]).T.astype(BF16)
    state = dot(c_cols, ge[...])
    keep = spread_row(jnp.exp(logv[rows - 1 : rows, :]) * mk[rows - 1 : rows, 3:4])
    emit_halves(state, keep, bit_of(me, 1), total_o, keep_o, msg_o)


def within_back_kernel(conv, dt, log, gy, st, mk, sr, gxdt_o, gb_o, gc_o, gl_o, xdt, ge, lcol, lrow, gscore, lsum, csum):
    rows = mk.shape[0]
    bf = silu(conv[:, tile(PAIRS)])
    cf = silu(conv[:, tile(PAIRS + 1)])
    b, c = bf.astype(BF16), cf.astype(BF16)
    scores = fine(dot_t, bf, cf)
    same = mk[:, 5:6] == sr[0:1, :]
    bias = jnp.where(jnp.logical_and(triangle(rows, False), same), 0.0, FAR)
    dtv, logv = dt[...], log[...]
    lrow[...] = logv.T
    inflow = jnp.exp(logv) * mk[:, 3:4]
    flow = jnp.zeros((rows, LANES), F32)
    for j in range(PAIRS):
        xdt[:, tile(j)] = (silu(conv[:, tile(j)]) * spread(dtv, j)).astype(BF16)
        gyv = gy[:, tile(j)].astype(F32) * spread(inflow, j)
        ge[:, tile(j)] = gyv.astype(BF16)
        flow = flow + head_sums(gyv * dot(c, st[:, tile(j)]), j)
    for h in range(HEADS):
        lcol[h] = jnp.broadcast_to(logv[:, h : h + 1], (rows, LANES))
    lanes = lanes_of(rows)
    low = lanes < HEAD_DIM
    gscore[...] = jnp.zeros_like(gscore)
    csum[...] = jnp.zeros_like(csum)
    lsum[...] = jnp.zeros_like(lsum)

    def pair(j, _):
        at = pl.ds(pl.multiple_of(j * LANES, LANES), LANES)
        xp, gp = xdt[:, at], gy[:, at]
        res = []
        for q in range(2):
            h = 2 * j + q
            span = lrow[pl.ds(h, 1), :] - jnp.concatenate([lcol[h]] * (rows // LANES), axis=1)
            decay = jnp.exp(span + bias)
            mix = scores * decay
            own = jnp.where(low if q == 0 else jnp.logical_not(low), gp, jnp.zeros_like(gp))
            gmix = dot_t(xp, own)
            gscore[...] += gmix * decay
            term = gmix * mix
            lsum[pl.ds(h, 1), :] = jnp.sum(term, axis=0, keepdims=True)
            csum[...] += jnp.where(lanes == h, jnp.sum(term, axis=1, keepdims=True), 0.0)
            res.append(dot(mix.astype(BF16), gp))
        gxdt_o[:, at] = jnp.where(low, res[0], res[1])
        return 0

    lax.fori_loop(0, PAIRS, pair, 0)
    gs = gscore[...]
    gb_o[...] = dot(gs.astype(BF16), c)
    gc_o[...] = dot(gs.T.astype(BF16), b) + dot_t(ge[...], st[...])
    gl_o[...] = lsum[...].T - csum[...] + flow


def mixer_back_kernel(
    mine, recv, gxdt, gbi, gci, gli, gy, conv, dt, log, st, pc, cw, hp, mk, me,
    gp_o, wide_o, head_o, gb16, xe, acc,
):
    rows = mk.shape[0]
    marks = mk[...]
    low, high = join_halves(mine, recv, bit_of(me, 1))
    half = INNER // 2
    kg = jnp.zeros((8, LANES), F32)
    for part, value in ((0, low), (half, high)):
        gb16[:, part : part + half] = value.astype(BF16)
        rowsum = jnp.sum(value * st[:, part : part + half].astype(F32), axis=0, keepdims=True)
        for j in range(PAIRS // 2):
            pair = part // LANES + j
            kg = kg + head_sums(jnp.broadcast_to(rowsum[:, tile(j)], (8, LANES)), pair)
    dtv, logv = dt[...], log[...]
    last = logv[rows - 1 : rows, :]
    b = silu(conv[:, tile(PAIRS)]).astype(BF16)
    outflow = marks[:, 4:5] * jnp.exp(last - logv)
    gv = jnp.zeros((rows, LANES), F32)
    gd = jnp.zeros((rows, LANES), F32)

    def conv_back(j, gact, s, out):
        gco = gact * (s * (1.0 + out * (1.0 - s)))
        ext = pc[:, tile(j)].astype(F32)
        acc[...] = jnp.zeros_like(acc)
        for k in range(CONV_K):
            gk = gco if k == CONV_K - 1 else gco * marks[:, k : k + 1]
            wide_o[k : k + 1, tile(j)] = jnp.sum(gk * ext[LEAD + k : LEAD + k + rows, :], axis=0, keepdims=True)
            acc[LEAD + k : LEAD + k + rows, :] += gk * cw[k : k + 1, tile(j)]
        wide_o[4:5, tile(j)] = jnp.sum(gco, axis=0, keepdims=True)
        gp_o[:, tile(j)] = acc[...].astype(BF16)

    wide_o[5:8, :] = jnp.zeros((3, CONV_CH), F32)
    for j in range(PAIRS):
        out = conv[:, tile(j)]
        s = sigmoid(out)
        x = out * s
        dtp = spread(dtv, j)
        flow = spread(outflow, j)
        xd = x * dtp
        gxs = dot(b, gb16[:, tile(j)]) * flow
        xe[:, tile(j)] = (xd * flow).astype(BF16)
        gxd = gxdt[:, tile(j)] + gxs
        gv = gv + head_sums(xd * gxs, j)
        gd = gd + head_sums(x * gxd, j)
        conv_back(j, dtp * gxd + spread(hp[2:3, :], j) * gy[:, tile(j)].astype(F32), s, out)
    gb = gbi[...] + dot_t(xe[...], gb16[...])
    for j, grad in ((PAIRS, gb), (PAIRS + 1, gci[...])):
        out = conv[:, tile(j)]
        conv_back(j, grad, sigmoid(out), out)
    keep = jnp.exp(last) * marks[rows - 1 : rows, 3:4]
    edge = jnp.sum(gv, axis=0, keepdims=True) + kg[0:1, :] * keep
    place = lax.broadcasted_iota(jnp.int32, (rows, LANES), 0)
    gl = gli[...] - gv + jnp.where(place == rows - 1, edge, 0.0)
    ga = dot(triangle(rows, False).astype(F32), gl, EXACT)
    rate = hp[1:2, :]
    raw = pc[HALO:, CONV_CH:WIDE].astype(F32) + hp[0:1, :]
    graw = jnp.where(lanes_of(rows) < HEADS, (ga * rate + gd) * sigmoid(raw), 0.0)
    gp_o[0:HALO, CONV_CH:WIDE] = jnp.zeros((HALO, LANES), BF16)
    gp_o[HALO:, CONV_CH:WIDE] = graw.astype(BF16)
    head_o[0:1, :] = jnp.sum(graw, axis=0, keepdims=True)
    head_o[1:2, :] = rate * jnp.sum(ga * dtv, axis=0, keepdims=True)
    head_o[2:8, :] = jnp.zeros((6, LANES), F32)


def row_of(values, rows=8):
    pad = [(0, rows - values.shape[0]), (0, max(0, LANES - values.shape[1]))]
    return jnp.pad(values.astype(F32), pad)


def per_device(
    hidden, segment_ids, in_weight, out_weight, conv_weight, conv_bias, norm_gain, gate_gain,
    dt_bias, a_log, skip_param, cotangent,
):
    layers_n, in_rows = in_weight.shape[:2]
    out_rows = out_weight.shape[1]
    rows, width = hidden.shape
    count = lax.axis_size("seq")
    me = lax.axis_index("seq")
    me_ref = me.reshape(1).astype(jnp.int32)
    conv_n = conv_bias.shape[1]

    small = jnp.concatenate(
        [conv_weight.reshape(-1), conv_bias.reshape(-1), norm_gain.reshape(-1), gate_gain.reshape(-1)]
    )
    per_row = HEADS
    small = jnp.pad(small, (0, in_rows * per_row - small.shape[0])).reshape(in_rows, per_row)
    side = [in_weight[layer, :, INNER:] for layer in range(layers_n)]
    shards = [
        jnp.pad(
            jnp.concatenate([side[layer], small], axis=1) if layer == 0 else side[layer],
            ((0, 0), (0, WIDE - SIDE - (per_row if layer == 0 else 0))),
        )
        for layer in range(layers_n)
    ]
    halo = shifted(hidden[rows - HALO :], 1)
    seg_halo = shifted(segment_ids[rows - HALO :] + 1, 1) - 1
    first_side = gather_side(shards[0])

    packs = [
        jnp.concatenate(
            [in_weight[layer, :, : INNER // 2], in_weight[layer, :, INNER // 2 : INNER], out_weight[layer]], axis=0
        )
        for layer in range(layers_n)
    ]
    gathered = [lax.all_gather(pack, "seq") for pack in packs]

    seg_pad = jnp.concatenate([seg_halo[LEAD:], segment_ids])
    before = seg_pad[CONV_K - 2]
    columns = [seg_pad[k : k + rows] == segment_ids for k in range(CONV_K - 1)]
    columns += [segment_ids == before, segment_ids == segment_ids[-1], segment_ids]
    marks = jnp.pad(jnp.stack([col.astype(F32) for col in columns], axis=1), ((0, 0), (0, LANES - 6)))
    seg_row = jnp.broadcast_to(segment_ids.astype(F32)[None, :], (8, rows))

    order = relative_order(count, me, in_rows)
    out_order = relative_order(count, me, out_rows)

    (left, left2), (right, right2) = first_side
    at = slice(SIDE - CUT, SIDE - CUT + per_row)
    smalls = jnp.concatenate([right[:, at], right2[:, at]], axis=0).reshape(count, in_rows * per_row)
    place = (jnp.arange(count)[:, None] == (jnp.asarray(relative_places(count)) ^ me)[None, :]).astype(BF16)
    smalls = dot(place, smalls)
    sizes = [layers_n * CONV_K * conv_n, layers_n * conv_n, layers_n * in_rows, layers_n * out_rows]
    cuts = np.cumsum([0] + sizes)
    taps, biases, gains, gate_gains = (smalls[:, cuts[i] : cuts[i + 1]] for i in range(4))
    taps = taps.reshape(count, layers_n, CONV_K, conv_n).transpose(1, 2, 0, 3).reshape(layers_n, CONV_K, CONV_CH)
    biases = biases.reshape(count, layers_n, 1, conv_n).transpose(1, 2, 0, 3).reshape(layers_n, 1, CONV_CH)
    conv_rows = jnp.pad(jnp.concatenate([taps, biases], axis=1), ((0, 0), (0, 3), (0, 0)))
    gains = gains.reshape(count, layers_n, in_rows).transpose(1, 0, 2).reshape(layers_n, 1, width)
    gate_gains = gate_gains.reshape(count, layers_n, out_rows).transpose(1, 0, 2).reshape(layers_n, 1, INNER)
    gains = jnp.broadcast_to(gains, (layers_n, 8, width))
    gate_gains = jnp.broadcast_to(gate_gains, (layers_n, 8, INNER))

    scratch_wide = pltpu.VMEM((rows, INNER), BF16)
    scratch_cols = pltpu.VMEM((HEADS, rows, LANES), F32)
    scratch_rows = pltpu.VMEM((LANES, rows), F32)

    residual = hidden
    saved = []
    for layer in range(layers_n):
        if layer == 0:
            sides = first_side
        precise = layer + 1 < layers_n
        gain, gate = gains[layer], gate_gains[layer]
        (normed,) = kernel_call(norm_kernel, [((HALO + rows, width), BF16)], (residual, halo, gain), limit=16)
        normed_rel = dot(normed, order).astype(BF16)
        lower, upper = normed_rel[:, : width // 2], normed_rel[:, width // 2 :]
        (left, left2), (right, right2) = sides
        pc = jnp.concatenate(
            [(dot(lower, left) + dot(upper, left2)).astype(BF16), (dot(lower, right) + dot(upper, right2)).astype(BF16)],
            axis=1,
        )
        heads = jnp.stack([dt_bias[layer], -jnp.exp(a_log[layer]), skip_param[layer]])
        hp = row_of(heads)
        conv, dt, log, total, keep, msg = kernel_call(
            partial(conv_state_kernel, precise=precise),
            [((rows, CONV_CH), F32), ((rows, LANES), F32), ((rows, LANES), F32)] + state_outs(INNER // 2, F32),
            (pc, conv_rows[layer], hp, marks, me_ref),
            scratch=[scratch_wide] * (2 if precise else 1), flops=2 * rows * STATE * INNER * 8,
        )
        mine, recv = exchange(total, keep, msg, me_ref, False)
        if layer + 1 < layers_n:
            shard, _ = lax.optimization_barrier((shards[layer + 1], total))
            next_sides = gather_side(shard)
        pack = gathered[layer]
        z_low = pack[:, :in_rows].reshape(width, INNER // 2)
        z_high = pack[:, in_rows : 2 * in_rows].reshape(width, INNER // 2)
        out_w = pack[:, 2 * in_rows :].reshape(INNER, width)
        own = normed[HALO:]
        z = jnp.concatenate([dot(own, z_low).astype(BF16), dot(own, z_high).astype(BF16)], axis=1)
        (yw,) = kernel_call(
            partial(within_kernel, precise=precise), [((rows, INNER), F32)], (conv, dt, log, hp, marks, seg_row),
            scratch=[scratch_wide, scratch_cols, scratch_rows] + [scratch_wide] * precise,
            flops=2 * rows * rows * INNER * 16,
        )
        y, gnormed, state = kernel_call(
            post_kernel,
            [((rows, INNER), F32), ((rows, INNER), BF16), ((STATE, INNER), BF16)],
            (yw, mine, recv, conv, log, marks, z, gate, me_ref),
            scratch=[pltpu.VMEM((rows, INNER), F32)], flops=2 * rows * STATE * INNER * 8,
        )
        saved.append((residual, normed, normed_rel, pc, conv, dt, log, hp, z, y, gnormed, state, z_low, z_high, out_w, sides))
        residual = residual.astype(F32) + dot(gnormed, out_w)
        if layer + 1 < layers_n:
            halo = shifted(residual[rows - HALO :], 1)
            sides = next_sides

    grad = cotangent
    in_grads, out_grads, smalls = [None] * layers_n, [None] * layers_n, [None] * layers_n
    for layer in range(layers_n - 1, -1, -1):
        h, normed, normed_rel, pc, conv, dt, log, hp, z, y, gnormed, state, z_low, z_high, out_w, sides = saved[layer]
        gain, gate = gains[layer], gate_gains[layer]
        mixed = grad.astype(BF16)
        ggn = dot_t(mixed, out_w)
        gy, gz, wide_rows, total, keep, msg = kernel_call(
            post_back_kernel,
            [((rows, INNER), BF16), ((rows, INNER), BF16), ((8, INNER), F32)] + state_outs(INNER // 2, BF16),
            (ggn, y, z, gate, conv, log, marks, me_ref),
            scratch=[scratch_wide], flops=2 * rows * STATE * INNER * 8,
        )
        mine, recv = exchange(total, keep, msg, me_ref, True)
        gn_rel = dot(gnormed, out_order).astype(BF16)
        out_term = lax.dot_general(gn_rel, mixed, (((0,), (0,)), ((), ())), preferred_element_type=F32).astype(BF16)
        z_term = lax.dot_general(
            normed_rel[HALO:], gz, (((0,), (0,)), ((), ())), preferred_element_type=F32
        ).astype(BF16)
        z_share = reduce_shares(z_term, ("x", "y"))
        out_share = reduce_shares(out_term, ("y", "x"))
        gxdt, gb, gc, gl = kernel_call(
            within_back_kernel,
            [((rows, INNER), F32), ((rows, LANES), F32), ((rows, LANES), F32), ((rows, LANES), F32)],
            (conv, dt, log, gy, state, marks, seg_row),
            scratch=[
                scratch_wide, scratch_wide, scratch_cols, scratch_rows,
                pltpu.VMEM((rows, rows), F32), scratch_rows, pltpu.VMEM((rows, LANES), F32),
            ],
            flops=2 * rows * rows * INNER * 32,
        )
        gn_z = dot_t(gz[:, : INNER // 2], z_low) + dot_t(gz[:, INNER // 2 :], z_high)
        gp, conv_grads, head_grads = kernel_call(
            mixer_back_kernel,
            [((HALO + rows, WIDE), BF16), ((8, CONV_CH), F32), ((8, LANES), F32)],
            (mine, recv, gxdt, gb, gc, gl, gy, conv, dt, log, state, pc, conv_rows[layer], hp, marks, me_ref),
            scratch=[pltpu.VMEM((STATE, INNER), BF16), scratch_wide, pltpu.VMEM((HALO + rows, LANES), F32)],
            flops=2 * rows * STATE * INNER * 24,
        )
        spilled = shifted(gp[:HALO], -1)
        side_left = lax.dot_general(
            normed_rel, gp[:, :CUT], (((0,), (0,)), ((), ())), preferred_element_type=F32
        ).astype(BF16)
        side_right = lax.dot_general(
            normed_rel, gp[:, CUT:], (((0,), (0,)), ((), ())), preferred_element_type=F32
        ).astype(BF16)
        left_share = reduce_shares(side_left, ("x", "y"))
        right_share = reduce_shares(side_right, ("y", "x"))
        gp_own = jnp.concatenate([gp[HALO:rows], gp[rows:] + spilled], axis=0)
        (left, left2), (right, right2) = sides
        gp_left, gp_right = gp_own[:, :CUT], gp_own[:, CUT:]
        gn_rel = jnp.concatenate(
            [dot_t(gp_left, left) + dot_t(gp_right, right), dot_t(gp_left, left2) + dot_t(gp_right, right2)], axis=1
        )
        gn_high = gn_rel.astype(BF16)
        gn_low = (gn_rel - gn_high.astype(F32)).astype(BF16)
        gn = gn_z + dot_t(gn_high, order) + dot_t(gn_low, order)
        grad, gain_rows = kernel_call(
            norm_back_kernel, [((rows, width), F32), ((8, width), F32)], (gn, h, grad, gain), limit=24,
        )
        in_grads[layer] = jnp.concatenate([z_share, left_share, right_share[:, : SIDE - CUT]], axis=1)
        out_grads[layer] = out_share
        skip_grad = wide_rows[1].reshape(HEADS, HEAD_DIM).sum(axis=1)
        smalls[layer] = jnp.concatenate(
            [
                conv_grads[: CONV_K + 1].reshape(-1), gain_rows[0], wide_rows[0],
                head_grads[0, :HEADS], head_grads[1, :HEADS], skip_grad,
            ]
        )
    flat = jnp.stack(smalls)
    length = flat.shape[1]
    padded = -(-length // LANES) * LANES
    sums = sum_all(jnp.pad(flat, ((0, 0), (0, padded - length))).reshape(-1, LANES))
    sums = sums.reshape(layers_n, padded)

    def share(start, span):
        full = sums[:, start : start + span]
        return lax.dynamic_slice_in_dim(full, me * (span // count), span // count, 1)

    tap_sums = sums[:, : CONV_K * CONV_CH].reshape(layers_n, CONV_K, CONV_CH)
    tap_share = lax.dynamic_slice_in_dim(tap_sums, me * conv_n, conv_n, 2)
    at = CONV_K * CONV_CH
    bias_share = share(at, CONV_CH)
    gain_share = share(at + CONV_CH, width)
    gate_share = share(at + CONV_CH + width, INNER)
    at = at + CONV_CH + width + INNER
    return (
        residual, grad, jnp.stack(in_grads), jnp.stack(out_grads), tap_share, bias_share, gain_share, gate_share,
        sums[:, at : at + HEADS], sums[:, at + HEADS : at + 2 * HEADS], sums[:, at + 2 * HEADS : at + 3 * HEADS],
    )


def solution(mesh):
    return jax.shard_map(
        per_device,
        mesh=mesh,
        in_specs=(
            P("seq", None), P("seq"), P(None, "seq", None), P(None, "seq", None), P(None, None, "seq"),
            P(None, "seq"), P(None, "seq"), P(None, "seq"), P(), P(), P(), P("seq", None),
        ),
        out_specs=(
            P("seq", None), P("seq", None), P(None, "seq", None), P(None, "seq", None), P(None, None, "seq"),
            P(None, "seq"), P(None, "seq"), P(None, "seq"), P(), P(), P(),
        ),
        check_vma=False,
    )
```

time: 2200 us -> 753 us (0.34)
  waiting for transfers between devices: 881 us -> 258 us
  other arithmetic: 512 us -> 48.6 us
  blocking collectives: 294 us -> 0 us
  local copies, waits for them, and re-layouts: 256 us -> 108 us
  matrix products: 213 us -> 77.5 us
  starting transfers between devices: 11.1 us -> 139 us
  Pallas kernels: 0 us -> 93.4 us
    reduce_scatter x4 -> x0, waiting for transfers between devices: 483 us -> none  [the longest x2 395 us: per_device(): lax.psum_scatter(in_term, 'seq', scatter_dimension=0, tiled=True)]
    all_gather x8 -> x2, waiting for transfers between devices: 270 us -> 0.01 us  [per_device(): gathered = [lax.all_gather(pack, 'seq') for pack in packs]]
    ppermute x5 -> x108, waiting for transfers between devices: 0.01 us -> 258 us  [the longest x103 257 us: swap(): return lax.ppermute(value, 'seq', [(i, i ^ flip) for i in range(count)])]
    all_gather x6 -> x0, blocking collectives: 251 us -> none  [the longest x2 94.1 us: per_device(): lax.all_gather(shards[2], 'seq', axis=1, tiled=True)]
    select_n x64 -> x0, other arithmetic: 169 us -> none  [the longest x62 167 us: lap(): jnp.where(position < mine, new, old)]
    add x66 -> x16, other arithmetic: 165 us -> 3.64 us  [the longest x2 1.81 us: per_device(): gp_own = jnp.concatenate([gp[HALO:rows], gp[rows:] + spilled], axis=0)]
    dot_general x40 -> x43, matrix products: 213 us -> 77.5 us  [the longest x18 25.1 us: dot_t(): lax.dot_general(left, right, (((1,), (1,)), ((), ())), preferred_element_...]
    ppermute x5 -> x108, starting transfers between devices: 10.1 us -> 138 us  [the longest x103 126 us: swap(): return lax.ppermute(value, 'seq', [(i, i ^ flip) for i in range(count)])]
  transfers between devices with their start and end apart: 18 -> 110, of which waited for: 9 -> 54; matrix products, arithmetic and copies ran while one was open for 33% -> 25% of each run, Pallas kernels for 0% -> 11%
where the time goes in v1:
time: 753 us; the launch traced here: 740 us
  waiting for transfers between devices  258 us (34%)
  starting transfers between devices  139 us (18%)
  local copies, waits for them, and re-layouts  108 us (14%)
  Pallas kernels  93.4 us (12%)
  matrix products  77.5 us (10%)
  other arithmetic  48.6 us (6%)
  between operations  17.1 us (2%)
    ppermute x103, waiting for transfers between devices, swap(): return lax.ppermute(value, 'seq', [(i, i ^ flip) for i in range(count)])  257 us
    ppermute x103, starting transfers between devices, swap(): return lax.ppermute(value, 'seq', [(i, i ^ flip) for i in range(count)])  126 us
    pallas_call x44, Pallas kernels, kernel_call(): pl.pallas_call(body, out_shape=tuple((jax.ShapeDtypeStruct(*o) for o in o...  93.4 us
    unnamed x402, local copies, waits for them, and re-layouts  47.4 us
    convert_element_type x24, other arithmetic, reduce_shares(): pieces = [total(d).astype(BF16) for d in range(size)]  27.6 us
    dot_general x18, matrix products, dot_t(): lax.dot_general(left, right, (((1,), (1,)), ((), ())), preferred_element_...  25.1 us
    dot_general x17, matrix products, dot(): return jnp.dot(left, right, precision=precision, preferred_element_type=F32)  22.3 us
    slice x8, local copies, waits for them, and re-layouts, reduce_shares(): pieces = [lax.index_in_dim(terms[0], d, axis, False) for d in range(size)]  18.2 us
  transfers between devices with their start and end apart: 110, of which 54 were waited for; matrix products, arithmetic and copies ran while one was open for 25% of the time, Pallas kernels for 11%

profile of v1, /device:TPU:0, one launch (start us, length us, event | category | flops | bytes accessed | tf_op | source)
XLA Modules:
  0.0 740.4 jit_solution(278670701763188350)
XLA Ops:
  11.5 3.0 collective-permute-start.1
  18.6 4.3 collective-permute-start
  23.1 8.7 %collective-permute-done.2 = bf16[32,2432]{1,0:T(8,128)(2,1)S(1)} collective-permute-done((bf16[32,2432]{1,0:T(8,128)(2,1)S(1)}, bf16[32,2432]{1,0:T(8,128)(2,1)S(1)}, u32[]{:S(2)}, u32[]{:S(2)}) %collective-permute-start.2) | collective-permute-done | bytes 155680 | tf_op jit(solution)/shard_map/ppermute | solution.py:41
  34.1 4.6 collective-permute-done.4
  41.0 17.9 %collective-permute-done.5 = bf16[2,4,32,1152]{3,2,1,0:T(8,128)(2,1)S(1)} collective-permute-done((bf16[2,4,32,1152]{3,2,1,0:T(8,128)(2,1)S(1)}, bf16[2,4,32,1152]{3,2,1,0:T(8,128)(2,1)S(1)}, u32[]{:S(2)}, u32[]{:S(2)}) %collective-permute-start.5) | collective-permute-done | bytes 589856 | tf_op jit(solution)/shard_map/ppermute | solution.py:41
  68.9 18.0 %collective-permute-done.8 = bf16[2,4,32,1280]{3,2,1,0:T(8,128)(2,1)S(1)} collective-permute-done((bf16[2,4,32,1280]{3,2,1,0:T(8,128)(2,1)}, bf16[2,4,32,1280]{3,2,1,0:T(8,128)(2,1)S(1)}, u32[]{:S(2)}, u32[]{:S(2)}) %collective-permute-start.8) | collective-permute-done | bytes 655392 | tf_op jit(solution)/shard_map/ppermute | solution.py:41
  100.7 3.7 shard_map.249
  106.6 13.4 %collective-permute-start.21 = (bf16[32,2432]{1,0:T(8,128)(2,1)}, bf16[32,2432]{1,0:T(8,128)(2,1)}, u32[]{:S(2)}, u32[]{:S(2)}) collective-permute-start(bf16[32,2432]{1,0:T(8,128)(2,1)} %pad.36), channel_id=1, source_target_pairs={{0,16},{1,17},{2,18},{3,19},{4,20},{5,21},{6,22},{7,23},{8,24},{9,... | collective-permute-start | bytes 466952 | tf_op jit(solution)/shard_map/ppermute | solution.py:41
  122.0 11.4 %collective-permute-done.21 = bf16[32,2432]{1,0:T(8,128)(2,1)} collective-permute-done((bf16[32,2432]{1,0:T(8,128)(2,1)}, bf16[32,2432]{1,0:T(8,128)(2,1)}, u32[]{:S(2)}, u32[]{:S(2)}) %collective-permute-start.21) | collective-permute-done | bytes 155680 | tf_op jit(solution)/shard_map/ppermute | solution.py:41
  141.0 7.0 collective-permute-done.12.recv
  150.8 2.6 collective-permute-done.13.recv
  154.0 7.6 %collective-permute-done.23 = bf16[4,32,1280]{2,1,0:T(8,128)(2,1)S(1)} collective-permute-done((bf16[4,32,1280]{2,1,0:T(8,128)(2,1)S(1)}, bf16[4,32,1280]{2,1,0:T(8,128)(2,1)S(1)}, u32[]{:S(2)}, u32[]{:S(2)}) %collective-permute-start.23) | collective-permute-done | bytes 327712 | tf_op jit(solution)/shard_map/ppermute | solution.py:41
  163.1 9.5 %shard_map.250.yw = f32[256,2048]{1,0:T(8,128)S(1)} custom-call(f32[256,2304]{1,0:T(8,128)S(1)} %get-tuple-element.156.conv, f32[256,128]{1,0:T(8,128)S(1)} %get-tuple-element.157.dt, f32[256,128]{1,0:T(8,128)S(1)} %get-tuple-element.158.log, f32[8,128]{1,0:T(8,128)S(1)} %get-tuple-element.429.hp, f32[256,128]{1,0:T(8,128)S(1)} %pad.35.mk, ...), custom_call_target="tpu_custom_call" | custom-call | flops 4294967296 | bytes 4861952 | tf_op jit(solution)/shard_map/pallas_call | solution.py:120
  175.9 3.9 collective-permute-done.16.recv
  183.1 10.2 %collective-permute-done.17.recv = f32[128,512]{1,0:T(8,128)S(1)} collective-permute-done((f32[128,512]{1,0:T(8,128)S(1)}, f32[128,512]{1,0:T(8,128)S(1)}, u32[]{:S(2)}, u32[]{:S(2)}) %collective-permute-start.17) | collective-permute-done | bytes 262176 | tf_op jit(solution)/shard_map/ppermute | solution.py:41
  195.0 2.9 fusion.210
  202.4 2.8 copy-done.20
  205.2 3.1 shard_map.258
  211.7 3.1 collective-permute-start.19
  227.4 3.1 shard_map.260
  238.7 2.6 collective-permute-start.30
  241.3 7.3 collective-permute-done.30.recv
  258.9 2.8 slice.1044
  262.9 3.8 collective-permute-start.32
  272.9 5.2 collective-permute-done.33.recv
  279.9 3.3 collective-permute-done.34.recv
  285.1 4.6 collective-permute-done.35.recv
  291.4 6.9 shard_map.261.yw
  300.3 4.1 shard_map.270
  311.8 2.9 collective-permute-done.38.recv
  316.6 2.6 collective-permute-done.39.recv
  337.6 8.4 %convolution_convert_fusion = bf16[2048,1024]{1,0:T(8,128)(2,1)} fusion(bf16[256,2048]{1,0:T(8,128)(2,1)} %copy-done.117, s32[2048]{0:T(1024)} %multiply_add_fusion, f32[256,1024]{1,0:T(8,128)} %g.1), kind=kOutput, calls=%fused_computation.12 | convolution fusion | flops 3228303360 | bytes 6299648 | tf_op jit(solution)/shard_map/dot_general | solution.py:733
  346.1 3.2 slice.1183
  350.7 10.4 %shard_map.278 = (f32[256,2048]{1,0:T(8,128)S(1)}, f32[256,128]{1,0:T(8,128)S(1)}, f32[256,128]{1,0:T(8,128)S(1)}, f32[256,128]{1,0:T(8,128)S(1)}) custom-call(f32[256,2304]{1,0:T(8,128)S(1)} %copy-done.2, f32[256,128]{1,0:T(8,128)S(1)} %copy-done.131, f32[256,128]{1,0:T(8,128)S(1)} %copy-done.39, bf16[256,2048]{1,0:T(8,128)(2,1)S(1)} %copy-done.116, ...), custom_call_target="tpu_custom_call" | custom-call | flops 8589934592 | bytes 6823936 | tf_op jit(solution)/shard_map/pallas_call | solution.py:120
  363.2 8.3 %shard_map.279 = (bf16[272,2432]{1,0:T(8,128)(2,1)S(1)}, f32[8,2304]{1,0:T(8,128)S(1)}, f32[8,128]{1,0:T(8,128)S(1)}) custom-call(f32[128,1024]{1,0:T(8,128)S(1)} %get-tuple-element.246.mine, bf16[128,1024]{1,0:T(8,128)(2,1)S(1)} %collective-permute-done.44.recv, f32[256,2048]{1,0:T(8,128)S(1)} %get-tuple-element.250.gxdt, ...), custom_call_target="tpu_custom_call" | custom-call | flops 3221225472 | bytes 10403844 | tf_op jit(solution)/shard_map/pallas_call | solution.py:120
  377.0 3.0 convolution_convert_fusion.3
  385.7 3.3 fusion.216
  403.3 4.8 shard_map.281
  411.5 10.4 %shard_map.289 = (f32[256,2048]{1,0:T(8,128)S(1)}, f32[256,128]{1,0:T(8,128)S(1)}, f32[256,128]{1,0:T(8,128)S(1)}, f32[256,128]{1,0:T(8,128)S(1)}) custom-call(f32[256,2304]{1,0:T(8,128)S(1)} %get-tuple-element.156.conv, f32[256,128]{1,0:T(8,128)S(1)} %copy-done.127, f32[256,128]{1,0:T(8,128)S(1)} %copy-done.35, ...), custom_call_target="tpu_custom_call" | custom-call | flops 8589934592 | bytes 6823936 | tf_op jit(solution)/shard_map/pallas_call | solution.py:120
  426.1 7.8 %convolution_convert_fusion.1 = bf16[2048,1024]{1,0:T(8,128)(2,1)} fusion(bf16[256,2048]{1,0:T(8,128)(2,1)} %copy-done.112, s32[2048]{0:T(1024)} %multiply_add_fusion, f32[256,1024]{1,0:T(8,128)S(1)} %copy-done.8), kind=kOutput, calls=%fused_computation.13 | convolution fusion | flops 3228303360 | bytes 6299648 | tf_op jit(solution)/shard_map/dot_general | solution.py:733
  445.8 2.7 collective-permute-start.48
  486.6 4.7 fusion.17
  491.4 3.8 add_convert_fusion.1
  495.3 3.0 fusion.33
  498.4 8.4 %shard_map.290 = (bf16[272,2432]{1,0:T(8,128)(2,1)S(1)}, f32[8,2304]{1,0:T(8,128)S(1)}, f32[8,128]{1,0:T(8,128)S(1)}) custom-call(f32[128,1024]{1,0:T(8,128)S(1)} %get-tuple-element.283.mine, bf16[128,1024]{1,0:T(8,128)(2,1)S(1)} %collective-permute-done.53.recv, f32[256,2048]{1,0:T(8,128)S(1)} %copy-done.125, f32[256,128]{1,0:T(8,128)S(1)} %copy-done.133, ...), custom_call_target="tpu_custom_call" | custom-call | flops 3221225472 | bytes 10403844 | tf_op jit(solution)/shard_map/pallas_call | solution.py:120
  506.9 3.0 convolution_convert_fusion.6
  524.3 3.2 collective-permute-start.103
  527.5 3.3 fusion.215
  531.0 4.1 collective-permute-start.104
  538.8 3.1 collective-permute-start.105
  549.6 22.2 %collective-permute-done.106 = f32[230,128]{1,0:T(8,128)S(1)} collective-permute-done((f32[230,128]{1,0:T(8,128)S(1)}, f32[230,128]{1,0:T(8,128)S(1)}, u32[]{:S(2)}, u32[]{:S(2)}) %collective-permute-start.106) | collective-permute-done | bytes 117792 | tf_op jit(solution)/shard_map/ppermute | solution.py:41
  579.0 12.9 %collective-permute-done.80 = bf16[2,4,32,1280]{3,2,1,0:T(8,128)(2,1)} collective-permute-done((bf16[2,4,32,1280]{3,2,1,0:T(8,128)(2,1)}, bf16[2,4,32,1280]{3,2,1,0:T(8,128)(2,1)}, u32[]{:S(2)}, u32[]{:S(2)}) %collective-permute-start.80) | collective-permute-done | bytes 655392 | tf_op jit(solution)/shard_map/ppermute | solution.py:41
  596.0 4.4 collective-permute-done.87
  610.7 2.6 add_convert_fusion.3
  613.3 4.6 collective-permute-done.81
  632.2 6.9 collective-permute-done.75
  639.2 2.8 collective-permute-start.76
  643.8 3.6 collective-permute-done.76
  647.4 2.8 collective-permute-done.78
  651.9 5.9 collective-permute-done.77
  660.0 3.7 collective-permute-done.101
  663.8 8.4 %collective-permute-done.68 = bf16[2,4,32,1152]{3,2,1,0:T(8,128)(2,1)S(1)} collective-permute-done((bf16[2,4,32,1152]{3,2,1,0:T(8,128)(2,1)S(1)}, bf16[2,4,32,1152]{3,2,1,0:T(8,128)(2,1)S(1)}, u32[]{:S(2)}, u32[]{:S(2)}) %collective-permute-start.68) | collective-permute-done | bytes 589856 | tf_op jit(solution)/shard_map/ppermute | solution.py:41
  673.6 21.6 %collective-permute-done.62 = bf16[2,4,32,1280]{3,2,1,0:T(8,128)(2,1)S(1)} collective-permute-done((bf16[2,4,32,1280]{3,2,1,0:T(8,128)(2,1)S(1)}, bf16[2,4,32,1280]{3,2,1,0:T(8,128)(2,1)S(1)}, u32[]{:S(2)}, u32[]{:S(2)}) %collective-permute-start.62) | collective-permute-done | bytes 655392 | tf_op jit(solution)/shard_map/ppermute | solution.py:41
  723.4 6.3 collective-permute-done.59
  (825 shorter events, 328.6 us)
Async XLA Ops:
  7.2 187.8 %all-gather.5.cloned.1.call-start = ((), (), s32[]{:S(2)}) async-start(), calls=%async_computation | async-start | bytes 8650752 | tf_op jit(solution)/shard_map/all_gather | solution.py:636
  10.1 248.8 %all-gather.7.cloned.1.call-start = ((), (), s32[]{:S(2)}) async-start(), calls=%async_computation.1 | async-start | bytes 8650752 | tf_op jit(solution)/shard_map/all_gather | solution.py:636
  11.5 11.5 %collective-permute-start.1 = (bf16[32,2432]{1,0:T(8,128)(2,1)S(1)}, bf16[32,2432]{1,0:T(8,128)(2,1)S(1)}, u32[]{:S(2)}, u32[]{:S(2)}) collective-permute-start(bf16[32,2432]{1,0:T(8,128)(2,1)S(1)} %fusion.135), channel_id=1, source_target_pairs={{0,8},{1,9},{2,10},{3,11},{4,12},{5,13},{6,14},{7,15},{8,0},{9,1},... | collective-permute-start | bytes 466952 | tf_op jit(solution)/shard_map/ppermute | solution.py:41
  14.6 17.2 %collective-permute-start.2 = (bf16[32,2432]{1,0:T(8,128)(2,1)S(1)}, bf16[32,2432]{1,0:T(8,128)(2,1)S(1)}, u32[]{:S(2)}, u32[]{:S(2)}) collective-permute-start(bf16[32,2432]{1,0:T(8,128)(2,1)S(1)} %fusion.135), channel_id=1, source_target_pairs={{0,16},{1,17},{2,18},{3,19},{4,20},{5,21},{6,22},{7,23},{8,24},{9,... | collective-permute-start | bytes 466952 | tf_op jit(solution)/shard_map/ppermute | solution.py:41
  17.2 14.7 %collective-permute-start.3 = (bf16[32,2432]{1,0:T(8,128)(2,1)S(1)}, bf16[32,2432]{1,0:T(8,128)(2,1)S(1)}, u32[]{:S(2)}, u32[]{:S(2)}) collective-permute-start(bf16[32,2432]{1,0:T(8,128)(2,1)S(1)} %fusion.135), channel_id=1, source_target_pairs={{0,24},{1,25},{2,26},{3,27},{4,28},{5,29},{6,30},{7,31},{8,16},{9,... | collective-permute-start | bytes 466952 | tf_op jit(solution)/shard_map/ppermute | solution.py:41
  17.2 48.3 %collective-permute-start.10 = (s32[16]{0:T(128)S(1)}, s32[16]{0:T(128)S(1)}, u32[]{:S(2)}, u32[]{:S(2)}) collective-permute-start(s32[16]{0:T(128)S(1)} %slice_add_fusion.2), channel_id=1, source_target_pairs={{0,1},{1,2},{2,3},{3,4},{4,5},{5,6},{6,7},{7,8},{8,9},{9,10},{10,1... | collective-permute-start | bytes 200 | tf_op jit(solution)/shard_map/ppermute | solution.py:46
  18.6 73.7 %collective-permute-start = (bf16[16,1024]{1,0:T(8,128)(2,1)S(1)}, bf16[16,1024]{1,0:T(8,128)(2,1)S(1)}, u32[]{:S(2)}, u32[]{:S(2)}) collective-permute-start(bf16[16,1024]{1,0:T(8,128)(2,1)S(1)} %slice.787), channel_id=1, source_target_pairs={{0,1},{1,2},{2,3},{3,4},{4,5},{5,6},{6,7},{7,8},{8,9},{9,10},{10,1... | collective-permute-start | bytes 98312 | tf_op jit(solution)/shard_map/ppermute | solution.py:46
  38.8 20.2 %collective-permute-start.5 = (bf16[2,4,32,1152]{3,2,1,0:T(8,128)(2,1)S(1)}, bf16[2,4,32,1152]{3,2,1,0:T(8,128)(2,1)S(1)}, u32[]{:S(2)}, u32[]{:S(2)}) collective-permute-start(bf16[2,4,32,1152]{3,2,1,0:T(8,128)(2,1)S(1)} %get-tuple-element.392), channel_id=1, source_target_pairs={{0,2},{1,3},{2,0},{3,1},{4,6},{5,7},{6,4},{7,5},{8,10},{9,11},{10,... | collective-permute-start | bytes 1769480 | tf_op jit(solution)/shard_map/ppermute | solution.py:41
  40.4 22.1 %collective-permute-start.7 = (bf16[4,32,1280]{2,1,0:T(8,128)(2,1)S(1)}, bf16[4,32,1280]{2,1,0:T(8,128)(2,1)S(1)}, u32[]{:S(2)}, u32[]{:S(2)}) collective-permute-start(bf16[4,32,1280]{2,1,0:T(8,128)(2,1)S(1)} %pad_maximum_fusion.19), channel_id=1, source_target_pairs={{0,2},{1,3},{2,0},{3,1},{4,6},{5,7},{6,4},{7,5},{8,10},{9,11},{10,... | collective-permute-start | bytes 983048 | tf_op jit(solution)/shard_map/ppermute | solution.py:41
  60.1 28.9 %collective-permute-start.6 = (bf16[512,1152]{1,0:T(8,128)(2,1)}, bf16[512,1152]{1,0:T(8,128)(2,1)}, u32[]{:S(2)}, u32[]{:S(2)}) collective-permute-start(bf16[512,1152]{1,0:T(8,128)(2,1)} %bitcast.10), channel_id=1, source_target_pairs={{0,1},{1,0},{2,3},{3,2},{4,5},{5,4},{6,7},{7,6},{8,9},{9,8},{10,11... | collective-permute-start | bytes 3538952 | tf_op jit(solution)/shard_map/ppermute | solution.py:41
  63.3 23.5 %collective-permute-start.8 = (bf16[2,4,32,1280]{3,2,1,0:T(8,128)(2,1)}, bf16[2,4,32,1280]{3,2,1,0:T(8,128)(2,1)S(1)}, u32[]{:S(2)}, u32[]{:S(2)}) collective-permute-start(bf16[2,4,32,1280]{3,2,1,0:T(8,128)(2,1)} %get-tuple-element.378), channel_id=1, source_target_pairs={{0,4},{1,5},{2,6},{3,7},{4,0},{5,1},{6,2},{7,3},{8,12},{9,13},{10,... | collective-permute-start | bytes 1966088 | tf_op jit(solution)/shard_map/ppermute | solution.py:41
  88.9 9.2 %collective-permute-start.9 = (bf16[512,1280]{1,0:T(8,128)(2,1)S(1)}, bf16[512,1280]{1,0:T(8,128)(2,1)}, u32[]{:S(2)}, u32[]{:S(2)}) collective-permute-start(bf16[512,1280]{1,0:T(8,128)(2,1)S(1)} %bitcast.539), channel_id=1, source_target_pairs={{0,1},{1,0},{2,3},{3,2},{4,5},{5,4},{6,7},{7,6},{8,9},{9,8},{10,11... | collective-permute-start | bytes 3932168 | tf_op jit(solution)/shard_map/ppermute | solution.py:41
  106.0 16.0 %collective-permute-start.22 = (bf16[32,2432]{1,0:T(8,128)(2,1)}, bf16[32,2432]{1,0:T(8,128)(2,1)}, u32[]{:S(2)}, u32[]{:S(2)}) collective-permute-start(bf16[32,2432]{1,0:T(8,128)(2,1)} %pad.36), channel_id=1, source_target_pairs={{0,24},{1,25},{2,26},{3,27},{4,28},{5,29},{6,30},{7,31},{8,16},{9,... | collective-permute-start | bytes 466952 | tf_op jit(solution)/shard_map/ppermute | solution.py:41
  106.6 26.8 %collective-permute-start.21 = (bf16[32,2432]{1,0:T(8,128)(2,1)}, bf16[32,2432]{1,0:T(8,128)(2,1)}, u32[]{:S(2)}, u32[]{:S(2)}) collective-permute-start(bf16[32,2432]{1,0:T(8,128)(2,1)} %pad.36), channel_id=1, source_target_pairs={{0,16},{1,17},{2,18},{3,19},{4,20},{5,21},{6,22},{7,23},{8,24},{9,... | collective-permute-start | bytes 466952 | tf_op jit(solution)/shard_map/ppermute | solution.py:41
  120.0 13.4 %collective-permute-start.20 = (bf16[32,2432]{1,0:T(8,128)(2,1)}, bf16[32,2432]{1,0:T(8,128)(2,1)}, u32[]{:S(2)}, u32[]{:S(2)}) collective-permute-start(bf16[32,2432]{1,0:T(8,128)(2,1)} %pad.36), channel_id=1, source_target_pairs={{0,8},{1,9},{2,10},{3,11},{4,12},{5,13},{6,14},{7,15},{8,0},{9,1},... | collective-permute-start | bytes 466952 | tf_op jit(solution)/shard_map/ppermute | solution.py:41
  122.0 15.6 %collective-permute-start.11 = (f32[136,1024]{1,0:T(8,128)}, f32[136,1024]{1,0:T(8,128)S(1)}, u32[]{:S(2)}, u32[]{:S(2)}) collective-permute-start(f32[136,1024]{1,0:T(8,128)} %copy-done.118), channel_id=1, source_target_pairs={{0,1},{1,0},{2,3},{3,2},{4,5},{5,4},{6,7},{7,6},{8,9},{9,8},{10,11... | collective-permute-start | bytes 1671176 | tf_op jit(solution)/shard_map/ppermute | solution.py:41
  134.4 13.7 %collective-permute-start.26 = (bf16[4,32,1152]{2,1,0:T(8,128)(2,1)S(1)}, bf16[4,32,1152]{2,1,0:T(8,128)(2,1)S(1)}, u32[]{:S(2)}, u32[]{:S(2)}) collective-permute-start(bf16[4,32,1152]{2,1,0:T(8,128)(2,1)S(1)} %pad_maximum_fusion.22), channel_id=1, source_target_pairs={{0,4},{1,5},{2,6},{3,7},{4,0},{5,1},{6,2},{7,3},{8,12},{9,13},{10,... | collective-permute-start | bytes 884744 | tf_op jit(solution)/shard_map/ppermute | solution.py:41
  137.8 10.2 %collective-permute-start.12 = (f32[136,512]{1,0:T(8,128)S(1)}, f32[136,512]{1,0:T(8,128)S(1)}, u32[]{:S(2)}, u32[]{:S(2)}) collective-permute-start(f32[136,512]{1,0:T(8,128)S(1)} %get-tuple-element.164), channel_id=1, source_target_pairs={{0,2},{1,3},{2,0},{3,1},{4,6},{5,7},{6,4},{7,5},{8,10},{9,11},{10,... | collective-permute-start | bytes 835592 | tf_op jit(solution)/shard_map/ppermute | solution.py:41
  139.5 22.1 %collective-permute-start.23 = (bf16[4,32,1280]{2,1,0:T(8,128)(2,1)S(1)}, bf16[4,32,1280]{2,1,0:T(8,128)(2,1)S(1)}, u32[]{:S(2)}, u32[]{:S(2)}) collective-permute-start(bf16[4,32,1280]{2,1,0:T(8,128)(2,1)S(1)} %get-tuple-element.380), channel_id=1, source_target_pairs={{0,2},{1,3},{2,0},{3,1},{4,6},{5,7},{6,4},{7,5},{8,10},{9,11},{10,... | collective-permute-start | bytes 983048 | tf_op jit(solution)/shard_map/ppermute | solution.py:41
  148.2 26.6 %collective-permute-start.27 = (bf16[2,4,32,1152]{3,2,1,0:T(8,128)(2,1)S(1)}, bf16[2,4,32,1152]{3,2,1,0:T(8,128)(2,1)S(1)}, u32[]{:S(2)}, u32[]{:S(2)}) collective-permute-start(bf16[2,4,32,1152]{3,2,1,0:T(8,128)(2,1)S(1)} %get-tuple-element.390), channel_id=1, source_target_pairs={{0,2},{1,3},{2,0},{3,1},{4,6},{5,7},{6,4},{7,5},{8,10},{9,11},{10,... | collective-permute-start | bytes 1769480 | tf_op jit(solution)/shard_map/ppermute | solution.py:41
  153.5 8.3 %collective-permute-start.14 = (f32[136,256]{1,0:T(8,128)S(1)}, f32[136,256]{1,0:T(8,128)S(1)}, u32[]{:S(2)}, u32[]{:S(2)}) collective-permute-start(f32[136,256]{1,0:T(8,128)S(1)} %get-tuple-element.170), channel_id=1, source_target_pairs={{0,8},{1,9},{2,10},{3,11},{4,12},{5,13},{6,14},{7,15},{8,0},{9,1},... | collective-permute-start | bytes 417800 | tf_op jit(solution)/shard_map/ppermute | solution.py:41
  161.6 20.3 %collective-permute-start.24 = (bf16[2,4,32,1280]{3,2,1,0:T(8,128)(2,1)S(1)}, bf16[2,4,32,1280]{3,2,1,0:T(8,128)(2,1)S(1)}, u32[]{:S(2)}, u32[]{:S(2)}) collective-permute-start(bf16[2,4,32,1280]{3,2,1,0:T(8,128)(2,1)S(1)} %get-tuple-element.376), channel_id=1, source_target_pairs={{0,4},{1,5},{2,6},{3,7},{4,0},{5,1},{6,2},{7,3},{8,12},{9,13},{10,... | collective-permute-start | bytes 1966088 | tf_op jit(solution)/shard_map/ppermute | solution.py:41
  163.1 9.6 %collective-permute-start.15 = (f32[136,256]{1,0:T(8,128)S(1)}, f32[136,256]{1,0:T(8,128)S(1)}, u32[]{:S(2)}, u32[]{:S(2)}) collective-permute-start(f32[136,256]{1,0:T(8,128)S(1)} %get-tuple-element.173), channel_id=1, source_target_pairs={{0,16},{1,17},{2,18},{3,19},{4,20},{5,21},{6,22},{7,23},{8,24},{9,... | collective-permute-start | bytes 417800 | tf_op jit(solution)/shard_map/ppermute | solution.py:41
  175.9 43.0 %collective-permute-start.28 = (bf16[512,1152]{1,0:T(8,128)(2,1)}, bf16[512,1152]{1,0:T(8,128)(2,1)}, u32[]{:S(2)}, u32[]{:S(2)}) collective-permute-start(bf16[512,1152]{1,0:T(8,128)(2,1)} %bitcast.52), channel_id=1, source_target_pairs={{0,1},{1,0},{2,3},{3,2},{4,5},{5,4},{6,7},{7,6},{8,9},{9,8},{10,11... | collective-permute-start | bytes 3538952 | tf_op jit(solution)/shard_map/ppermute | solution.py:41
  179.9 13.4 %collective-permute-start.17 = (f32[128,512]{1,0:T(8,128)S(1)}, f32[128,512]{1,0:T(8,128)S(1)}, u32[]{:S(2)}, u32[]{:S(2)}) collective-permute-start(f32[128,512]{1,0:T(8,128)S(1)} %get-tuple-element.181), channel_id=1, source_target_pairs={{0,2},{1,3},{2,0},{3,1},{4,6},{5,7},{6,4},{7,5},{8,10},{9,11},{10,... | collective-permute-start | bytes 786440 | tf_op jit(solution)/shard_map/ppermute | solution.py:41
  183.1 37.9 %collective-permute-start.25 = (bf16[512,1280]{1,0:T(8,128)(2,1)}, bf16[512,1280]{1,0:T(8,128)(2,1)}, u32[]{:S(2)}, u32[]{:S(2)}) collective-permute-start(bf16[512,1280]{1,0:T(8,128)(2,1)} %bitcast.46), channel_id=1, source_target_pairs={{0,1},{1,0},{2,3},{3,2},{4,5},{5,4},{6,7},{7,6},{8,9},{9,8},{10,11... | collective-permute-start | bytes 3932168 | tf_op jit(solution)/shard_map/ppermute | solution.py:41
  238.7 9.9 %collective-permute-start.30 = (f32[136,512]{1,0:T(8,128)}, f32[136,512]{1,0:T(8,128)}, u32[]{:S(2)}, u32[]{:S(2)}) collective-permute-start(f32[136,512]{1,0:T(8,128)} %get-tuple-element.196), channel_id=1, source_target_pairs={{0,2},{1,3},{2,0},{3,1},{4,6},{5,7},{6,4},{7,5},{8,10},{9,11},{10,... | collective-permute-start | bytes 835592 | tf_op jit(solution)/shard_map/ppermute | solution.py:41
  289.9 8.4 %collective-permute-start.36 = (f32[128,1024]{1,0:T(8,128)S(1)}, f32[128,1024]{1,0:T(8,128)S(1)}, u32[]{:S(2)}, u32[]{:S(2)}) collective-permute-start(f32[128,1024]{1,0:T(8,128)S(1)} %get-tuple-element.217), channel_id=1, source_target_pairs={{0,1},{1,0},{2,3},{3,2},{4,5},{5,4},{6,7},{7,6},{8,9},{9,8},{10,11... | collective-permute-start | bytes 1572872 | tf_op jit(solution)/shard_map/ppermute | solution.py:41
  329.6 161.7 %collective-permute-start.73 = (bf16[2,2,4,32,2048]{4,3,2,1,0:T(8,128)(2,1)}, bf16[2,2,4,32,2048]{4,3,2,1,0:T(8,128)(2,1)}, u32[]{:S(2)}, u32[]{:S(2)}) collective-permute-start(bf16[2,2,4,32,2048]{4,3,2,1,0:T(8,128)(2,1)} %bitcast.582), channel_id=1, source_target_pairs={{0,1},{1,0},{2,3},{3,2},{4,5},{5,4},{6,7},{7,6},{8,9},{9,8},{10,11... | collective-permute-start | bytes 6291464 | tf_op jit(solution)/shard_map/ppermute | solution.py:41
  336.6 12.7 %collective-permute-start.42 = (bf16[128,256]{1,0:T(8,128)(2,1)}, bf16[128,256]{1,0:T(8,128)(2,1)}, u32[]{:S(2)}, u32[]{:S(2)}) collective-permute-start(bf16[128,256]{1,0:T(8,128)(2,1)} %get-tuple-element.239), channel_id=1, source_target_pairs={{0,4},{1,5},{2,6},{3,7},{4,0},{5,1},{6,2},{7,3},{8,12},{9,13},{10,... | collective-permute-start | bytes 196616 | tf_op jit(solution)/shard_map/ppermute | solution.py:41
  349.3 136.7 %collective-permute-start.97 = (bf16[2,2,4,64,1024]{4,3,2,1,0:T(8,128)(2,1)}, bf16[2,2,4,64,1024]{4,3,2,1,0:T(8,128)(2,1)}, u32[]{:S(2)}, u32[]{:S(2)}) collective-permute-start(bf16[2,2,4,64,1024]{4,3,2,1,0:T(8,128)(2,1)} %bitcast.164), channel_id=1, source_target_pairs={{0,1},{1,0},{2,3},{3,2},{4,5},{5,4},{6,7},{7,6},{8,9},{9,8},{10,11... | collective-permute-start | bytes 6291464 | tf_op jit(solution)/shard_map/ppermute | solution.py:41
  350.3 10.8 %collective-permute-start.43 = (bf16[128,512]{1,0:T(8,128)(2,1)S(1)}, bf16[128,512]{1,0:T(8,128)(2,1)S(1)}, u32[]{:S(2)}, u32[]{:S(2)}) collective-permute-start(bf16[128,512]{1,0:T(8,128)(2,1)S(1)} %get-tuple-element.243), channel_id=1, source_target_pairs={{0,2},{1,3},{2,0},{3,1},{4,6},{5,7},{6,4},{7,5},{8,10},{9,11},{10,... | collective-permute-start | bytes 393224 | tf_op jit(solution)/shard_map/ppermute | solution.py:41
  384.5 110.7 %collective-permute-start.85 = (bf16[2,2,4,32,1152]{4,3,2,1,0:T(8,128)(2,1)}, bf16[2,2,4,32,1152]{4,3,2,1,0:T(8,128)(2,1)}, u32[]{:S(2)}, u32[]{:S(2)}) collective-permute-start(bf16[2,2,4,32,1152]{4,3,2,1,0:T(8,128)(2,1)} %bitcast.584), channel_id=1, source_target_pairs={{0,1},{1,0},{2,3},{3,2},{4,5},{5,4},{6,7},{7,6},{8,9},{9,8},{10,11... | collective-permute-start | bytes 3538952 | tf_op jit(solution)/shard_map/ppermute | solution.py:41
  389.1 157.7 %collective-permute-start.79 = (bf16[2,2,4,32,1280]{4,3,2,1,0:T(8,128)(2,1)}, bf16[2,2,4,32,1280]{4,3,2,1,0:T(8,128)(2,1)}, u32[]{:S(2)}, u32[]{:S(2)}) collective-permute-start(bf16[2,2,4,32,1280]{4,3,2,1,0:T(8,128)(2,1)} %bitcast.120), channel_id=1, source_target_pairs={{0,1},{1,0},{2,3},{3,2},{4,5},{5,4},{6,7},{7,6},{8,9},{9,8},{10,11... | collective-permute-start | bytes 3932168 | tf_op jit(solution)/shard_map/ppermute | solution.py:41
  411.1 22.8 %collective-permute-start.46 = (bf16[144,1024]{1,0:T(8,128)(2,1)}, bf16[144,1024]{1,0:T(8,128)(2,1)}, u32[]{:S(2)}, u32[]{:S(2)}) collective-permute-start(bf16[144,1024]{1,0:T(8,128)(2,1)} %get-tuple-element.260), channel_id=1, source_target_pairs={{0,1},{1,0},{2,3},{3,2},{4,5},{5,4},{6,7},{7,6},{8,9},{9,8},{10,11... | collective-permute-start | bytes 884744 | tf_op jit(solution)/shard_map/ppermute | solution.py:41
  463.1 9.1 %collective-permute-start.51 = (bf16[128,256]{1,0:T(8,128)(2,1)}, bf16[128,256]{1,0:T(8,128)(2,1)}, u32[]{:S(2)}, u32[]{:S(2)}) collective-permute-start(bf16[128,256]{1,0:T(8,128)(2,1)} %get-tuple-element.276), channel_id=1, source_target_pairs={{0,4},{1,5},{2,6},{3,7},{4,0},{5,1},{6,2},{7,3},{8,12},{9,13},{10,... | collective-permute-start | bytes 196616 | tf_op jit(solution)/shard_map/ppermute | solution.py:41
  482.2 139.3 %collective-permute-start.91 = (bf16[2,2,4,64,1024]{4,3,2,1,0:T(8,128)(2,1)}, bf16[2,2,4,64,1024]{4,3,2,1,0:T(8,128)(2,1)}, u32[]{:S(2)}, u32[]{:S(2)}) collective-permute-start(bf16[2,2,4,64,1024]{4,3,2,1,0:T(8,128)(2,1)} %bitcast.580), channel_id=1, source_target_pairs={{0,1},{1,0},{2,3},{3,2},{4,5},{5,4},{6,7},{7,6},{8,9},{9,8},{10,11... | collective-permute-start | bytes 6291464 | tf_op jit(solution)/shard_map/ppermute | solution.py:41
  486.0 124.6 %collective-permute-start.55 = (bf16[2,2,4,32,2048]{4,3,2,1,0:T(8,128)(2,1)}, bf16[2,2,4,32,2048]{4,3,2,1,0:T(8,128)(2,1)}, u32[]{:S(2)}, u32[]{:S(2)}) collective-permute-start(bf16[2,2,4,32,2048]{4,3,2,1,0:T(8,128)(2,1)} %bitcast.581), channel_id=1, source_target_pairs={{0,1},{1,0},{2,3},{3,2},{4,5},{5,4},{6,7},{7,6},{8,9},{9,8},{10,11... | collective-permute-start | bytes 6291464 | tf_op jit(solution)/shard_map/ppermute | solution.py:41
  498.3 74.8 %collective-permute-start.86 = (bf16[2,4,32,1152]{3,2,1,0:T(8,128)(2,1)}, bf16[2,4,32,1152]{3,2,1,0:T(8,128)(2,1)}, u32[]{:S(2)}, u32[]{:S(2)}) collective-permute-start(bf16[2,4,32,1152]{3,2,1,0:T(8,128)(2,1)} %get-tuple-element.356), channel_id=1, source_target_pairs={{0,4},{1,5},{2,6},{3,7},{4,0},{5,1},{6,2},{7,3},{8,12},{9,13},{10,... | collective-permute-start | bytes 1769480 | tf_op jit(solution)/shard_map/ppermute | solution.py:41
  544.9 49.3 %collective-permute-start.74 = (bf16[2,4,32,2048]{3,2,1,0:T(8,128)(2,1)}, bf16[2,4,32,2048]{3,2,1,0:T(8,128)(2,1)}, u32[]{:S(2)}, u32[]{:S(2)}) collective-permute-start(bf16[2,4,32,2048]{3,2,1,0:T(8,128)(2,1)} %get-tuple-element.318), channel_id=1, source_target_pairs={{0,2},{1,3},{2,0},{3,1},{4,6},{5,7},{6,4},{7,5},{8,10},{9,11},{10,... | collective-permute-start | bytes 3145736 | tf_op jit(solution)/shard_map/ppermute | solution.py:41
  546.8 25.0 %collective-permute-start.106 = (f32[230,128]{1,0:T(8,128)S(1)}, f32[230,128]{1,0:T(8,128)S(1)}, u32[]{:S(2)}, u32[]{:S(2)}) collective-permute-start(f32[230,128]{1,0:T(8,128)S(1)} %add.536), channel_id=1, source_target_pairs={{0,2},{1,3},{2,0},{3,1},{4,6},{5,7},{6,4},{7,5},{8,10},{9,11},{10,... | collective-permute-start | bytes 353288 | tf_op jit(solution)/shard_map/ppermute | solution.py:41
  571.8 30.8 %collective-permute-start.98 = (bf16[2,4,64,1024]{3,2,1,0:T(8,128)(2,1)}, bf16[2,4,64,1024]{3,2,1,0:T(8,128)(2,1)}, u32[]{:S(2)}, u32[]{:S(2)}) collective-permute-start(bf16[2,4,64,1024]{3,2,1,0:T(8,128)(2,1)} %get-tuple-element.340), channel_id=1, source_target_pairs={{0,4},{1,5},{2,6},{3,7},{4,0},{5,1},{6,2},{7,3},{8,12},{9,13},{10,... | collective-permute-start | bytes 3145736 | tf_op jit(solution)/shard_map/ppermute | solution.py:41
  574.5 17.4 %collective-permute-start.80 = (bf16[2,4,32,1280]{3,2,1,0:T(8,128)(2,1)}, bf16[2,4,32,1280]{3,2,1,0:T(8,128)(2,1)}, u32[]{:S(2)}, u32[]{:S(2)}) collective-permute-start(bf16[2,4,32,1280]{3,2,1,0:T(8,128)(2,1)} %get-tuple-element.326), channel_id=1, source_target_pairs={{0,2},{1,3},{2,0},{3,1},{4,6},{5,7},{6,4},{7,5},{8,10},{9,11},{10,... | collective-permute-start | bytes 1966088 | tf_op jit(solution)/shard_map/ppermute | solution.py:41
  591.9 8.6 %collective-permute-start.87 = (bf16[4,32,1152]{2,1,0:T(8,128)(2,1)S(1)}, bf16[4,32,1152]{2,1,0:T(8,128)(2,1)S(1)}, u32[]{:S(2)}, u32[]{:S(2)}) collective-permute-start(bf16[4,32,1152]{2,1,0:T(8,128)(2,1)S(1)} %get-tuple-element.354), channel_id=1, source_target_pairs={{0,2},{1,3},{2,0},{3,1},{4,6},{5,7},{6,4},{7,5},{8,10},{9,11},{10,... | collective-permute-start | bytes 884744 | tf_op jit(solution)/shard_map/ppermute | solution.py:41
  606.4 23.9 %collective-permute-start.67 = (bf16[2,2,4,32,1152]{4,3,2,1,0:T(8,128)(2,1)S(1)}, bf16[2,2,4,32,1152]{4,3,2,1,0:T(8,128)(2,1)S(1)}, u32[]{:S(2)}, u32[]{:S(2)}) collective-permute-start(bf16[2,2,4,32,1152]{4,3,2,1,0:T(8,128)(2,1)S(1)} %bitcast.585), channel_id=1, source_target_pairs={{0,1},{1,0},{2,3},{3,2},{4,5},{5,4},{6,7},{7,6},{8,9},{9,8},{10,11... | collective-permute-start | bytes 3538952 | tf_op jit(solution)/shard_map/ppermute | solution.py:41
  607.7 24.2 %collective-permute-start.61 = (bf16[2,2,4,32,1280]{4,3,2,1,0:T(8,128)(2,1)S(1)}, bf16[2,2,4,32,1280]{4,3,2,1,0:T(8,128)(2,1)S(1)}, u32[]{:S(2)}, u32[]{:S(2)}) collective-permute-start(bf16[2,2,4,32,1280]{4,3,2,1,0:T(8,128)(2,1)S(1)} %bitcast.583), channel_id=1, source_target_pairs={{0,1},{1,0},{2,3},{3,2},{4,5},{5,4},{6,7},{7,6},{8,9},{9,8},{10,11... | collective-permute-start | bytes 3932168 | tf_op jit(solution)/shard_map/ppermute | solution.py:41
  624.2 14.9 %collective-permute-start.75 = (bf16[4,32,2048]{2,1,0:T(8,128)(2,1)S(1)}, bf16[4,32,2048]{2,1,0:T(8,128)(2,1)S(1)}, u32[]{:S(2)}, u32[]{:S(2)}) collective-permute-start(bf16[4,32,2048]{2,1,0:T(8,128)(2,1)S(1)} %get-tuple-element.344), channel_id=1, source_target_pairs={{0,4},{1,5},{2,6},{3,7},{4,0},{5,1},{6,2},{7,3},{8,12},{9,13},{10,... | collective-permute-start | bytes 1572872 | tf_op jit(solution)/shard_map/ppermute | solution.py:41
  626.6 17.0 %collective-permute-start.99 = (bf16[4,64,1024]{2,1,0:T(8,128)(2,1)S(1)}, bf16[4,64,1024]{2,1,0:T(8,128)(2,1)S(1)}, u32[]{:S(2)}, u32[]{:S(2)}) collective-permute-start(bf16[4,64,1024]{2,1,0:T(8,128)(2,1)S(1)} %get-tuple-element.338), channel_id=1, source_target_pairs={{0,2},{1,3},{2,0},{3,1},{4,6},{5,7},{6,4},{7,5},{8,10},{9,11},{10,... | collective-permute-start | bytes 1572872 | tf_op jit(solution)/shard_map/ppermute | solution.py:41
  629.2 66.9 %collective-permute-start.92 = (bf16[2,4,64,1024]{3,2,1,0:T(8,128)(2,1)S(1)}, bf16[2,4,64,1024]{3,2,1,0:T(8,128)(2,1)S(1)}, u32[]{:S(2)}, u32[]{:S(2)}) collective-permute-start(bf16[2,4,64,1024]{3,2,1,0:T(8,128)(2,1)S(1)} %get-tuple-element.336), channel_id=1, source_target_pairs={{0,4},{1,5},{2,6},{3,7},{4,0},{5,1},{6,2},{7,3},{8,12},{9,13},{10,... | collective-permute-start | bytes 3145736 | tf_op jit(solution)/shard_map/ppermute | solution.py:41
  630.6 41.6 %collective-permute-start.68 = (bf16[2,4,32,1152]{3,2,1,0:T(8,128)(2,1)S(1)}, bf16[2,4,32,1152]{3,2,1,0:T(8,128)(2,1)S(1)}, u32[]{:S(2)}, u32[]{:S(2)}) collective-permute-start(bf16[2,4,32,1152]{3,2,1,0:T(8,128)(2,1)S(1)} %get-tuple-element.352), channel_id=1, source_target_pairs={{0,4},{1,5},{2,6},{3,7},{4,0},{5,1},{6,2},{7,3},{8,12},{9,13},{10,... | collective-permute-start | bytes 1769480 | tf_op jit(solution)/shard_map/ppermute | solution.py:41
  639.2 8.2 %collective-permute-start.76 = (bf16[32,2048]{1,0:T(8,128)(2,1)S(1)}, bf16[32,2048]{1,0:T(8,128)(2,1)S(1)}, u32[]{:S(2)}, u32[]{:S(2)}) collective-permute-start(bf16[32,2048]{1,0:T(8,128)(2,1)S(1)} %get-tuple-element.366), channel_id=1, source_target_pairs={{0,8},{1,9},{2,10},{3,11},{4,12},{5,13},{6,14},{7,15},{8,0},{9,1},... | collective-permute-start | bytes 393224 | tf_op jit(solution)/shard_map/ppermute | solution.py:41
  642.0 8.2 %collective-permute-start.78 = (bf16[32,2048]{1,0:T(8,128)(2,1)S(1)}, bf16[32,2048]{1,0:T(8,128)(2,1)S(1)}, u32[]{:S(2)}, u32[]{:S(2)}) collective-permute-start(bf16[32,2048]{1,0:T(8,128)(2,1)S(1)} %get-tuple-element.367), channel_id=1, source_target_pairs={{0,24},{1,25},{2,26},{3,27},{4,28},{5,29},{6,30},{7,31},{8,16},{9,... | collective-permute-start | bytes 393224 | tf_op jit(solution)/shard_map/ppermute | solution.py:41
  643.6 14.1 %collective-permute-start.77 = (bf16[32,2048]{1,0:T(8,128)(2,1)S(1)}, bf16[32,2048]{1,0:T(8,128)(2,1)S(1)}, u32[]{:S(2)}, u32[]{:S(2)}) collective-permute-start(bf16[32,2048]{1,0:T(8,128)(2,1)S(1)} %get-tuple-element.368), channel_id=1, source_target_pairs={{0,16},{1,17},{2,18},{3,19},{4,20},{5,21},{6,22},{7,23},{8,24},{9,... | collective-permute-start | bytes 393224 | tf_op jit(solution)/shard_map/ppermute | solution.py:41
  647.4 10.5 %collective-permute-start.100 = (bf16[64,1024]{1,0:T(8,128)(2,1)S(1)}, bf16[64,1024]{1,0:T(8,128)(2,1)S(1)}, u32[]{:S(2)}, u32[]{:S(2)}) collective-permute-start(bf16[64,1024]{1,0:T(8,128)(2,1)S(1)} %get-tuple-element.360), channel_id=1, source_target_pairs={{0,8},{1,9},{2,10},{3,11},{4,12},{5,13},{6,14},{7,15},{8,0},{9,1},... | collective-permute-start | bytes 393224 | tf_op jit(solution)/shard_map/ppermute | solution.py:41
  650.1 8.8 %collective-permute-start.102 = (bf16[64,1024]{1,0:T(8,128)(2,1)S(1)}, bf16[64,1024]{1,0:T(8,128)(2,1)S(1)}, u32[]{:S(2)}, u32[]{:S(2)}) collective-permute-start(bf16[64,1024]{1,0:T(8,128)(2,1)S(1)} %get-tuple-element.361), channel_id=1, source_target_pairs={{0,24},{1,25},{2,26},{3,27},{4,28},{5,29},{6,30},{7,31},{8,16},{9,... | collective-permute-start | bytes 393224 | tf_op jit(solution)/shard_map/ppermute | solution.py:41
  657.9 40.0 %collective-permute-start.56 = (bf16[2,4,32,2048]{3,2,1,0:T(8,128)(2,1)S(1)}, bf16[2,4,32,2048]{3,2,1,0:T(8,128)(2,1)S(1)}, u32[]{:S(2)}, u32[]{:S(2)}) collective-permute-start(bf16[2,4,32,2048]{3,2,1,0:T(8,128)(2,1)S(1)} %get-tuple-element.314), channel_id=1, source_target_pairs={{0,2},{1,3},{2,0},{3,1},{4,6},{5,7},{6,4},{7,5},{8,10},{9,11},{10,... | collective-permute-start | bytes 3145736 | tf_op jit(solution)/shard_map/ppermute | solution.py:41
  659.0 36.2 %collective-permute-start.62 = (bf16[2,4,32,1280]{3,2,1,0:T(8,128)(2,1)S(1)}, bf16[2,4,32,1280]{3,2,1,0:T(8,128)(2,1)S(1)}, u32[]{:S(2)}, u32[]{:S(2)}) collective-permute-start(bf16[2,4,32,1280]{3,2,1,0:T(8,128)(2,1)S(1)} %get-tuple-element.322), channel_id=1, source_target_pairs={{0,2},{1,3},{2,0},{3,1},{4,6},{5,7},{6,4},{7,5},{8,10},{9,11},{10,... | collective-permute-start | bytes 1966088 | tf_op jit(solution)/shard_map/ppermute | solution.py:41
  672.4 26.8 %collective-permute-start.69 = (bf16[4,32,1152]{2,1,0:T(8,128)(2,1)S(1)}, bf16[4,32,1152]{2,1,0:T(8,128)(2,1)S(1)}, u32[]{:S(2)}, u32[]{:S(2)}) collective-permute-start(bf16[4,32,1152]{2,1,0:T(8,128)(2,1)S(1)} %get-tuple-element.350), channel_id=1, source_target_pairs={{0,2},{1,3},{2,0},{3,1},{4,6},{5,7},{6,4},{7,5},{8,10},{9,11},{10,... | collective-permute-start | bytes 884744 | tf_op jit(solution)/shard_map/ppermute | solution.py:41
  696.4 23.3 %collective-permute-start.93 = (bf16[4,64,1024]{2,1,0:T(8,128)(2,1)S(1)}, bf16[4,64,1024]{2,1,0:T(8,128)(2,1)S(1)}, u32[]{:S(2)}, u32[]{:S(2)}) collective-permute-start(bf16[4,64,1024]{2,1,0:T(8,128)(2,1)S(1)} %get-tuple-element.334), channel_id=1, source_target_pairs={{0,2},{1,3},{2,0},{3,1},{4,6},{5,7},{6,4},{7,5},{8,10},{9,11},{10,... | collective-permute-start | bytes 1572872 | tf_op jit(solution)/shard_map/ppermute | solution.py:41
  698.3 17.8 %collective-permute-start.57 = (bf16[4,32,2048]{2,1,0:T(8,128)(2,1)S(1)}, bf16[4,32,2048]{2,1,0:T(8,128)(2,1)S(1)}, u32[]{:S(2)}, u32[]{:S(2)}) collective-permute-start(bf16[4,32,2048]{2,1,0:T(8,128)(2,1)S(1)} %get-tuple-element.342), channel_id=1, source_target_pairs={{0,4},{1,5},{2,6},{3,7},{4,0},{5,1},{6,2},{7,3},{8,12},{9,13},{10,... | collective-permute-start | bytes 1572872 | tf_op jit(solution)/shard_map/ppermute | solution.py:41
  718.4 11.3 %collective-permute-start.59 = (bf16[32,2048]{1,0:T(8,128)(2,1)S(1)}, bf16[32,2048]{1,0:T(8,128)(2,1)S(1)}, u32[]{:S(2)}, u32[]{:S(2)}) collective-permute-start(bf16[32,2048]{1,0:T(8,128)(2,1)S(1)} %get-tuple-element.365), channel_id=1, source_target_pairs={{0,16},{1,17},{2,18},{3,19},{4,20},{5,21},{6,22},{7,23},{8,24},{9,... | collective-permute-start | bytes 393224 | tf_op jit(solution)/shard_map/ppermute | solution.py:41
  719.9 11.0 %collective-permute-start.94 = (bf16[64,1024]{1,0:T(8,128)(2,1)S(1)}, bf16[64,1024]{1,0:T(8,128)(2,1)S(1)}, u32[]{:S(2)}, u32[]{:S(2)}) collective-permute-start(bf16[64,1024]{1,0:T(8,128)(2,1)S(1)} %get-tuple-element.357), channel_id=1, source_target_pairs={{0,8},{1,9},{2,10},{3,11},{4,12},{5,13},{6,14},{7,15},{8,0},{9,1},... | collective-permute-start | bytes 393224 | tf_op jit(solution)/shard_map/ppermute | solution.py:41
  720.9 10.0 %collective-permute-start.96 = (bf16[64,1024]{1,0:T(8,128)(2,1)S(1)}, bf16[64,1024]{1,0:T(8,128)(2,1)S(1)}, u32[]{:S(2)}, u32[]{:S(2)}) collective-permute-start(bf16[64,1024]{1,0:T(8,128)(2,1)S(1)} %get-tuple-element.358), channel_id=1, source_target_pairs={{0,24},{1,25},{2,26},{3,27},{4,28},{5,29},{6,30},{7,31},{8,16},{9,... | collective-permute-start | bytes 393224 | tf_op jit(solution)/shard_map/ppermute | solution.py:41
  723.0 9.5 %collective-permute-start.95 = (bf16[64,1024]{1,0:T(8,128)(2,1)S(1)}, bf16[64,1024]{1,0:T(8,128)(2,1)S(1)}, u32[]{:S(2)}, u32[]{:S(2)}) collective-permute-start(bf16[64,1024]{1,0:T(8,128)(2,1)S(1)} %get-tuple-element.359), channel_id=1, source_target_pairs={{0,16},{1,17},{2,18},{3,19},{4,20},{5,21},{6,22},{7,23},{8,24},{9,... | collective-permute-start | bytes 393224 | tf_op jit(solution)/shard_map/ppermute | solution.py:41
  (247 other events, 1532.5 us)
Sparse Core Ops, SparseCore 0:
  11.5 100.1 all-gather.4
  114.5 96.6 all-gather.6

commit v2 on v1

v2 whole, which is shorter than its diff:
```python
from functools import partial

import jax
import jax.numpy as jnp
import numpy as np
from jax import lax
from jax.experimental import pallas as pl
from jax.experimental.pallas import tpu as pltpu
from jax.sharding import PartitionSpec as P

HEADS = 32
HEAD_DIM = 64
STATE = 128
CONV_K = 4
INNER = 2048
CONV_CH = 2304
SIDE = CONV_CH + HEADS
WIDE = 2432
CUT = 1280
LANES = 128
PAIRS = HEADS // 2
HALO = 16
LEAD = HALO - (CONV_K - 1)
FAR = -1e30

EPS = 1e-05
F32 = jnp.float32
BF16 = jnp.bfloat16
EXACT = lax.Precision.HIGHEST
MB = 1024 * 1024
CAP = 16 * MB


def axes_of(count):
    side = 4 if count >= 128 else 2
    plane = 2 * side * side
    return {"c": (2, 1), "x": (side, 2), "y": (side, 2 * side), "z": (count // plane, plane)}


def swap(value, flip):
    count = lax.axis_size("seq")
    return lax.ppermute(value, "seq", [(i, i ^ flip) for i in range(count)])


def shifted(shard, by):
    count = lax.axis_size("seq")
    return lax.ppermute(shard, "seq", [(i, i + by) for i in range(count) if 0 <= i + by < count])


def relative_places(count):
    axes = axes_of(count)
    places = np.zeros((1,), np.int32)
    for name in ("c", "y", "x", "z"):
        size, shift = axes[name]
        places = (places[:, None] + np.arange(size, dtype=np.int32)[None, :] * shift).reshape(-1)
    return places


def column_order(places, me, block):
    count = len(places)
    places = jnp.asarray(np.repeat(places, block))
    inner = jnp.asarray(np.tile(np.arange(block, dtype=np.int32), count))
    source = (places ^ me) * block + inner
    return (jnp.arange(count * block)[:, None] == source[None, :]).astype(BF16)


class Gather:

    def __init__(self, shard):
        self.axes = axes_of(lax.axis_size("seq"))
        self.rows = shard.shape[0]
        self.kind = shard.dtype
        self.shard, self.sent = shard, self.send(shard, "z")

    def send(self, value, name):
        size, shift = self.axes[name]
        return [swap(value, d * shift) for d in range(1, size)]

    def outs(self, *lead):
        return [((*lead, self.rows, CUT), self.kind), ((*lead, self.rows, WIDE - CUT), self.kind)]

    def line(self, deps=()):
        everything = slice(None)
        cuts = ((everything, slice(0, CUT)), (everything, slice(CUT, WIDE)))
        pieces = [
            (value, side, cuts[side], d) for side in range(2) for d, value in enumerate([self.shard, *self.sent])
        ]
        self.left, self.right = copies_call(pieces, self.outs(self.axes["z"][0]), deps)
        self.sent = self.send(self.left, "x"), self.send(self.right, "y")
        return self.left

    def plane(self, deps=()):
        sides = ((self.left, *self.sent[0]), (self.right, *self.sent[1]))
        pieces = [(value, side, None, d) for side in range(2) for d, value in enumerate(sides[side])]
        line, across, up = (self.axes[name][0] for name in ("z", "x", "y"))
        outs = [self.outs(across, line)[0], self.outs(up, line)[1]]
        self.left, self.right = copies_call(pieces, outs, deps)
        self.sent = self.send(self.left, "y"), self.send(self.right, "x")
        return self.left

    def whole(self, deps=()):
        line, across, up = (self.axes[name][0] for name in ("z", "x", "y"))
        pieces = [(value, 0, None, d) for d, value in enumerate([self.left, *self.sent[0]])]
        pieces += [
            (value, 1, i, (i, d)) for d, value in enumerate([self.right, *self.sent[1]]) for i in range(up)
        ]
        left, right = copies_call(pieces, self.outs(up, across, line), deps)
        left, right = left.reshape(-1, left.shape[-1]), right.reshape(-1, right.shape[-1])
        return (left, swap(left, 1)), (right, swap(right, 1))


class Shares:

    def __init__(self, keep, send):
        line, plane = axes_of(lax.axis_size("seq"))["z"]
        self.groups = [(plane // 2, 2), (line, plane)]
        shape = (plane // 2, line, keep.shape[0] // (plane // 2 * line), keep.shape[1])
        self.send = send
        self.terms = [keep.reshape(shape), swap(send.reshape(shape), 1)]

    def step(self, deps=(), behind=None):
        size, shift = self.groups.pop(0)
        if deps:
            pieces = list(
                kernel_call(pieces_kernel, [(self.terms[0].shape[1:], BF16)] * size, self.terms, deps=deps)
            )
        else:
            none = 0.0
            if behind is not None:
                none = jnp.minimum(jnp.abs(behind[(0,) * behind.ndim].astype(F32)), 0.0)
            pieces = []
            for d in range(size):
                picked = [t[d].astype(F32) for t in self.terms]
                pieces.append((sum(picked[1:], picked[0]) + none).astype(BF16))
        self.terms = [pieces[0]] + [swap(pieces[d], d * shift) for d in range(1, size)]
        return pieces


def pieces_kernel(*refs):
    size = refs[0].shape[0]
    terms, outs = refs[:-size], refs[-size:]
    for d, out in enumerate(outs):
        total = terms[0][d].astype(F32)
        for term in terms[1:]:
            total = total + term[d].astype(F32)
        out[...] = total.astype(BF16)


def turned_dot(left, right):
    return lax.dot_general(left, right, (((0,), (0,)), ((), ())), preferred_element_type=F32).astype(BF16)


def share_terms(left, right):
    half = left.shape[1] // 2
    return Shares(turned_dot(left[:, :half], right), turned_dot(left[:, half:], right))


def plane_first(count):
    plane = axes_of(count)["z"][1]
    return np.arange(count).reshape(-1, plane).T.reshape(-1)


def scatter_planes(grad):
    count = lax.axis_size("seq")
    plane = axes_of(count)["z"][1]
    groups = np.arange(count).reshape(-1, plane).tolist()
    return lax.psum_scatter(grad, "seq", scatter_dimension=0, tiled=True, axis_index_groups=groups)


def scatter_lines(grad):
    count = lax.axis_size("seq")
    plane = axes_of(count)["z"][1]
    groups = np.arange(count).reshape(-1, plane).T.tolist()
    return lax.psum_scatter(grad, "seq", scatter_dimension=0, tiled=True, axis_index_groups=groups)


def round_kernel(value, out):
    out[...] = value[...].astype(BF16)


def add_kernel(left, right, *outs):
    total = left[...].astype(F32) + right[...].astype(F32)
    for out in outs:
        out[...] = total.astype(out.dtype)


def sum_rounds(value, first, last, deps=()):
    flip = first
    while flip >= last:
        kind = BF16 if flip > 1 else F32
        (value,) = kernel_call(add_kernel, [(value.shape, kind)], (value, swap(value, flip)), deps=deps)
        flip, deps = flip // 2, ()
    return value


def gather_small(value):
    flip = 1
    while flip < lax.axis_size("seq"):
        value = jnp.concatenate([value, swap(value, flip)], axis=0)
        flip *= 2
    return value


def held_bytes(shape, kind):
    *lead, rows, lanes = (1, *shape) if len(shape) < 2 else shape
    rows, lanes = -(-rows // 16) * 16, -(-lanes // LANES) * LANES
    return int(np.prod(lead, dtype=np.int64)) * rows * lanes * jnp.dtype(kind).itemsize


def room_for(arrays, scratch):
    total = sum(held_bytes(*a) for a in arrays) + sum(held_bytes(r.shape, r.dtype) for r in scratch)
    return total + total // 8 + 3 * MB


def far(array):
    return pltpu.with_memory_space_constraint(array, pltpu.HBM)


def kernel_call(body, outs, args, scratch=(), flops=0, deps=()):
    places = [pltpu.SMEM if a.dtype == jnp.int32 else pltpu.VMEM for a in args] + [pl.ANY] * len(deps)
    known = len(args)

    def run(*refs):
        body(*refs[:known], *refs[known + len(deps) :])

    size = sum(int(np.prod(a.shape)) * a.dtype.itemsize for a in args) + sum(
        int(np.prod(o[0])) * jnp.dtype(o[1]).itemsize for o in outs
    )
    return pl.pallas_call(
        run,
        out_shape=tuple(jax.ShapeDtypeStruct(*o) for o in outs),
        in_specs=[pl.BlockSpec(memory_space=p) for p in places],
        out_specs=tuple(pl.BlockSpec(memory_space=pltpu.VMEM) for _ in outs),
        scratch_shapes=list(scratch),
        compiler_params=pltpu.CompilerParams(vmem_limit_bytes=min(CAP, room_for([(a.shape, a.dtype) for a in args] + list(outs), scratch))
        ),
        cost_estimate=pl.CostEstimate(flops=flops, bytes_accessed=size, transcendentals=0),
    )(*args, *deps)


def streamed_call(body, outs, args, scratch=(), flops=0, streamed=None, raw=()):
    places = [pltpu.SMEM if a.dtype == jnp.int32 else pltpu.VMEM for a in args]
    size = sum(int(np.prod(a.shape)) * a.dtype.itemsize for a in (*args, streamed)) + sum(
        int(np.prod(o[0])) * jnp.dtype(o[1]).itemsize for o in (*outs, *raw)
    )
    return pl.pallas_call(
        body,
        out_shape=tuple(jax.ShapeDtypeStruct(*o) for o in (*outs, *raw)),
        in_specs=[pl.BlockSpec(memory_space=p) for p in (pltpu.HBM, *places)],
        out_specs=tuple(pl.BlockSpec(memory_space=p) for p in [pltpu.VMEM] * len(outs) + [pltpu.HBM] * len(raw)),
        scratch_shapes=[*scratch, pltpu.SemaphoreType.DMA((3 * len(raw),))],
        compiler_params=pltpu.CompilerParams(vmem_limit_bytes=room_for([], scratch) + 8 * MB),
        cost_estimate=pl.CostEstimate(flops=flops, bytes_accessed=size, transcendentals=0),
    )(streamed, *args)


def copies_call(pieces, outs, deps=()):
    arrays = [p[0] for p in pieces]
    known, written = len(arrays), len(outs)

    def run(*refs):
        refs = refs[:known] + refs[known + len(deps) :]
        results, held, (sems, out_sems) = refs[known : known + written], refs[known + written : -2], refs[-2:]
        copies = []
        for k, (_, out, source, target) in enumerate(pieces):
            src = refs[k] if source is None else refs[k].at[source]
            copies.append(pltpu.make_async_copy(src, held[out].at[target], sems.at[k]))
            copies[-1].start()
        for copy in copies:
            copy.wait()
        copies = []
        for k in range(written):
            copies.append(pltpu.make_async_copy(held[k], results[k], out_sems.at[k]))
            copies[-1].start()
        for copy in copies:
            copy.wait()

    size = sum(2 * int(np.prod(o[0])) * jnp.dtype(o[1]).itemsize for o in outs)
    return pl.pallas_call(
        run,
        out_shape=tuple(jax.ShapeDtypeStruct(*o) for o in outs),
        in_specs=[pl.BlockSpec(memory_space=pltpu.HBM)] * known + [pl.BlockSpec(memory_space=pl.ANY)] * len(deps),
        out_specs=tuple(pl.BlockSpec(memory_space=pltpu.HBM) for _ in outs),
        scratch_shapes=[pltpu.VMEM(*o) for o in outs]
        + [pltpu.SemaphoreType.DMA((known,)), pltpu.SemaphoreType.DMA((written,))],
        compiler_params=pltpu.CompilerParams(vmem_limit_bytes=room_for(outs, ())),
        cost_estimate=pl.CostEstimate(flops=0, bytes_accessed=size, transcendentals=0),
    )(*arrays, *deps)


def copy_kernel(value, out):
    out[...] = value[...]


def after(value, *deps):
    return kernel_call(copy_kernel, [(value.shape, value.dtype)], (value,), deps=deps)[0]


def dot(left, right, precision=None):
    return jnp.dot(left, right, precision=precision, preferred_element_type=F32)


def dot_t(left, right):
    return lax.dot_general(left, right, (((1,), (1,)), ((), ())), preferred_element_type=F32)


def halves(value):
    high = value.astype(BF16)
    return high, (value - high.astype(F32)).astype(BF16)


def fine(form, left, right):
    (lh, ll), (rh, rl) = halves(left), halves(right)
    return form(lh, rh) + (form(ll, rh) + form(lh, rl))


def lanes_of(rows):
    return lax.broadcasted_iota(jnp.int32, (rows, LANES), 1)


def spread(values, pair):
    low = lanes_of(values.shape[0]) < HEAD_DIM
    return jnp.where(low, values[:, 2 * pair : 2 * pair + 1], values[:, 2 * pair + 1 : 2 * pair + 2])


def spread_row(row):
    return jnp.concatenate([spread(row, pair) for pair in range(PAIRS)], axis=1)


def head_sums(product, pair):
    rows = lax.broadcasted_iota(jnp.int32, (LANES, LANES), 0)
    cols = lax.broadcasted_iota(jnp.int32, (LANES, LANES), 1)
    pick = (cols == 2 * pair + (rows >= HEAD_DIM).astype(jnp.int32)).astype(BF16)
    high = product.astype(BF16)
    low = (product - high.astype(F32)).astype(BF16)
    return dot(high, pick) + dot(low, pick)


def sigmoid(v):
    return 1.0 / (1.0 + jnp.exp(-v))


def silu(v):
    return v * sigmoid(v)


def parted(j, parts):
    half = PAIRS // 2
    return parts[j // half], tile(j % half)


def tile(pair):
    return slice(pair * LANES, (pair + 1) * LANES)


def pack_row(row):
    first = row.astype(BF16).astype(F32)
    second = (row - first).astype(BF16).astype(F32)
    third = row - first - second
    place = lax.broadcasted_iota(jnp.int32, (16, row.shape[1]), 0)
    packed = jnp.where(place == 0, first, jnp.where(place == 1, second, third))
    return jnp.where(place < 3, packed, 0.0).astype(BF16)


def unpack_row(rows):
    return jnp.sum(rows.astype(F32), axis=0, keepdims=True)


def emit_msg(total, keep, msg_o):
    msg_o[0:STATE, :] = total.astype(msg_o.dtype)
    if msg_o.dtype == F32:
        msg_o[STATE:, :] = jnp.broadcast_to(keep, (msg_o.shape[0] - STATE, keep.shape[1]))
    else:
        msg_o[STATE:, :] = pack_row(keep)


def read_msg(recv):
    if recv.dtype == F32:
        return recv[0:STATE, :], recv[STATE : STATE + 1, :]
    return recv[0:STATE, :].astype(F32), unpack_row(recv[STATE:, :])


def emit_halves(total, keep, upper, own_o, msg_o):
    half = total.shape[1] // 2
    low, high = total[:, :half], total[:, half:]
    klow, khigh = keep[:, :half], keep[:, half:]
    emit_msg(jnp.where(upper, high, low), jnp.where(upper, khigh, klow), own_o)
    emit_msg(jnp.where(upper, low, high), jnp.where(upper, klow, khigh), msg_o)


def bit_of(me, flip):
    return (me[0] & flip) != 0


def state_out(width, kind=F32):
    return ((STATE + (8 if kind == F32 else 16), width), kind)


def in_order(relative, place, back):
    size = len(relative)
    ordered = []
    for step in range(size):
        member = size - 1 - step if back else step
        value = relative[0]
        for d in range(1, size):
            value = jnp.where(jnp.bitwise_xor(place, member) == d, relative[d], value)
        ordered.append(value)
    return ordered


def place_of(me, shift, size):
    return jnp.bitwise_and(lax.shift_right_logical(me[0], shift.bit_length() - 1), size - 1)


def pair_kernel(own, recv, me, first_o, mine_o, m1, m2, m3, joined, *, back):
    other, kother = read_msg(recv)
    mine, kmine = read_msg(own)
    first = jnp.logical_xor(bit_of(me, 1), not back)
    t_first, k_first = jnp.where(first, mine, other), jnp.where(first, kmine, kother)
    t_second, k_second = jnp.where(first, other, mine), jnp.where(first, kother, kmine)
    emit_msg(t_first, k_first, first_o)
    emit_msg(k_second * t_first + t_second, k_first * k_second, joined)
    place = place_of(me, 2, 4)
    width = mine_o.shape[1]
    for d, out in enumerate((mine_o, m1, m2, m3)):
        at = pl.ds(pl.multiple_of(jnp.bitwise_xor(place, d) * width, LANES), width)
        emit_msg(joined[0:STATE, at], joined[STATE : STATE + 1, at], out)


def scan_group(own, recvs, place, back):
    read = [read_msg(r) for r in (own, *recvs)]
    totals = in_order([r[0] for r in read], place, back)
    keeps = in_order([r[1] for r in read], place, back)
    prefixes, value, decay = [], jnp.zeros_like(totals[0]), jnp.ones_like(keeps[0])
    for t, k in zip(totals, keeps):
        prefixes.append((value, decay))
        value, decay = k * value + t, decay * k
    return prefixes, value, decay


def own_prefix(prefixes, place, back):
    size = len(prefixes)
    value, decay = prefixes[0]
    for step in range(1, size):
        mine = place == (size - 1 - step if back else step)
        value = jnp.where(mine, prefixes[step][0], value)
        decay = jnp.where(mine, prefixes[step][1], decay)
    return value, decay


def plane_kernel(mine, r1, r2, r3, me, pre_o, *outs, back):
    prefixes, value, decay = scan_group(mine, (r1, r2, r3), place_of(me, 2, 4), back)
    for step, (prefix, kprefix) in enumerate(prefixes):
        emit_msg(prefix, kprefix, pre_o.at[3 - step if back else step])
    for out in outs:
        emit_msg(value, decay, out)


def line_kernel(own, *refs, size, shift, back, carried, final):
    recvs, refs = refs[: size - 1], refs[size - 1 :]
    if carried:
        state, *refs = refs
    if final:
        pre, *refs = refs
    me, *outs = refs
    place = place_of(me, shift, size)
    prefixes, value, decay = scan_group(own, recvs, place, back)
    into, kinto = own_prefix(prefixes, place, back)
    if carried:
        before, kbefore = read_msg(state)
        into, kinto = kbefore * into + before, kbefore * kinto
    if not final:
        emit_msg(into, kinto, outs[0])
        for out in outs[1:]:
            emit_msg(value, decay, out)
        return
    plane = place_of(me, 2, 4)
    for d, out in enumerate(outs):
        prefix, kprefix = read_msg(pre.at[jnp.bitwise_xor(plane, d)])
        out[...] = (kprefix * into + prefix).astype(out.dtype)


def down_kernel(mine, r1, r2, r3, first, me, mine_o, msg_o, whole, *, back):
    place = place_of(me, 2, 4)
    width = mine.shape[1]
    for d, ref in enumerate((mine, r1, r2, r3)):
        at = pl.ds(pl.multiple_of(jnp.bitwise_xor(place, d) * width, LANES), width)
        whole[:, at] = ref[...].astype(F32)
    into = whole[...]
    t_first, k_first = read_msg(first)
    beyond = k_first * into + t_first
    second = jnp.logical_xor(bit_of(me, 1), back)
    mine_o[...] = jnp.where(second, beyond, into)
    msg_o[...] = jnp.where(second, into, beyond).astype(msg_o.dtype)


def join_halves(mine, recv, upper):
    theirs = recv[...].astype(F32)
    own = mine[...]
    return jnp.where(upper, theirs, own), jnp.where(upper, own, theirs)


def exchange(own, msg, me, back, deps=((), (), (), ())):
    count = lax.axis_size("seq")
    kind = msg.dtype
    width = INNER // 2
    quarter = width // 4
    part, message = state_out(quarter), state_out(quarter, kind)
    both = [message] if kind == F32 else [part, message]
    recv = swap(msg, 1)
    first, mine, *msgs = kernel_call(
        partial(pair_kernel, back=back), [state_out(width), part] + [message] * 3,
        (own, recv, me), deps=deps[0], scratch=[pltpu.VMEM(*state_out(width))],
    )
    recvs = [swap(m, 2 * (d + 1)) for d, m in enumerate(msgs)]
    pre, *totals = kernel_call(
        partial(plane_kernel, back=back), [((4, *part[0]), F32)] + both,
        (mine, *recvs, me), deps=deps[1],
    )
    carried = ()
    shift = 8
    while True:
        size = min(4, count // shift)
        recvs = [swap(totals[-1], shift * d) for d in range(1, size)]
        final = shift * size == count
        form = partial(line_kernel, size=size, shift=shift, back=back, carried=bool(carried), final=final)
        shift *= size
        if final:
            break
        state, *totals = kernel_call(form, [part] + both, (totals[0], *recvs, *carried, me))
        carried = (state,)
    mine, *msgs = kernel_call(
        form, [((STATE, quarter), F32)] + [((STATE, quarter), kind)] * 3,
        (totals[0], *recvs, *carried, pre, me), deps=deps[2],
    )
    recvs = [swap(m, 2 * (d + 1)) for d, m in enumerate(msgs)]
    mine, msg = kernel_call(
        partial(down_kernel, back=back), [((STATE, width), F32), ((STATE, width), kind)],
        (mine, *recvs, first, me), deps=deps[3], scratch=[pltpu.VMEM((STATE, width), F32)],
    )
    return mine, swap(msg, 1)


def norm_kernel(h, halo, gain, out):
    for ref, at in ((halo, slice(0, HALO)), (h, slice(HALO, HALO + h.shape[0]))):
        v = ref[...].astype(F32)
        inv = lax.rsqrt(jnp.mean(v * v, axis=-1, keepdims=True) + EPS)
        out[at, :] = (v * inv * gain[0:1, :]).astype(BF16)


def norm_back_kernel(gn, h, g, gain, wide, *refs):
    *others, out, wide_o = refs
    v = h[...].astype(F32)
    grad = gn[...]
    inv = lax.rsqrt(jnp.mean(v * v, axis=-1, keepdims=True) + EPS)
    n = v * inv
    q = grad * gain[0:1, :]
    out[...] = g[...] + inv * (q - n * jnp.mean(q * n, axis=-1, keepdims=True))
    wide_o[0:8, :] = wide[...]
    wide_o[6:7, 0 : v.shape[1]] = jnp.sum(grad * n, axis=0, keepdims=True)
    for other in others:
        wide_o[8:, :] = other[...]


def grads_kernel(gn, normed, mixed, gz, *outs, steps):
    half = INNER // 2
    several, rows = outs[0].shape[0], outs[0].shape[1] // 4
    for k, out in enumerate(outs):

        @pl.when(pl.program_id(0) // steps == k)
        def _(out=out):
            turned = lax.dot_general(gn[...], mixed[...], (((0,), (0,)), ((), ())), preferred_element_type=F32)
            out[:, 2 * rows :, :] = turned.astype(BF16).reshape(several, 2 * rows, half)
            narrow = normed[HALO:, :]
            for q in range(2):
                part = gz[:, q * half : (q + 1) * half]
                turned = lax.dot_general(narrow, part, (((0,), (0,)), ((), ())), preferred_element_type=F32)
                out[:, q * rows : (q + 1) * rows, :] = turned.astype(BF16).reshape(several, rows, half)


def grads_call(gn, normed, mixed, gz, count, parts):
    rows, half = mixed.shape
    wide = 2 * LANES
    several = wide * count // INNER
    steps = count // several // parts
    shape = (several, 4 * half // count, half)

    def share(k):
        return pl.BlockSpec(shape, lambda i: (jnp.clip(i - k * steps, 0, steps - 1), 0, 0))

    return pl.pallas_call(
        partial(grads_kernel, steps=steps),
        grid=(parts * steps,),
        out_shape=[jax.ShapeDtypeStruct((count // parts, *shape[1:]), BF16)] * parts,
        in_specs=[
            pl.BlockSpec((rows, wide), lambda i: (0, i)), pl.BlockSpec((HALO + rows, wide // 2), lambda i: (0, i)),
            pl.BlockSpec(mixed.shape, lambda i: (0, 0)), pl.BlockSpec(gz.shape, lambda i: (0, 0)),
        ],
        out_specs=[share(k) for k in range(parts)],
        compiler_params=pltpu.CompilerParams(vmem_limit_bytes=14 * MB),
        cost_estimate=pl.CostEstimate(flops=8 * rows * half * half, bytes_accessed=10 * MB, transcendentals=0),
    )(gn, normed, mixed, gz)


def own_rows_kernel(gp, spilled, gz, out, gz_o):
    gz_o[...] = gz[...]
    end = out.shape[0] - HALO
    out[0:end, :] = gp[HALO : HALO + end, :]
    out[end:, :] = (gp[HALO + end :, :].astype(F32) + spilled[...].astype(F32)).astype(BF16)


def shares_kernel(*refs, split):
    terms, (in_o, out_o) = refs[:-2], refs[-2:]
    layers_n, rows = in_o.shape[:2]
    half = INNER // 2
    at = 0
    for layer in range(layers_n):
        sums = []
        for size in split[layer]:
            total = terms[at][...].astype(F32)
            for term in terms[at + 1 : at + size]:
                total = total + term[...].astype(F32)
            sums.append(total)
            at += size
        pack, side = sums
        in_o[layer, :, 0:half] = pack[0:rows]
        in_o[layer, :, half:INNER] = pack[rows : 2 * rows]
        in_o[layer, :, INNER:] = side[:, :SIDE]
        out_o[layer] = pack[2 * rows :]


def triangle(rows, lower):
    r = lax.broadcasted_iota(jnp.int32, (rows, rows), 0)
    c = lax.broadcasted_iota(jnp.int32, (rows, rows), 1)
    return r >= c if lower else r <= c


def conv_state_kernel(pc, cw, hp, mk, me, left_o, right_o, bc_o, dt_o, log_o, own_o, msg_o, xw, *low, precise):
    rows = mk.shape[0]
    marks = mk[...]
    raw = pc[HALO:, CONV_CH:WIDE].astype(F32) + hp[0:1, :]
    soft = jnp.maximum(raw, 0.0) + jnp.log1p(jnp.exp(-jnp.abs(raw)))
    dt = jnp.where(lanes_of(rows) < HEADS, soft, 0.0)
    log = dot(triangle(rows, True).astype(F32), dt * hp[1:2, :], EXACT)
    last = log[rows - 1 : rows, :]
    weight = marks[:, 4:5] * jnp.exp(last - log) * dt
    dt_o[...] = dt
    log_o[...] = log
    b_cols = None
    for j in range(CONV_CH // LANES):
        ext = pc[:, tile(j)].astype(F32)
        out = cw[4:5, tile(j)] + cw[3:4, tile(j)] * ext[HALO:, :]
        for k in range(CONV_K - 1):
            out = out + cw[k : k + 1, tile(j)] * ext[LEAD + k : LEAD + k + rows, :] * marks[:, k : k + 1]
        part, at = parted(j, (left_o, right_o, bc_o))
        part[:, at] = out
        if j < PAIRS:
            high, rest = halves(silu(out) * spread(weight, j))
            xw[:, tile(j)] = high
            if precise:
                low[0][:, tile(j)] = rest
        elif j == PAIRS:
            b_cols, b_rest = halves(silu(out).T)
    total = dot(b_cols, xw[...])
    if precise:
        total = total + (dot(b_rest, xw[...]) + dot(b_cols, low[0][...]))
    keep = spread_row(jnp.exp(last) * marks[rows - 1 : rows, 3:4])
    emit_halves(total, keep, bit_of(me, 1), own_o, msg_o)


def mask_bias(mk, sr, rows):
    same = mk[:, 5:6] == sr[0:1, :]
    return jnp.where(jnp.logical_and(triangle(rows, True), same), 0.0, FAR)


def within_kernel(conv, bc, dt, log, hp, mk, sr, y_o, xdt, lcol, lrow, *lower, precise, first):
    rows = mk.shape[0]
    pairs = PAIRS // 2
    scores = fine(dot_t, silu(bc[:, tile(1)]), silu(bc[:, tile(0)]))
    bias = mask_bias(mk, sr, rows)
    dtv, logv = dt[...], log[...]
    lrow[...] = logv.T
    for j in range(pairs):
        x = silu(conv[:, tile(j)])
        high, rest = halves(x * spread(dtv, first + j))
        xdt[:, tile(j)] = high
        if precise:
            lower[0][:, tile(j)] = rest
        y_o[:, tile(j)] = x * spread(hp[2:3, :], first + j)
    for h in range(2 * pairs):
        lcol[h] = jnp.broadcast_to(logv[:, 2 * first + h : 2 * first + h + 1], (rows, LANES))
    low = lanes_of(rows) < HEAD_DIM

    def pair(j, _):
        at = pl.ds(pl.multiple_of(j * LANES, LANES), LANES)
        xp = xdt[:, at]
        res = []
        for q in range(2):
            col = lcol[2 * j + q]
            row = lrow[pl.ds(2 * (first + j) + q, 1), :]
            span = jnp.concatenate([col] * (rows // LANES), axis=1) - row
            mix = scores * jnp.exp(span + bias)
            if precise:
                high, rest = halves(mix)
                res.append(dot(high, xp) + (dot(rest, xp) + dot(high, lower[0][:, at])))
            else:
                res.append(dot(mix.astype(BF16), xp))
        y_o[:, at] += jnp.where(low, res[0], res[1])
        return 0

    lax.fori_loop(0, pairs, pair, 0)


def post_kernel(*refs, places, relative, spans, aligned):
    if spans:
        pack, *refs = refs
        *refs, gated, zbuf, obuf, sems = refs
        parts = len(spans) - 1
        refs, raw = [*refs[:-parts], gated], refs[-parts:]
    else:
        z_low, z_high, out_w, *refs = refs
    normed, h, yw, yw2, mine, recv, bc, log, mk, gg, me, z, y_o, gn_o, st_o, st2_o, h_o, *rel_o, gated = refs
    rows = mk.shape[0]
    wide = 2 * LANES
    half = INNER // 2
    own = normed[HALO:, :]
    flying = []

    def moved(source, target):
        copy = pltpu.make_async_copy(source, target, sems.at[len(flying)])
        flying.append(copy)
        copy.start()
        return copy

    def apart(buffer, base, k):
        return moved(buffer.at[:, spans[k] - base : spans[k + 1] - base, :], raw[k])

    if spans:
        coming = [moved(pack.at[:, spans[0] : spans[2], :], zbuf), moved(pack.at[:, spans[2] : spans[3], :], obuf)]
        coming[0].wait()
        leaving = [apart(zbuf, 0, 0), apart(zbuf, 0, 1)]

    def project(i, _):
        for q in range(2):
            at = pl.ds(pl.multiple_of(i * wide, wide), wide)
            if spans:
                part = zbuf[:, spans[q] : spans[q + 1], at]
                part = part.reshape(-1, part.shape[-1])
            else:
                part = (z_low, z_high)[q][:, at]
            z[:, pl.ds(pl.multiple_of(q * half + i * wide, wide), wide)] = dot(own, part).astype(BF16)
        return 0

    lax.fori_loop(0, half // wide, project, 0)
    if spans:
        for copy in leaving:
            copy.wait()
        more = len(spans) > 4
        if more:
            second = moved(pack.at[:, spans[3] : spans[5], :], zbuf)
        coming[1].wait()
        leaving = [apart(obuf, spans[2], 2)]
    low, high = join_halves(mine, recv, bit_of(me, 1))
    st_o[...] = low.astype(BF16)
    st2_o[...] = high.astype(BF16)
    c = silu(bc[:, tile(1)])
    inflow = jnp.exp(log[...]) * mk[:, 3:4]
    total = jnp.zeros((rows, LANES), F32)
    for j in range(PAIRS):
        part = (yw if j < PAIRS // 2 else yw2)[:, tile(j % (PAIRS // 2))]
        state = (low if j < PAIRS // 2 else high)[:, tile(j % (PAIRS // 2))]
        y = part + fine(dot, c, state) * spread(inflow, j)
        y_o[:, tile(j)] = y
        v = y * silu(z[:, tile(j)].astype(F32))
        gated[:, tile(j)] = v
        total = total + v * v
    inv = lax.rsqrt(jnp.sum(total, axis=-1, keepdims=True) / INNER + EPS)
    for j in range(PAIRS):
        gn_o[:, tile(j)] = (gated[:, tile(j)] * inv * gg[0:1, tile(j)]).astype(BF16)

    if spans and more:
        second.wait()
        leaving += [apart(zbuf, spans[3], 3), apart(zbuf, spans[3], 4)]

    def output(i, _):
        at = pl.ds(pl.multiple_of(i * wide, wide), wide)
        if spans:
            part = obuf[:, :, at]
            part = part.reshape(-1, part.shape[-1])
        else:
            part = out_w[:, at]
        h_o[:, at] = h[:, at].astype(F32) + dot(gn_o[...], part)
        return 0

    lax.fori_loop(0, h.shape[1] // wide, output, 0)
    if spans and more:
        leaving[0].wait()
        last = obuf.at[:, : spans[6] - spans[5], :]
        moved(pack.at[:, spans[5] : spans[6], :], last).wait()
        leaving = leaving[1:] + [moved(last, raw[5])]
    if rel_o:
        lower = lanes_of(rows) < HEAD_DIM
        for j in range(PAIRS):
            base = me[0] if relative else jnp.int32(0)
            sources = [jnp.bitwise_xor(base, jnp.int32(int(places[2 * j + q]))) for q in range(2)]
            upper = jnp.bitwise_and(sources[0], 1) == 1
            tiles = []
            for src in sources:
                at = pl.multiple_of(lax.shift_right_logical(src, 1) * LANES, LANES)
                tiles.append(gn_o[:, pl.ds(at, LANES)].astype(F32))
            left = jnp.where(upper, pltpu.roll(tiles[0], HEAD_DIM, 1), tiles[0])
            right = jnp.where(upper, tiles[1], pltpu.roll(tiles[1], HEAD_DIM, 1))
            rel_o[0][:, tile(j)] = jnp.where(lower, left, right).astype(BF16)
    if spans:
        for copy in leaving:
            copy.wait()


def post_back_kernel(ggn, y, z, gg, left, right, bc, log, mk, me, gy_o, gy2_o, gz_o, gate_o, skip_o, own_o, msg_o, ge):
    rows = mk.shape[0]
    logv = log[...]
    inflow = jnp.exp(logv) * mk[:, 3:4]
    total = jnp.zeros((rows, LANES), F32)
    cross = jnp.zeros((rows, LANES), F32)
    for j in range(PAIRS):
        v = y[:, tile(j)] * silu(z[:, tile(j)].astype(F32))
        total = total + v * v
        cross = cross + v * ggn[:, tile(j)] * gg[0:1, tile(j)]
    inv = lax.rsqrt(jnp.sum(total, axis=-1, keepdims=True) / INNER + EPS)
    mean = jnp.sum(cross, axis=-1, keepdims=True) * inv / INNER
    skips = jnp.zeros((8, LANES), F32)
    for j in range(PAIRS):
        zf = z[:, tile(j)].astype(F32)
        s = sigmoid(zf)
        sz = zf * s
        yv = y[:, tile(j)]
        n = yv * sz * inv
        up = ggn[:, tile(j)]
        gga = inv * (up * gg[0:1, tile(j)] - n * mean)
        gy = gga * sz
        gz_o[:, tile(j)] = (gga * yv * (s * (1.0 + zf * (1.0 - s)))).astype(BF16)
        part, at = parted(j, (gy_o, gy2_o))
        part[:, at] = gy.astype(BF16)
        ge[:, tile(j)] = (gy * spread(inflow, j)).astype(BF16)
        gate_o[:, tile(j)] = jnp.broadcast_to(jnp.sum(up * n, axis=0, keepdims=True), (8, LANES))
        part, at = parted(j, (left, right))
        through = jnp.sum(gy * silu(part[:, at]), axis=0, keepdims=True)
        skips = skips + head_sums(jnp.broadcast_to(through, (8, LANES)), j)
    skip_o[...] = skips
    c_cols = silu(bc[:, tile(1)]).T.astype(BF16)
    state = dot(c_cols, ge[...])
    keep = spread_row(jnp.exp(logv[rows - 1 : rows, :]) * mk[rows - 1 : rows, 3:4])
    emit_halves(state, keep, bit_of(me, 1), own_o, msg_o)


def within_back_kernel(
    conv, bc, dt, log, gy, st, mk, sr, gxdt_o, gb_o, gc_o, gl_o, xdt, ge, lcol, lrow, gscore, lsum, csum, *, first
):
    rows = mk.shape[0]
    pairs = PAIRS // 2
    bf, cf = silu(bc[:, tile(0)]), silu(bc[:, tile(1)])
    b, c = bf.astype(BF16), cf.astype(BF16)
    scores = fine(dot_t, bf, cf)
    same = mk[:, 5:6] == sr[0:1, :]
    bias = jnp.where(jnp.logical_and(triangle(rows, False), same), 0.0, FAR)
    dtv, logv = dt[...], log[...]
    lrow[...] = logv.T
    inflow = jnp.exp(logv) * mk[:, 3:4]
    flow = jnp.zeros((rows, LANES), F32)
    for j in range(pairs):
        xdt[:, tile(j)] = (silu(conv[:, tile(j)]) * spread(dtv, first + j)).astype(BF16)
        gyv = gy[:, tile(j)].astype(F32) * spread(inflow, first + j)
        ge[:, tile(j)] = gyv.astype(BF16)
        flow = flow + head_sums(gyv * dot(c, st[:, tile(j)]), first + j)
    for h in range(2 * pairs):
        lcol[h] = jnp.broadcast_to(logv[:, 2 * first + h : 2 * first + h + 1], (rows, LANES))
    lanes = lanes_of(rows)
    low = lanes < HEAD_DIM
    gscore[...] = jnp.zeros_like(gscore)
    csum[...] = jnp.zeros_like(csum)
    lsum[...] = jnp.zeros_like(lsum)

    def pair(j, _):
        at = pl.ds(pl.multiple_of(j * LANES, LANES), LANES)
        xp, gp = xdt[:, at], gy[:, at]
        res = []
        for q in range(2):
            h = 2 * (first + j) + q
            span = lrow[pl.ds(h, 1), :] - jnp.concatenate([lcol[2 * j + q]] * (rows // LANES), axis=1)
            decay = jnp.exp(span + bias)
            mix = scores * decay
            own = jnp.where(low if q == 0 else jnp.logical_not(low), gp, jnp.zeros_like(gp))
            gmix = dot_t(xp, own)
            gscore[...] += gmix * decay
            term = gmix * mix
            lsum[pl.ds(h, 1), :] = jnp.sum(term, axis=0, keepdims=True)
            csum[...] += jnp.where(lanes == h, jnp.sum(term, axis=1, keepdims=True), 0.0)
            res.append(dot(mix.astype(BF16), gp))
        gxdt_o[:, at] = jnp.where(low, res[0], res[1])
        return 0

    lax.fori_loop(0, pairs, pair, 0)
    gs = gscore[...]
    gb_o[...] = dot(gs.astype(BF16), c)
    gc_o[...] = dot(gs.T.astype(BF16), b) + dot_t(ge[...], st[...])
    gl_o[...] = lsum[...].T - csum[...] + flow


def mixer_back_kernel(
    gxdt2, gy2, right, pc, cw, gxdt, gbi, gci, gli, gbi2, gci2, gli2, mine, recv, gy, left, bc, dt, log, st, st2,
    hp, mk, gate, skip, me, gp_o, wide_o, gb16, xe, acc,
):
    rows = mk.shape[0]
    marks = mk[...]
    low, high = join_halves(mine, recv, bit_of(me, 1))
    half = INNER // 2
    kg = jnp.zeros((8, LANES), F32)
    for part, value in ((0, low), (half, high)):
        gb16[:, part : part + half] = value.astype(BF16)
        rowsum = jnp.sum(value * (st if part == 0 else st2)[...].astype(F32), axis=0, keepdims=True)
        for j in range(PAIRS // 2):
            pair = part // LANES + j
            kg = kg + head_sums(jnp.broadcast_to(rowsum[:, tile(j)], (8, LANES)), pair)
    dtv, logv = dt[...], log[...]
    last = logv[rows - 1 : rows, :]
    b = silu(bc[:, tile(0)]).astype(BF16)
    outflow = marks[:, 4:5] * jnp.exp(last - logv)
    gv = jnp.zeros((rows, LANES), F32)
    gd = jnp.zeros((rows, LANES), F32)

    def conv_back(j, gact, s, out):
        gco = gact * (s * (1.0 + out * (1.0 - s)))
        ext = pc[:, tile(j)].astype(F32)
        acc[...] = jnp.zeros_like(acc)
        for k in range(CONV_K):
            gk = gco if k == CONV_K - 1 else gco * marks[:, k : k + 1]
            wide_o[k : k + 1, tile(j)] = jnp.sum(gk * ext[LEAD + k : LEAD + k + rows, :], axis=0, keepdims=True)
            acc[LEAD + k : LEAD + k + rows, :] += gk * cw[k : k + 1, tile(j)]
        wide_o[4:5, tile(j)] = jnp.sum(gco, axis=0, keepdims=True)
        gp_o[:, tile(j)] = acc[...].astype(BF16)

    wide_o[6:8, :] = jnp.zeros((2, CONV_CH), F32)
    for j in range(PAIRS):
        part, at = parted(j, (left, right))
        out = part[:, at]
        s = sigmoid(out)
        x = out * s
        dtp = spread(dtv, j)
        flow = spread(outflow, j)
        xd = x * dtp
        gxs = dot(b, gb16[:, tile(j)]) * flow
        xe[:, tile(j)] = (xd * flow).astype(BF16)
        gxd = (gxdt if j < PAIRS // 2 else gxdt2)[:, at] + gxs
        gv = gv + head_sums(xd * gxs, j)
        gd = gd + head_sums(x * gxd, j)
        conv_back(j, dtp * gxd + spread(hp[2:3, :], j) * (gy if j < PAIRS // 2 else gy2)[:, at].astype(F32), s, out)
    gb = gbi[...] + gbi2[...] + dot_t(xe[...], gb16[...])
    for j, grad in ((PAIRS, gb), (PAIRS + 1, gci[...] + gci2[...])):
        out = bc[:, tile(j - PAIRS)]
        conv_back(j, grad, sigmoid(out), out)
    keep = jnp.exp(last) * marks[rows - 1 : rows, 3:4]
    edge = jnp.sum(gv, axis=0, keepdims=True) + kg[0:1, :] * keep
    place = lax.broadcasted_iota(jnp.int32, (rows, LANES), 0)
    gl = gli[...] + gli2[...] - gv + jnp.where(place == rows - 1, edge, 0.0)
    ga = dot(triangle(rows, False).astype(F32), gl, EXACT)
    rate = hp[1:2, :]
    raw = pc[HALO:, CONV_CH:WIDE].astype(F32) + hp[0:1, :]
    graw = jnp.where(lanes_of(rows) < HEADS, (ga * rate + gd) * sigmoid(raw), 0.0)
    gp_o[0:HALO, CONV_CH:WIDE] = jnp.zeros((HALO, LANES), BF16)
    gp_o[HALO:, CONV_CH:WIDE] = graw.astype(BF16)
    wide_o[5:6, 0:INNER] = gate[0:1, :]
    place = lanes_of(1)
    heads = jnp.where(place < HEADS, jnp.sum(graw, axis=0, keepdims=True), 0.0)
    for k, row in enumerate((rate * jnp.sum(ga * dtv, axis=0, keepdims=True), skip[0:1, :])):
        heads = heads + jnp.where(place // HEADS == k + 1, pltpu.roll(row, HEADS * (k + 1), 1), 0.0)
    wide_o[5:6, INNER : INNER + LANES] = heads
    wide_o[5:6, INNER + LANES :] = jnp.zeros((1, CONV_CH - INNER - LANES), F32)


def row_of(values, rows=8):
    pad = [(0, rows - values.shape[0]), (0, max(0, LANES - values.shape[1]))]
    return jnp.pad(values.astype(F32), pad)


def per_device(
    hidden, segment_ids, in_weight, out_weight, conv_weight, conv_bias, norm_gain, gate_gain,
    dt_bias, a_log, skip_param, cotangent,
):
    layers_n, in_rows = in_weight.shape[:2]
    out_rows = out_weight.shape[1]
    rows, width = hidden.shape
    count = lax.axis_size("seq")
    me = lax.axis_index("seq")
    me_ref = me.reshape(1).astype(jnp.int32)
    conv_n = conv_bias.shape[1]
    half = INNER // 2
    plane_n = axes_of(count)["z"][1]

    small = jnp.concatenate(
        [conv_weight.reshape(-1), conv_bias.reshape(-1), norm_gain.reshape(-1), gate_gain.reshape(-1)]
    )
    length = small.shape[0]
    small_rows = -(-length // (16 * LANES)) * 16
    small = jnp.pad(small, (0, small_rows * LANES - length)).reshape(small_rows, LANES)
    in_weight_side = jnp.pad(in_weight[0, :, INNER:], ((0, 0), (0, WIDE - SIDE)))
    halo = shifted(hidden[rows - HALO :], 1)
    seg_halo = shifted(segment_ids[rows - HALO :] + 1, 1) - 1
    packs = []
    for layer in range(layers_n):
        parts = [in_weight[layer, :, :half], in_weight[layer, :, half:INNER], out_weight[layer]]
        if layer + 1 < layers_n:
            later = in_weight[layer + 1, :, INNER:]
            parts += [later[:, :half], later[:, half : 2 * half]]
            parts.append(jnp.pad(later[:, 2 * half :], ((0, 0), (0, 3 * half - SIDE))))
        packs.append((jnp.concatenate(parts, axis=0), np.cumsum([0] + [p.shape[0] for p in parts]).tolist()))
    first = Gather(in_weight_side)
    smalls = gather_small(small)
    started = first.line(tuple(pack for pack, _ in packs))
    gathered = [lax.all_gather(after(pack, started), "seq") for pack, _ in packs]
    first.plane()

    seg_pad = jnp.concatenate([seg_halo[LEAD:], segment_ids])
    before = seg_pad[CONV_K - 2]
    columns = [seg_pad[k : k + rows] == segment_ids for k in range(CONV_K - 1)]
    columns += [segment_ids == before, segment_ids == segment_ids[-1], segment_ids]
    marks = jnp.pad(jnp.stack([col.astype(F32) for col in columns], axis=1), ((0, 0), (0, LANES - 6)))
    seg_row = jnp.broadcast_to(segment_ids.astype(F32)[None, :], (8, rows))

    relative, planes = relative_places(count), plane_first(count)
    order = column_order(relative, me, in_rows)
    plane_order = column_order(planes, 0, in_rows)

    place = (jnp.arange(count)[:, None] == (jnp.arange(count) ^ me)[None, :]).astype(BF16)
    smalls = dot(place, smalls.reshape(count, small_rows * LANES))
    sizes = [layers_n * CONV_K * conv_n, layers_n * conv_n, layers_n * in_rows, layers_n * out_rows]
    cuts = np.cumsum([0] + sizes)
    taps, biases, gains, gate_gains = (smalls[:, cuts[i] : cuts[i + 1]] for i in range(4))
    taps = taps.reshape(count, layers_n, CONV_K, conv_n).transpose(1, 2, 0, 3).reshape(layers_n, CONV_K, CONV_CH)
    biases = biases.reshape(count, layers_n, 1, conv_n).transpose(1, 2, 0, 3).reshape(layers_n, 1, CONV_CH)
    conv_rows = jnp.pad(jnp.concatenate([taps, biases], axis=1), ((0, 0), (0, 3), (0, 0)))
    gains = gains.reshape(count, layers_n, in_rows).transpose(1, 0, 2).reshape(layers_n, 1, width)
    gate_gains = gate_gains.reshape(count, layers_n, out_rows).transpose(1, 0, 2).reshape(layers_n, 1, INNER)
    gains = [jnp.broadcast_to(gains[layer], (8, width)) for layer in range(layers_n)]
    gate_gains = [jnp.broadcast_to(gate_gains[layer], (8, INNER)) for layer in range(layers_n)]
    conv_rows = [conv_rows[layer] for layer in range(layers_n)]
    heads = [
        row_of(jnp.stack([dt_bias[layer], -jnp.exp(a_log[layer]), skip_param[layer]])) for layer in range(layers_n)
    ]

    (left, left2), (right, right2) = first.whole((*conv_rows, *gains, *gate_gains, *heads, marks, seg_row, halo, order))

    scratch_wide = pltpu.VMEM((rows, INNER), BF16)
    scratch_half = pltpu.VMEM((rows, INNER // 2), BF16)
    scratch_cols = pltpu.VMEM((HEADS // 2, rows, LANES), F32)
    scratch_rows = pltpu.VMEM((LANES, rows), F32)

    residual = hidden
    saved, sides = [], ()
    for layer in range(layers_n):
        precise = layer + 1 < layers_n
        gain, gate = gains[layer], gate_gains[layer]
        (normed,) = kernel_call(norm_kernel, [((HALO + rows, width), BF16)], (residual, halo, gain))
        if layer == 0:
            normed_rel = dot(normed, order).astype(BF16)
            lower, upper = normed_rel[:, : width // 2], normed_rel[:, width // 2 :]
            parts = [dot(lower, left) + dot(upper, left2), dot(lower, right) + dot(upper, right2)]
        else:
            normed_rel = dot(normed, plane_order).astype(BF16)
            parts = [dot(normed, part) for part in side_parts[:2]]
            parts.append(dot(normed, side_parts[2][:, : WIDE - 2 * half]))
        pc = jnp.concatenate([part.astype(BF16) for part in parts], axis=1)
        hp = heads[layer]
        conv_l, conv_r, bc, dt, log, own, msg = kernel_call(
            partial(conv_state_kernel, precise=precise),
            [((rows, half), F32)] * 2 + [((rows, 2 * STATE), F32)] + [((rows, LANES), F32)] * 2
            + [state_out(half)] * 2,
            (pc, conv_rows[layer], hp, marks, me_ref),
            scratch=[scratch_wide] * (2 if precise else 1), flops=2 * rows * STATE * INNER * 8,
        )
        yw = [
            kernel_call(
                partial(within_kernel, precise=precise, first=part * PAIRS // 2), [((rows, half), F32)],
                ((conv_l, conv_r)[part], bc, dt, log, hp, marks, seg_row),
                scratch=[scratch_half, scratch_cols, scratch_rows] + [scratch_half] * precise,
                flops=2 * rows * rows * half * 16, deps=(own,),
            )[0]
            for part in range(2)
        ]
        mine, recv = exchange(own, msg, me_ref, False, [(), (yw[0],), (yw[1],), ()])
        aligned = out_rows == HEAD_DIM
        places = relative if layer == 0 else planes
        pack, spans = gathered[layer], packs[layer][1]
        weights = [pack[:, a:b].reshape(-1, width) for a, b in zip(spans, spans[1:])]
        outs = [((rows, INNER), BF16), ((rows, INNER), F32), ((rows, INNER), BF16)] + [((STATE, half), BF16)] * 2
        outs += [((rows, width), F32)] + [((rows, INNER), BF16)] * aligned
        form = partial(post_kernel, places=places, relative=layer == 0)
        args = (normed, residual, *yw, mine, recv, bc, log, marks, gate, me_ref)
        scratch = [pltpu.VMEM((rows, INNER), F32)]
        flops = 2 * rows * width * INNER * 2
        if in_rows % HALO:
            z, y, gnormed, state, state2, after_h, *gn_rel = kernel_call(
                partial(form, spans=(), aligned=aligned), outs, (*weights[:3], *args), scratch=scratch, flops=flops
            )
        else:
            z, y, gnormed, state, state2, after_h, *rest = streamed_call(
                partial(form, spans=spans, aligned=aligned), outs, args, flops=flops, streamed=pack,
                scratch=scratch + [pltpu.VMEM((count, 2 * in_rows, width), BF16)] * 2,
                raw=[((count, b - a, width), BF16) for a, b in zip(spans, spans[1:])],
            )
            gn_rel = rest[:aligned]
            weights = [part.reshape(-1, width) for part in rest[aligned:]]
        weights, side_parts = weights[:3], weights[3:]
        if not aligned:
            gn_rel = [dot(gnormed, column_order(places, me if layer == 0 else 0, out_rows)).astype(BF16)]
        saved.append((residual, normed_rel, pc, conv_l, conv_r, bc, dt, log, hp, z, y, gn_rel[0], state, state2, weights, sides))
        sides = side_parts
        residual = after_h
        if layer + 1 < layers_n:
            halo = shifted(residual[rows - HALO :], 1)

    grad = cotangent
    for layer in range(layers_n - 1, -1, -1):
        h, normed_rel, pc, conv_l, conv_r, bc, dt, log, hp, z, y, gn_rel, state, state2, weights, sides = saved[layer]
        z_low, z_high, out_w = weights
        gain, gate = gains[layer], gate_gains[layer]
        mixed = grad.astype(BF16)
        gy, gy2, gz, gate_grad, skip_grad, own, msg = kernel_call(
            post_back_kernel,
            [((rows, half), BF16)] * 2 + [((rows, INNER), BF16), ((8, INNER), F32), ((8, LANES), F32)]
            + [state_out(half), state_out(half, BF16)],
            (dot_t(mixed, out_w), y, z, gate, conv_l, conv_r, bc, log, marks, me_ref),
            scratch=[scratch_wide], flops=2 * rows * STATE * INNER * 8,
        )
        halves_back = [
            kernel_call(
                partial(within_back_kernel, first=part * PAIRS // 2),
                [((rows, half), F32), ((rows, LANES), F32), ((rows, LANES), F32), ((rows, LANES), F32)],
                ((conv_l, conv_r)[part], bc, dt, log, (gy, gy2)[part], (state, state2)[part], marks, seg_row),
                scratch=[
                    scratch_half, scratch_half, scratch_cols, scratch_rows,
                    pltpu.VMEM((rows, rows), F32), scratch_rows, pltpu.VMEM((rows, LANES), F32),
                ],
                flops=2 * rows * rows * half * 32,
            )
            for part in range(2)
        ]
        terms = grads_call(gn_rel, normed_rel, mixed, gz, count, 1 if layer else 2)
        deps = [(), (terms[0],), (halves_back[0][0],), (halves_back[1][0],)]
        late = ()
        if layer:
            planes_sum = scatter_planes(terms[0].reshape(-1, width))
        else:
            pack_share = Shares(*(term.reshape(-1, width) for term in terms))
            late = tuple(far(piece) for piece in pack_share.step())
        if layer + 1 < layers_n:
            deps[3] += (far(above[0]),)
        mine, recv = exchange(own, msg, me_ref, True, deps)

        (gx, *sums), (gx2, *sums2) = halves_back
        gp, wide = kernel_call(
            mixer_back_kernel,
            [((HALO + rows, WIDE), BF16), ((8, CONV_CH), F32)],
            (
                gx2, gy2, conv_r, pc, conv_rows[layer], gx, *sums, *sums2, mine, recv, gy, conv_l, bc, dt, log,
                state, state2, hp, marks, gate_grad, skip_grad, me_ref,
            ),
            scratch=[pltpu.VMEM((STATE, INNER), BF16), scratch_wide, pltpu.VMEM((HALO + rows, LANES), F32)],
            flops=2 * rows * STATE * INNER * 24, deps=late,
        )
        if layer + 1 < layers_n:
            above = (above[0], after(above[1], gp))
        spilled = shifted(gp[:HALO], -1)
        if layer:
            above = (planes_sum, scatter_planes(turned_dot(normed_rel, gp)))
        else:
            side_share = share_terms(normed_rel, gp)
            both = (side_share.terms[0], side_share.send, far(pack_share.terms[1]))
        gp_own, gz = kernel_call(
            own_rows_kernel, [((rows, WIDE), BF16), ((rows, INNER), BF16)], (gp, spilled, gz),
            deps=() if layer else both,
        )
        gn_z = dot_t(gz[:, :half], z_low) + dot_t(gz[:, half:], z_high)
        if layer:
            gn = gn_z
            for k, part in enumerate(sides):
                piece = gp_own[:, k * half : min((k + 1) * half, WIDE)]
                gn = gn + dot_t(piece, part[:, : piece.shape[1]])
        else:
            gp_left, gp_right = gp_own[:, :CUT], gp_own[:, CUT:]
            gn_side = jnp.concatenate(
                [dot_t(gp_left, left) + dot_t(gp_right, right), dot_t(gp_left, left2) + dot_t(gp_right, right2)],
                axis=1,
            )
            gn_high, gn_low = halves(gn_side)
            gn = gn_z + dot_t(gn_high, order) + dot_t(gn_low, order)
        grad, small_grads = kernel_call(
            norm_back_kernel, [((rows, width), F32), ((8 * (layers_n - layer), CONV_CH), F32)],
            (gn, h, grad, gain, wide) + ((small_grads,) if layer + 1 < layers_n else ()),
            deps=() if layer else (far(pack_share.terms[2]),),
        )
    (sums,) = kernel_call(round_kernel, [(small_grads.shape, BF16)], (small_grads,))
    sums = sum_rounds(sums, count // 2, plane_n)
    pieces = pack_share.step((sums,))
    side_share.step(behind=pieces[0])
    side_share.step()
    passed = (*pack_share.terms[1:], side_share.terms[1])
    sums = sum_rounds(sums, plane_n // 2, 1, tuple(far(part) for part in passed))
    terms, split = [*pack_share.terms, *side_share.terms], [(len(pack_share.terms), len(side_share.terms))]
    for part in above:
        terms.append(scatter_lines(part))
    split += [(1, 1)] * (layers_n - 1)
    in_grads, out_grads = kernel_call(
        partial(shares_kernel, split=split),
        [((layers_n, in_rows, INNER + SIDE), F32), ((layers_n, out_rows, width), F32)], terms, deps=(sums,),
    )
    sums = sums.reshape(layers_n, 8, CONV_CH)

    def share(values):
        span = values.shape[-1] // count
        return lax.dynamic_slice_in_dim(values, me * span, span, values.ndim - 1)

    heads = sums[:, 5, INNER : INNER + 3 * HEADS]
    return (
        residual, grad, in_grads, out_grads,
        share(sums[:, :CONV_K]), share(sums[:, CONV_K]), share(sums[:, 6, :width]), share(sums[:, 5, :INNER]),
        heads[:, :HEADS], heads[:, HEADS : 2 * HEADS], heads[:, 2 * HEADS :],
    )


def solution(mesh):
    return jax.shard_map(
        per_device,
        mesh=mesh,
        in_specs=(
            P("seq", None), P("seq"), P(None, "seq", None), P(None, "seq", None), P(None, None, "seq"),
            P(None, "seq"), P(None, "seq"), P(None, "seq"), P(), P(), P(), P("seq", None),
        ),
        out_specs=(
            P("seq", None), P("seq", None), P(None, "seq", None), P(None, "seq", None), P(None, None, "seq"),
            P(None, "seq"), P(None, "seq"), P(None, "seq"), P(), P(), P(),
        ),
        check_vma=False,
    )
```

time: 753 us -> 590 us (0.78)
  waiting for transfers between devices: 258 us -> 148 us
  matrix products: 77.5 us -> 29.9 us
  other arithmetic: 48.6 us -> 16.2 us
  Pallas kernels: 93.4 us -> 124 us
    ppermute x103 -> x77, waiting for transfers between devices: 257 us -> 145 us  [swap(): return lax.ppermute(value, 'seq', [(i, i ^ flip) for i in range(count)])]
    slice x31 -> x11, local copies, waits for them, and re-layouts: 38.7 us -> 3.61 us  [the longest x1 1.52 us: per_device(): gains[layer]]
    unnamed x402 -> x450, local copies, waits for them, and re-layouts: 47.4 us -> 82 us
    pallas_call x44 -> x54, Pallas kernels: 93.4 us -> 124 us  [the longest x47 86.1 us: kernel_call(): pl.pallas_call(run, out_shape=tuple((jax.ShapeDtypeStruct(*o) for o in ou...]
    dot_general x8 -> x3, matrix products: 30.2 us -> 9.1 us  [turned_dot(): lax.dot_general(left, right, (((0,), (0,)), ((), ())), preferred_element_...]
    convert_element_type x24 -> x5, other arithmetic: 27.6 us -> 11.2 us  [the longest x2 9.41 us: step(): pieces.append((sum(picked[1:], picked[0]) + none).astype(BF16))]
    dot_general x17 -> x10, matrix products: 22.3 us -> 7.9 us  [dot(): return jnp.dot(left, right, precision=precision, preferred_element_type=F32)]
    dot_general x18 -> x15, matrix products: 25.1 us -> 12.9 us  [dot_t(): lax.dot_general(left, right, (((1,), (1,)), ((), ())), preferred_element_...]
  transfers between devices with their start and end apart: 110 -> 88, of which waited for: 54 -> 50; matrix products, arithmetic and copies ran while one was open for 25% -> 14% of each run, Pallas kernels for 11% -> 17%
where the time goes in v2:
time: 590 us; the launch traced here: 583 us
  waiting for transfers between devices  148 us (25%)
  starting transfers between devices  135 us (23%)
  Pallas kernels  124 us (21%)
  local copies, waits for them, and re-layouts  114 us (19%)
  matrix products  29.9 us (5%)
  between operations  17.8 us (3%)
  other arithmetic  16.2 us (3%)
    ppermute x77, waiting for transfers between devices, swap(): return lax.ppermute(value, 'seq', [(i, i ^ flip) for i in range(count)])  145 us
    ppermute x77, starting transfers between devices, swap(): return lax.ppermute(value, 'seq', [(i, i ^ flip) for i in range(count)])  123 us
    pallas_call x47, Pallas kernels, kernel_call(): pl.pallas_call(run, out_shape=tuple((jax.ShapeDtypeStruct(*o) for o in ou...  86.1 us
    unnamed x450, local copies, waits for them, and re-layouts  82 us
    pallas_call x2, Pallas kernels, streamed_call(): pl.pallas_call(body, out_shape=tuple((jax.ShapeDtypeStruct(*o) for o in (...  23.7 us
    dot_general x15, matrix products, dot_t(): lax.dot_general(left, right, (((1,), (1,)), ((), ())), preferred_element_...  12.9 us
  transfers between devices with their start and end apart: 88, of which 50 were waited for; matrix products, arithmetic and copies ran while one was open for 14% of the time, Pallas kernels for 17%

profile of v2, /device:TPU:0, one launch (start us, length us, event | category | flops | bytes accessed | tf_op | source)
XLA Modules:
  0.0 583.4 jit_solution(6910594412366116411)
XLA Ops:
  8.3 3.1 collective-permute-start
  11.4 2.6 collective-permute-start.1
  18.6 7.3 %collective-permute-done.1.refs_2_.refs_6_ = bf16[32,2432]{1,0:T(8,128)(2,1)S(1)} collective-permute-done((bf16[32,2432]{1,0:T(8,128)(2,1)S(1)}, bf16[32,2432]{1,0:T(8,128)(2,1)S(1)}, u32[]{:S(2)}, u32[]{:S(2)}) %collective-permute-start.1) | collective-permute-done | bytes 155680 | tf_op jit(solution)/shard_map/ppermute | solution.py:42
  31.6 3.0 collective-permute-start.3
  45.1 2.6 collective-permute-start.7
  48.3 2.7 collective-permute-done.7
  73.7 4.8 collective-permute-done.10.refs_3_
  88.4 14.8 %collective-permute-done.12.refs_4_.refs_5_ = bf16[2,4,32,1152]{3,2,1,0:T(8,128)(2,1)S(1)} collective-permute-done((bf16[2,4,32,1152]{3,2,1,0:T(8,128)(2,1)}, bf16[2,4,32,1152]{3,2,1,0:T(8,128)(2,1)S(1)}, u32[]{:S(2)}, u32[]{:S(2)}) %collective-permute-start.12) | collective-permute-done | bytes 589856 | tf_op jit(solution)/shard_map/ppermute | solution.py:42
  115.4 3.7 shard_map.245
  125.3 4.6 shard_map.246.refs_5_.refs_3_
  132.1 2.4 collective-permute-start.20
  137.0 4.9 shard_map.247.refs_6_.refs_4_
  141.9 2.7 collective-permute-done.20.refs_1_
  144.6 5.0 collective-permute-done.22.refs_3_
  154.2 2.9 collective-permute-done.23.refs_1_
  168.7 13.3 %shard_map.252 = (bf16[256,2048]{1,0:T(8,128)(2,1)S(1)}, f32[256,2048]{1,0:T(8,128)S(1)}, bf16[256,2048]{1,0:T(8,128)(2,1)}, bf16[128,1024]{1,0:T(8,128)(2,1)S(1...) custom-call(bf16[32,224,1024]{2,1,0:T(8,128)(2,1)} %bitcast.188, ...), custom_call_target="tpu_custom_call" | custom-call | flops 2147483648 | bytes 40992772 | tf_op jit(solution)/shard_map/pallas_call | solution.py:246
  194.5 3.1 shard_map.254
  201.3 2.7 collective-permute-start.29
  206.0 3.8 shard_map.255.refs_5_.refs_3_
  211.4 3.0 collective-permute-done.30.refs_2_
  214.4 4.7 collective-permute-done.31.refs_3_
  219.3 2.5 collective-permute-start.32
  221.8 2.4 collective-permute-start.34
  224.3 3.4 shard_map.256.refs_6_.refs_4_
  227.7 4.0 collective-permute-done.32.refs_1_
  231.7 7.8 %collective-permute-done.33.refs_2_ = f32[136,256]{1,0:T(8,128)S(1)} collective-permute-done((f32[136,256]{1,0:T(8,128)S(1)}, f32[136,256]{1,0:T(8,128)S(1)}, u32[]{:S(2)}, u32[]{:S(2)}) %collective-permute-start.33) | collective-permute-done | bytes 139296 | tf_op jit(solution)/shard_map/ppermute | solution.py:42
  244.3 2.4 collective-permute-done.35.refs_1_
  254.7 3.4 copy-done.5
  264.1 10.4 %shard_map.261 = (bf16[256,2048]{1,0:T(8,128)(2,1)S(1)}, f32[256,2048]{1,0:T(8,128)S(1)}, bf16[256,2048]{1,0:T(8,128)(2,1)}, bf16[128,1024]{1,0:T(8,128)(2,1)S(1...) custom-call(bf16[32,128,1024]{2,1,0:T(8,128)(2,1)S(1)} %bitcast.164,, ...), custom_call_target="tpu_custom_call" | custom-call | flops 2147483648 | bytes 28934148 | tf_op jit(solution)/shard_map/pallas_call | solution.py:246
  277.8 5.6 shard_map.262
  283.5 4.1 shard_map.266.refs_5_
  287.7 3.3 copy-done
  299.6 2.4 collective-permute-done.42.refs_3_
  302.0 4.9 copy-done.1
  307.2 2.5 collective-permute-start.43
  309.7 2.4 collective-permute-start.45
  312.2 5.5 shard_map.264
  321.5 5.3 shard_map.263
  328.8 8.5 %shard_map.270 = (bf16[272,2432]{1,0:T(8,128)(2,1)S(1)}, f32[8,2304]{1,0:T(8,128)S(1)}) custom-call(f32[256,1024]{1,0:T(8,128)S(1)} %get-tuple-element.212.refs_6_.refs_0_, bf16[256,1024]{1,0:T(8,128)(2,1)S(1)} %copy-done.186, f32[256,1024]{1,0:T(8,128)S(1)} %copy-done.84, bf16[272,2432]{1,0:T(8,128)(2,1)S(1)} %copy-done.67, f32[8,2304]{1,0:T(8,128)S(1)} %copy-done.134, ...), custom_call_target="tpu_custom_call" | custom-call | flops 3221225472 | bytes 10862596 | tf_op jit(solution)/shard_map/pallas_call | solution.py:229
  353.2 5.7 shard_map.273
  361.0 5.9 %shard_map.277 = (bf16[16,128,1024]{2,1,0:T(8,128)(2,1)S(1)}, bf16[16,128,1024]{2,1,0:T(8,128)(2,1)}) custom-call(bf16[256,2048]{1,0:T(8,128)(2,1)S(1)} %copy-done.182, bf16[272,1024]{1,0:T(8,128)(2,1)S(1)} %copy-done.45, bf16[256,1024]{1,0:T(8,128)(2,1)S(1)} %convert_element_type.262.mixed, bf16[256,2048]{1,0:T(8,128)(2,1)S(1)} %get-tuple-element.271.gz.refs_2_), custom_call_target="tpu_custom_call" | custom-call | flops 2147483648 | bytes 10485760 | tf_op jit(solution)/shard_map/pallas_call | solution.py:591
  368.9 3.9 collective-permute-start.62
  372.8 4.6 convolution_convert_fusion
  377.5 2.7 collective-permute-done.51.refs_1_
  397.8 5.3 shard_map.275
  407.8 5.3 shard_map.274
  424.2 6.0 %fusion.7 = (bf16[4,128,1024]{2,1,0:T(8,128)(2,1)}, bf16[4,128,1024]{2,1,0:T(8,128)(2,1)S(1)}, bf16[4,128,1024]{2,1,0:T(8,128)(2,1)S(1)}, bf16[4,128,1024]{2,1,0:T(8,128)(2,1)}) fusion(bf16[4,4,128,1024]{3,2,1,0:T(8,128)(2,1)} %collective-permute-done.62, bf16[16,128,1024]{2,1,0:T(8,128)(2,1)} %copy-done.2), kind=kLoop, calls=%fused_computation.16 | loop fusion | flops 8388608 | bytes 12582912 | tf_op jit(solution)/shard_map/convert_element_type | solution.py:134
  434.0 8.4 %shard_map.281 = (bf16[272,2432]{1,0:T(8,128)(2,1)S(1)}, f32[8,2304]{1,0:T(8,128)S(1)}) custom-call(f32[256,1024]{1,0:T(8,128)S(1)} %copy-done.21, bf16[256,1024]{1,0:T(8,128)(2,1)S(1)} %copy-done.124, f32[256,1024]{1,0:T(8,128)S(1)} %copy-done.18, bf16[272,2432]{1,0:T(8,128)(2,1)S(1)} %pad_maximum_fusion.refs_0_.refs_3_, f32[8,2304]{1,0:T(8,128)S(1)} %copy-done.98, ...), custom_call_target="tpu_custom_call" | custom-call | flops 3221225472 | bytes 10862596 | tf_op jit(solution)/shard_map/pallas_call | solution.py:229
  443.9 3.0 convolution_convert_fusion.1.refs_4_
  449.6 6.6 %collective-permute-done.64.refs_5_.refs_1_ = bf16[4,128,1024]{2,1,0:T(8,128)(2,1)S(1)} collective-permute-done((bf16[4,128,1024]{2,1,0:T(8,128)(2,1)S(1)}, bf16[4,128,1024]{2,1,0:T(8,128)(2,1)S(1)}, u32[]{:S(2)}, u32[]{:S(2)}) %collective-permute-start.64) | collective-permute-done | bytes 1048608 | tf_op jit(solution)/shard_map/ppermute | solution.py:42
  475.8 3.1 collective-permute-done.68.refs_1_
  482.0 3.4 fusion.29
  485.5 21.5 %collective-permute-start.73 = (bf16[4,32,2432]{2,1,0:T(8,128)(2,1)}, bf16[4,32,2432]{2,1,0:T(8,128)(2,1)S(1)}, u32[]{:S(2)}, u32[]{:S(2)}) collective-permute-start(bf16[4,32,2432]{2,1,0:T(8,128)(2,1)} %get-tuple-element.316), channel_id=1, source_target_pairs={{0,2},{1,3},{2,0},{3,1},{4,6},{5,7},{6,4},{7,5},{8,10},{9,11},{10,... | collective-permute-start | bytes 1867784 | tf_op jit(solution)/shard_map/ppermute | solution.py:42
  508.5 2.4 collective-permute-start.69
  510.9 2.6 collective-permute-start.70
  513.5 8.5 %collective-permute-done.73 = bf16[4,32,2432]{2,1,0:T(8,128)(2,1)S(1)} collective-permute-done((bf16[4,32,2432]{2,1,0:T(8,128)(2,1)}, bf16[4,32,2432]{2,1,0:T(8,128)(2,1)S(1)}, u32[]{:S(2)}, u32[]{:S(2)}) %collective-permute-start.73) | collective-permute-done | bytes 622624 | tf_op jit(solution)/shard_map/ppermute | solution.py:42
  522.1 4.5 collective-permute-start.71
  526.6 10.0 %collective-permute-done.74 = bf16[4,32,2432]{2,1,0:T(8,128)(2,1)} collective-permute-done((bf16[4,32,2432]{2,1,0:T(8,128)(2,1)}, bf16[4,32,2432]{2,1,0:T(8,128)(2,1)}, u32[]{:S(2)}, u32[]{:S(2)}) %collective-permute-start.74) | collective-permute-done | bytes 622624 | tf_op jit(solution)/shard_map/ppermute | solution.py:42
  536.5 2.4 fusion.63
  541.5 4.1 collective-permute-done.79.refs_1_
  545.6 3.7 collective-permute-done.76.refs_5_
  550.5 3.9 collective-permute-done.80.refs_1_
  556.3 2.6 collective-permute-start.78
  562.2 7.0 %collective-permute-done.77.refs_6_ = bf16[32,2432]{1,0:T(8,128)(2,1)S(1)} collective-permute-done((bf16[32,2432]{1,0:T(8,128)(2,1)}, bf16[32,2432]{1,0:T(8,128)(2,1)S(1)}, u32[]{:S(2)}, u32[]{:S(2)}) %collective-permute-start.77) | collective-permute-done | bytes 155680 | tf_op jit(solution)/shard_map/ppermute | solution.py:42
  (735 shorter events, 249.9 us)
Async XLA Ops:
  7.2 155.9 %all-gather.7.cloned.1.call-start = ((), (), s32[]{:S(2)}) async-start(), calls=%async_computation.9 | async-start | bytes 15138816 | tf_op jit(solution)/shard_map/all_gather | solution.py:1019
  8.3 10.3 %collective-permute-start = (bf16[32,2432]{1,0:T(8,128)(2,1)S(1)}, bf16[32,2432]{1,0:T(8,128)(2,1)S(1)}, u32[]{:S(2)}, u32[]{:S(2)}) collective-permute-start(bf16[32,2432]{1,0:T(8,128)(2,1)S(1)} %pad.27.refs_0_.refs_4_), channel_id=1, source_target_pairs={{0,8},{1,9},{2,10},{3,11},{4,12},{5,13},{6,14},{7,15},{8,0},{9,1},... | collective-permute-start | bytes 466952 | tf_op jit(solution)/shard_map/ppermute | solution.py:42
  11.4 14.5 %collective-permute-start.1 = (bf16[32,2432]{1,0:T(8,128)(2,1)S(1)}, bf16[32,2432]{1,0:T(8,128)(2,1)S(1)}, u32[]{:S(2)}, u32[]{:S(2)}) collective-permute-start(bf16[32,2432]{1,0:T(8,128)(2,1)S(1)} %pad.27.refs_0_.refs_4_), channel_id=1, source_target_pairs={{0,16},{1,17},{2,18},{3,19},{4,20},{5,21},{6,22},{7,23},{8,24},{9,... | collective-permute-start | bytes 466952 | tf_op jit(solution)/shard_map/ppermute | solution.py:42
  13.9 11.9 %collective-permute-start.2 = (bf16[32,2432]{1,0:T(8,128)(2,1)S(1)}, bf16[32,2432]{1,0:T(8,128)(2,1)S(1)}, u32[]{:S(2)}, u32[]{:S(2)}) collective-permute-start(bf16[32,2432]{1,0:T(8,128)(2,1)S(1)} %pad.27.refs_0_.refs_4_), channel_id=1, source_target_pairs={{0,24},{1,25},{2,26},{3,27},{4,28},{5,29},{6,30},{7,31},{8,16},{9,... | collective-permute-start | bytes 466952 | tf_op jit(solution)/shard_map/ppermute | solution.py:42
  27.2 227.5 %all-gather.5.cloned.1.call-start = ((), (), s32[]{:S(2)}) async-start(), calls=%async_computation.8 | async-start | bytes 8650752 | tf_op jit(solution)/shard_map/all_gather | solution.py:1019
  28.0 390.0 %reduce-scatter.5.cloned.1.call-start = ((), (), s32[]{:S(2)}) async-start(), calls=%async_computation.4 | async-start | bytes 9437184 | tf_op jit(solution)/shard_map/reduce_scatter | solution.py:167
  28.5 9.2 %collective-permute-start.4 = (bf16[16,128]{1,0:T(8,128)(2,1)S(1)}, bf16[16,128]{1,0:T(8,128)(2,1)S(1)}, u32[]{:S(2)}, u32[]{:S(2)}) collective-permute-start(bf16[16,128]{1,0:T(8,128)(2,1)S(1)} %fusion.73), channel_id=1, source_target_pairs={{0,1},{1,0},{2,3},{3,2},{4,5},{5,4},{6,7},{7,6},{8,9},{9,8},{10,11... | collective-permute-start | bytes 12296 | tf_op jit(solution)/shard_map/ppermute | solution.py:42
  28.6 8.3 %collective-permute-start.13 = (s32[16]{0:T(128)S(1)}, s32[16]{0:T(128)S(1)}, u32[]{:S(2)}, u32[]{:S(2)}) collective-permute-start(s32[16]{0:T(128)S(1)} %slice_add_fusion), channel_id=1, source_target_pairs={{0,1},{1,2},{2,3},{3,4},{4,5},{5,6},{6,7},{7,8},{8,9},{9,10},{10,1... | collective-permute-start | bytes 200 | tf_op jit(solution)/shard_map/ppermute | solution.py:47
  31.6 56.9 %collective-permute-start.3 = (bf16[16,1024]{1,0:T(8,128)(2,1)}, bf16[16,1024]{1,0:T(8,128)(2,1)S(1)}, u32[]{:S(2)}, u32[]{:S(2)}) collective-permute-start(bf16[16,1024]{1,0:T(8,128)(2,1)} %slice.300), channel_id=1, source_target_pairs={{0,1},{1,2},{2,3},{3,4},{4,5},{5,6},{6,7},{7,8},{8,9},{9,10},{10,1... | collective-permute-start | bytes 98312 | tf_op jit(solution)/shard_map/ppermute | solution.py:47
  51.6 6.1 %collective-permute-start.8 = (bf16[256,128]{1,0:T(8,128)(2,1)}, bf16[256,128]{1,0:T(8,128)(2,1)S(1)}, u32[]{:S(2)}, u32[]{:S(2)}) collective-permute-start(bf16[256,128]{1,0:T(8,128)(2,1)} %get-tuple-element.327), channel_id=1, source_target_pairs={{0,16},{1,17},{2,18},{3,19},{4,20},{5,21},{6,22},{7,23},{8,24},{9,... | collective-permute-start | bytes 196616 | tf_op jit(solution)/shard_map/ppermute | solution.py:42
  70.4 8.6 %collective-permute-start.9 = (bf16[4,32,1280]{2,1,0:T(8,128)(2,1)S(1)}, bf16[4,32,1280]{2,1,0:T(8,128)(2,1)S(1)}, u32[]{:S(2)}, u32[]{:S(2)}) collective-permute-start(bf16[4,32,1280]{2,1,0:T(8,128)(2,1)S(1)} %get-tuple-element.156.refs_1_.refs_0_), channel_id=1, source_target_pairs={{0,2},{1,3},{2,0},{3,1},{4,6},{5,7},{6,4},{7,5},{8,10},{9,11},{10,... | collective-permute-start | bytes 983048 | tf_op jit(solution)/shard_map/ppermute | solution.py:42
  71.7 6.7 %collective-permute-start.10 = (bf16[4,32,1152]{2,1,0:T(8,128)(2,1)S(1)}, bf16[4,32,1152]{2,1,0:T(8,128)(2,1)S(1)}, u32[]{:S(2)}, u32[]{:S(2)}) collective-permute-start(bf16[4,32,1152]{2,1,0:T(8,128)(2,1)S(1)} %get-tuple-element.157.refs_2_), channel_id=1, source_target_pairs={{0,4},{1,5},{2,6},{3,7},{4,0},{5,1},{6,2},{7,3},{8,12},{9,13},{10,... | collective-permute-start | bytes 884744 | tf_op jit(solution)/shard_map/ppermute | solution.py:42
  80.6 23.1 %collective-permute-start.11 = (bf16[2,4,32,1280]{3,2,1,0:T(8,128)(2,1)}, bf16[2,4,32,1280]{3,2,1,0:T(8,128)(2,1)}, u32[]{:S(2)}, u32[]{:S(2)}) collective-permute-start(bf16[2,4,32,1280]{3,2,1,0:T(8,128)(2,1)} %get-tuple-element.158.refs_0_), channel_id=1, source_target_pairs={{0,4},{1,5},{2,6},{3,7},{4,0},{5,1},{6,2},{7,3},{8,12},{9,13},{10,... | collective-permute-start | bytes 1966088 | tf_op jit(solution)/shard_map/ppermute | solution.py:42
  82.1 21.1 %collective-permute-start.12 = (bf16[2,4,32,1152]{3,2,1,0:T(8,128)(2,1)}, bf16[2,4,32,1152]{3,2,1,0:T(8,128)(2,1)S(1)}, u32[]{:S(2)}, u32[]{:S(2)}) collective-permute-start(bf16[2,4,32,1152]{3,2,1,0:T(8,128)(2,1)} %get-tuple-element.159.refs_2_.refs_3_), channel_id=1, source_target_pairs={{0,2},{1,3},{2,0},{3,1},{4,6},{5,7},{6,4},{7,5},{8,10},{9,11},{10,... | collective-permute-start | bytes 1769480 | tf_op jit(solution)/shard_map/ppermute | solution.py:42
  121.5 8.5 %collective-permute-start.17 = (f32[136,256]{1,0:T(8,128)S(1)}, f32[136,256]{1,0:T(8,128)S(1)}, u32[]{:S(2)}, u32[]{:S(2)}) collective-permute-start(f32[136,256]{1,0:T(8,128)S(1)} %get-tuple-element.170), channel_id=1, source_target_pairs={{0,2},{1,3},{2,0},{3,1},{4,6},{5,7},{6,4},{7,5},{8,10},{9,11},{10,... | collective-permute-start | bytes 417800 | tf_op jit(solution)/shard_map/ppermute | solution.py:42
  121.7 8.4 %collective-permute-start.18 = (f32[136,256]{1,0:T(8,128)S(1)}, f32[136,256]{1,0:T(8,128)S(1)}, u32[]{:S(2)}, u32[]{:S(2)}) collective-permute-start(f32[136,256]{1,0:T(8,128)S(1)} %get-tuple-element.171), channel_id=1, source_target_pairs={{0,4},{1,5},{2,6},{3,7},{4,0},{5,1},{6,2},{7,3},{8,12},{9,13},{10,... | collective-permute-start | bytes 417800 | tf_op jit(solution)/shard_map/ppermute | solution.py:42
  123.9 8.1 %collective-permute-start.19 = (f32[136,256]{1,0:T(8,128)S(1)}, f32[136,256]{1,0:T(8,128)S(1)}, u32[]{:S(2)}, u32[]{:S(2)}) collective-permute-start(f32[136,256]{1,0:T(8,128)S(1)} %get-tuple-element.172), channel_id=1, source_target_pairs={{0,6},{1,7},{2,4},{3,5},{4,2},{5,3},{6,0},{7,1},{8,14},{9,15},{10,... | collective-permute-start | bytes 417800 | tf_op jit(solution)/shard_map/ppermute | solution.py:42
  132.1 12.5 %collective-permute-start.20 = (f32[136,256]{1,0:T(8,128)S(1)}, f32[136,256]{1,0:T(8,128)S(1)}, u32[]{:S(2)}, u32[]{:S(2)}) collective-permute-start(f32[136,256]{1,0:T(8,128)S(1)} %get-tuple-element.173.refs_0_), channel_id=1, source_target_pairs={{0,8},{1,9},{2,10},{3,11},{4,12},{5,13},{6,14},{7,15},{8,0},{9,1},... | collective-permute-start | bytes 417800 | tf_op jit(solution)/shard_map/ppermute | solution.py:42
  134.5 10.1 %collective-permute-start.21 = (f32[136,256]{1,0:T(8,128)S(1)}, f32[136,256]{1,0:T(8,128)S(1)}, u32[]{:S(2)}, u32[]{:S(2)}) collective-permute-start(f32[136,256]{1,0:T(8,128)S(1)} %get-tuple-element.173.refs_0_), channel_id=1, source_target_pairs={{0,16},{1,17},{2,18},{3,19},{4,20},{5,21},{6,22},{7,23},{8,24},{9,... | collective-permute-start | bytes 417800 | tf_op jit(solution)/shard_map/ppermute | solution.py:42
  136.8 12.8 %collective-permute-start.22 = (f32[136,256]{1,0:T(8,128)S(1)}, f32[136,256]{1,0:T(8,128)S(1)}, u32[]{:S(2)}, u32[]{:S(2)}) collective-permute-start(f32[136,256]{1,0:T(8,128)S(1)} %get-tuple-element.173.refs_0_), channel_id=1, source_target_pairs={{0,24},{1,25},{2,26},{3,27},{4,28},{5,29},{6,30},{7,31},{8,16},{9,... | collective-permute-start | bytes 417800 | tf_op jit(solution)/shard_map/ppermute | solution.py:42
  150.7 6.3 %collective-permute-start.23 = (f32[128,256]{1,0:T(8,128)S(1)}, f32[128,256]{1,0:T(8,128)S(1)}, u32[]{:S(2)}, u32[]{:S(2)}) collective-permute-start(f32[128,256]{1,0:T(8,128)S(1)} %get-tuple-element.176), channel_id=1, source_target_pairs={{0,2},{1,3},{2,0},{3,1},{4,6},{5,7},{6,4},{7,5},{8,10},{9,11},{10,... | collective-permute-start | bytes 393224 | tf_op jit(solution)/shard_map/ppermute | solution.py:42
  151.2 6.1 %collective-permute-start.24 = (f32[128,256]{1,0:T(8,128)S(1)}, f32[128,256]{1,0:T(8,128)S(1)}, u32[]{:S(2)}, u32[]{:S(2)}) collective-permute-start(f32[128,256]{1,0:T(8,128)S(1)} %get-tuple-element.177), channel_id=1, source_target_pairs={{0,4},{1,5},{2,6},{3,7},{4,0},{5,1},{6,2},{7,3},{8,12},{9,13},{10,... | collective-permute-start | bytes 393224 | tf_op jit(solution)/shard_map/ppermute | solution.py:42
  152.7 6.6 %collective-permute-start.25 = (f32[128,256]{1,0:T(8,128)S(1)}, f32[128,256]{1,0:T(8,128)S(1)}, u32[]{:S(2)}, u32[]{:S(2)}) collective-permute-start(f32[128,256]{1,0:T(8,128)S(1)} %get-tuple-element.178), channel_id=1, source_target_pairs={{0,6},{1,7},{2,4},{3,5},{4,2},{5,3},{6,0},{7,1},{8,14},{9,15},{10,... | collective-permute-start | bytes 393224 | tf_op jit(solution)/shard_map/ppermute | solution.py:42
  201.3 10.2 %collective-permute-start.29 = (f32[136,256]{1,0:T(8,128)S(1)}, f32[136,256]{1,0:T(8,128)S(1)}, u32[]{:S(2)}, u32[]{:S(2)}) collective-permute-start(f32[136,256]{1,0:T(8,128)S(1)} %get-tuple-element.194), channel_id=1, source_target_pairs={{0,2},{1,3},{2,0},{3,1},{4,6},{5,7},{6,4},{7,5},{8,10},{9,11},{10,... | collective-permute-start | bytes 417800 | tf_op jit(solution)/shard_map/ppermute | solution.py:42
  204.0 10.4 %collective-permute-start.30 = (f32[136,256]{1,0:T(8,128)S(1)}, f32[136,256]{1,0:T(8,128)S(1)}, u32[]{:S(2)}, u32[]{:S(2)}) collective-permute-start(f32[136,256]{1,0:T(8,128)S(1)} %get-tuple-element.195), channel_id=1, source_target_pairs={{0,4},{1,5},{2,6},{3,7},{4,0},{5,1},{6,2},{7,3},{8,12},{9,13},{10,... | collective-permute-start | bytes 417800 | tf_op jit(solution)/shard_map/ppermute | solution.py:42
  206.0 13.2 %collective-permute-start.31 = (f32[136,256]{1,0:T(8,128)S(1)}, f32[136,256]{1,0:T(8,128)S(1)}, u32[]{:S(2)}, u32[]{:S(2)}) collective-permute-start(f32[136,256]{1,0:T(8,128)S(1)} %get-tuple-element.196), channel_id=1, source_target_pairs={{0,6},{1,7},{2,4},{3,5},{4,2},{5,3},{6,0},{7,1},{8,14},{9,15},{10,... | collective-permute-start | bytes 417800 | tf_op jit(solution)/shard_map/ppermute | solution.py:42
  219.3 12.4 %collective-permute-start.32 = (f32[136,256]{1,0:T(8,128)S(1)}, f32[136,256]{1,0:T(8,128)S(1)}, u32[]{:S(2)}, u32[]{:S(2)}) collective-permute-start(f32[136,256]{1,0:T(8,128)S(1)} %get-tuple-element.197.refs_0_), channel_id=1, source_target_pairs={{0,8},{1,9},{2,10},{3,11},{4,12},{5,13},{6,14},{7,15},{8,0},{9,1},... | collective-permute-start | bytes 417800 | tf_op jit(solution)/shard_map/ppermute | solution.py:42
  221.8 17.7 %collective-permute-start.33 = (f32[136,256]{1,0:T(8,128)S(1)}, f32[136,256]{1,0:T(8,128)S(1)}, u32[]{:S(2)}, u32[]{:S(2)}) collective-permute-start(f32[136,256]{1,0:T(8,128)S(1)} %get-tuple-element.197.refs_0_), channel_id=1, source_target_pairs={{0,16},{1,17},{2,18},{3,19},{4,20},{5,21},{6,22},{7,23},{8,24},{9,... | collective-permute-start | bytes 417800 | tf_op jit(solution)/shard_map/ppermute | solution.py:42
  221.8 17.7 %collective-permute-start.34 = (f32[136,256]{1,0:T(8,128)S(1)}, f32[136,256]{1,0:T(8,128)S(1)}, u32[]{:S(2)}, u32[]{:S(2)}) collective-permute-start(f32[136,256]{1,0:T(8,128)S(1)} %get-tuple-element.197.refs_0_), channel_id=1, source_target_pairs={{0,24},{1,25},{2,26},{3,27},{4,28},{5,29},{6,30},{7,31},{8,16},{9,... | collective-permute-start | bytes 417800 | tf_op jit(solution)/shard_map/ppermute | solution.py:42
  240.7 6.0 %collective-permute-start.35 = (f32[128,256]{1,0:T(8,128)S(1)}, f32[128,256]{1,0:T(8,128)S(1)}, u32[]{:S(2)}, u32[]{:S(2)}) collective-permute-start(f32[128,256]{1,0:T(8,128)S(1)} %get-tuple-element.200), channel_id=1, source_target_pairs={{0,2},{1,3},{2,0},{3,1},{4,6},{5,7},{6,4},{7,5},{8,10},{9,11},{10,... | collective-permute-start | bytes 393224 | tf_op jit(solution)/shard_map/ppermute | solution.py:42
  242.0 6.8 %collective-permute-start.36 = (f32[128,256]{1,0:T(8,128)S(1)}, f32[128,256]{1,0:T(8,128)S(1)}, u32[]{:S(2)}, u32[]{:S(2)}) collective-permute-start(f32[128,256]{1,0:T(8,128)S(1)} %get-tuple-element.201), channel_id=1, source_target_pairs={{0,4},{1,5},{2,6},{3,7},{4,0},{5,1},{6,2},{7,3},{8,12},{9,13},{10,... | collective-permute-start | bytes 393224 | tf_op jit(solution)/shard_map/ppermute | solution.py:42
  243.5 6.7 %collective-permute-start.37 = (f32[128,256]{1,0:T(8,128)S(1)}, f32[128,256]{1,0:T(8,128)S(1)}, u32[]{:S(2)}, u32[]{:S(2)}) collective-permute-start(f32[128,256]{1,0:T(8,128)S(1)} %get-tuple-element.202), channel_id=1, source_target_pairs={{0,6},{1,7},{2,4},{3,5},{4,2},{5,3},{6,0},{7,1},{8,14},{9,15},{10,... | collective-permute-start | bytes 393224 | tf_op jit(solution)/shard_map/ppermute | solution.py:42
  291.0 179.4 %reduce-scatter.9.cloned.1.call-start = ((), (), s32[]{:S(2)}) async-start(), calls=%async_computation.6 | async-start | bytes 5603328 | tf_op jit(solution)/shard_map/reduce_scatter | solution.py:167
  307.2 10.6 %collective-permute-start.43 = (bf16[144,256]{1,0:T(8,128)(2,1)S(1)}, bf16[144,256]{1,0:T(8,128)(2,1)S(1)}, u32[]{:S(2)}, u32[]{:S(2)}) collective-permute-start(bf16[144,256]{1,0:T(8,128)(2,1)S(1)} %get-tuple-element.231), channel_id=1, source_target_pairs={{0,8},{1,9},{2,10},{3,11},{4,12},{5,13},{6,14},{7,15},{8,0},{9,1},... | collective-permute-start | bytes 221192 | tf_op jit(solution)/shard_map/ppermute | solution.py:42
  309.7 8.1 %collective-permute-start.44 = (bf16[144,256]{1,0:T(8,128)(2,1)S(1)}, bf16[144,256]{1,0:T(8,128)(2,1)S(1)}, u32[]{:S(2)}, u32[]{:S(2)}) collective-permute-start(bf16[144,256]{1,0:T(8,128)(2,1)S(1)} %get-tuple-element.231), channel_id=1, source_target_pairs={{0,16},{1,17},{2,18},{3,19},{4,20},{5,21},{6,22},{7,23},{8,24},{9,... | collective-permute-start | bytes 221192 | tf_op jit(solution)/shard_map/ppermute | solution.py:42
  309.7 8.1 %collective-permute-start.45 = (bf16[144,256]{1,0:T(8,128)(2,1)S(1)}, bf16[144,256]{1,0:T(8,128)(2,1)S(1)}, u32[]{:S(2)}, u32[]{:S(2)}) collective-permute-start(bf16[144,256]{1,0:T(8,128)(2,1)S(1)} %get-tuple-element.231), channel_id=1, source_target_pairs={{0,24},{1,25},{2,26},{3,27},{4,28},{5,29},{6,30},{7,31},{8,16},{9,... | collective-permute-start | bytes 221192 | tf_op jit(solution)/shard_map/ppermute | solution.py:42
  317.9 9.0 %collective-permute-start.46 = (bf16[128,256]{1,0:T(8,128)(2,1)S(1)}, bf16[128,256]{1,0:T(8,128)(2,1)S(1)}, u32[]{:S(2)}, u32[]{:S(2)}) collective-permute-start(bf16[128,256]{1,0:T(8,128)(2,1)S(1)} %get-tuple-element.234), channel_id=1, source_target_pairs={{0,2},{1,3},{2,0},{3,1},{4,6},{5,7},{6,4},{7,5},{8,10},{9,11},{10,... | collective-permute-start | bytes 196616 | tf_op jit(solution)/shard_map/ppermute | solution.py:42
  318.9 8.0 %collective-permute-start.47 = (bf16[128,256]{1,0:T(8,128)(2,1)S(1)}, bf16[128,256]{1,0:T(8,128)(2,1)S(1)}, u32[]{:S(2)}, u32[]{:S(2)}) collective-permute-start(bf16[128,256]{1,0:T(8,128)(2,1)S(1)} %get-tuple-element.235), channel_id=1, source_target_pairs={{0,4},{1,5},{2,6},{3,7},{4,0},{5,1},{6,2},{7,3},{8,12},{9,13},{10,... | collective-permute-start | bytes 196616 | tf_op jit(solution)/shard_map/ppermute | solution.py:42
  320.3 6.6 %collective-permute-start.48 = (bf16[128,256]{1,0:T(8,128)(2,1)S(1)}, bf16[128,256]{1,0:T(8,128)(2,1)S(1)}, u32[]{:S(2)}, u32[]{:S(2)}) collective-permute-start(bf16[128,256]{1,0:T(8,128)(2,1)S(1)} %get-tuple-element.236), channel_id=1, source_target_pairs={{0,6},{1,7},{2,4},{3,5},{4,2},{5,3},{6,0},{7,1},{8,14},{9,15},{10,... | collective-permute-start | bytes 196616 | tf_op jit(solution)/shard_map/ppermute | solution.py:42
  368.9 55.3 %collective-permute-start.62 = (bf16[4,4,128,1024]{3,2,1,0:T(8,128)(2,1)}, bf16[4,4,128,1024]{3,2,1,0:T(8,128)(2,1)}, u32[]{:S(2)}, u32[]{:S(2)}) collective-permute-start(bf16[4,4,128,1024]{3,2,1,0:T(8,128)(2,1)} %bitcast.37), channel_id=1, source_target_pairs={{0,1},{1,0},{2,3},{3,2},{4,5},{5,4},{6,7},{7,6},{8,9},{9,8},{10,11... | collective-permute-start | bytes 12582920 | tf_op jit(solution)/shard_map/ppermute | solution.py:42
  377.4 184.8 %reduce-scatter.11.cloned.1.call-start = ((), (), s32[]{:S(2)}) async-start(), calls=%async_computation.7 | async-start | bytes 778240 | tf_op jit(solution)/shard_map/reduce_scatter | solution.py:174
  393.3 9.9 %collective-permute-start.55 = (bf16[144,256]{1,0:T(8,128)(2,1)S(1)}, bf16[144,256]{1,0:T(8,128)(2,1)S(1)}, u32[]{:S(2)}, u32[]{:S(2)}) collective-permute-start(bf16[144,256]{1,0:T(8,128)(2,1)S(1)} %get-tuple-element.274), channel_id=1, source_target_pairs={{0,8},{1,9},{2,10},{3,11},{4,12},{5,13},{6,14},{7,15},{8,0},{9,1},... | collective-permute-start | bytes 221192 | tf_op jit(solution)/shard_map/ppermute | solution.py:42
  394.4 8.8 %collective-permute-start.56 = (bf16[144,256]{1,0:T(8,128)(2,1)S(1)}, bf16[144,256]{1,0:T(8,128)(2,1)S(1)}, u32[]{:S(2)}, u32[]{:S(2)}) collective-permute-start(bf16[144,256]{1,0:T(8,128)(2,1)S(1)} %get-tuple-element.274), channel_id=1, source_target_pairs={{0,16},{1,17},{2,18},{3,19},{4,20},{5,21},{6,22},{7,23},{8,24},{9,... | collective-permute-start | bytes 221192 | tf_op jit(solution)/shard_map/ppermute | solution.py:42
  395.5 7.7 %collective-permute-start.57 = (bf16[144,256]{1,0:T(8,128)(2,1)S(1)}, bf16[144,256]{1,0:T(8,128)(2,1)S(1)}, u32[]{:S(2)}, u32[]{:S(2)}) collective-permute-start(bf16[144,256]{1,0:T(8,128)(2,1)S(1)} %get-tuple-element.274), channel_id=1, source_target_pairs={{0,24},{1,25},{2,26},{3,27},{4,28},{5,29},{6,30},{7,31},{8,16},{9,... | collective-permute-start | bytes 221192 | tf_op jit(solution)/shard_map/ppermute | solution.py:42
  404.2 11.8 %collective-permute-start.58 = (bf16[128,256]{1,0:T(8,128)(2,1)S(1)}, bf16[128,256]{1,0:T(8,128)(2,1)S(1)}, u32[]{:S(2)}, u32[]{:S(2)}) collective-permute-start(bf16[128,256]{1,0:T(8,128)(2,1)S(1)} %get-tuple-element.277), channel_id=1, source_target_pairs={{0,2},{1,3},{2,0},{3,1},{4,6},{5,7},{6,4},{7,5},{8,10},{9,11},{10,... | collective-permute-start | bytes 196616 | tf_op jit(solution)/shard_map/ppermute | solution.py:42
  404.9 11.8 %collective-permute-start.59 = (bf16[128,256]{1,0:T(8,128)(2,1)S(1)}, bf16[128,256]{1,0:T(8,128)(2,1)S(1)}, u32[]{:S(2)}, u32[]{:S(2)}) collective-permute-start(bf16[128,256]{1,0:T(8,128)(2,1)S(1)} %get-tuple-element.278), channel_id=1, source_target_pairs={{0,4},{1,5},{2,6},{3,7},{4,0},{5,1},{6,2},{7,3},{8,12},{9,13},{10,... | collective-permute-start | bytes 196616 | tf_op jit(solution)/shard_map/ppermute | solution.py:42
  405.7 11.6 %collective-permute-start.60 = (bf16[128,256]{1,0:T(8,128)(2,1)S(1)}, bf16[128,256]{1,0:T(8,128)(2,1)S(1)}, u32[]{:S(2)}, u32[]{:S(2)}) collective-permute-start(bf16[128,256]{1,0:T(8,128)(2,1)S(1)} %get-tuple-element.279), channel_id=1, source_target_pairs={{0,6},{1,7},{2,4},{3,5},{4,2},{5,3},{6,0},{7,1},{8,14},{9,15},{10,... | collective-permute-start | bytes 196616 | tf_op jit(solution)/shard_map/ppermute | solution.py:42
  424.1 9.6 %collective-permute-start.61 = (bf16[128,1024]{1,0:T(8,128)(2,1)S(1)}, bf16[128,1024]{1,0:T(8,128)(2,1)S(1)}, u32[]{:S(2)}, u32[]{:S(2)}) collective-permute-start(bf16[128,1024]{1,0:T(8,128)(2,1)S(1)} %get-tuple-element.282), channel_id=1, source_target_pairs={{0,1},{1,0},{2,3},{3,2},{4,5},{5,4},{6,7},{7,6},{8,9},{9,8},{10,11... | collective-permute-start | bytes 786440 | tf_op jit(solution)/shard_map/ppermute | solution.py:42
  430.2 26.1 %collective-permute-start.64 = (bf16[4,128,1024]{2,1,0:T(8,128)(2,1)S(1)}, bf16[4,128,1024]{2,1,0:T(8,128)(2,1)S(1)}, u32[]{:S(2)}, u32[]{:S(2)}) collective-permute-start(bf16[4,128,1024]{2,1,0:T(8,128)(2,1)S(1)} %get-tuple-element.307.refs_27_), channel_id=1, source_target_pairs={{0,2},{1,3},{2,0},{3,1},{4,6},{5,7},{6,4},{7,5},{8,10},{9,11},{10,... | collective-permute-start | bytes 3145736 | tf_op jit(solution)/shard_map/ppermute | solution.py:42
  431.2 34.5 %collective-permute-start.65 = (bf16[4,128,1024]{2,1,0:T(8,128)(2,1)S(1)}, bf16[4,128,1024]{2,1,0:T(8,128)(2,1)S(1)}, u32[]{:S(2)}, u32[]{:S(2)}) collective-permute-start(bf16[4,128,1024]{2,1,0:T(8,128)(2,1)S(1)} %get-tuple-element.306.refs_28_), channel_id=1, source_target_pairs={{0,4},{1,5},{2,6},{3,7},{4,0},{5,1},{6,2},{7,3},{8,12},{9,13},{10,... | collective-permute-start | bytes 3145736 | tf_op jit(solution)/shard_map/ppermute | solution.py:42
  431.9 47.2 %collective-permute-start.66 = (bf16[4,128,1024]{2,1,0:T(8,128)(2,1)}, bf16[4,128,1024]{2,1,0:T(8,128)(2,1)}, u32[]{:S(2)}, u32[]{:S(2)}) collective-permute-start(bf16[4,128,1024]{2,1,0:T(8,128)(2,1)} %get-tuple-element.305.refs_29_), channel_id=1, source_target_pairs={{0,6},{1,7},{2,4},{3,5},{4,2},{5,3},{6,0},{7,1},{8,14},{9,15},{10,... | collective-permute-start | bytes 3145736 | tf_op jit(solution)/shard_map/ppermute | solution.py:42
  442.3 13.9 %collective-permute-start.63 = (bf16[16,2432]{1,0:T(8,128)(2,1)S(1)}, bf16[16,2432]{1,0:T(8,128)(2,1)S(1)}, u32[]{:S(2)}, u32[]{:S(2)}) collective-permute-start(bf16[16,2432]{1,0:T(8,128)(2,1)S(1)} %slice.342), channel_id=1, source_target_pairs={{1,0},{2,1},{3,2},{4,3},{5,4},{6,5},{7,6},{8,7},{9,8},{10,9},{11,1... | collective-permute-start | bytes 233480 | tf_op jit(solution)/shard_map/ppermute | solution.py:47
  448.4 33.6 %collective-permute-start.72 = (bf16[4,4,32,2432]{3,2,1,0:T(8,128)(2,1)}, bf16[4,4,32,2432]{3,2,1,0:T(8,128)(2,1)}, u32[]{:S(2)}, u32[]{:S(2)}) collective-permute-start(bf16[4,4,32,2432]{3,2,1,0:T(8,128)(2,1)} %bitcast.46), channel_id=1, source_target_pairs={{0,1},{1,0},{2,3},{3,2},{4,5},{5,4},{6,7},{7,6},{8,9},{9,8},{10,11... | collective-permute-start | bytes 7471112 | tf_op jit(solution)/shard_map/ppermute | solution.py:42
  468.3 6.1 %collective-permute-start.67 = (bf16[16,2304]{1,0:T(8,128)(2,1)S(1)}, bf16[16,2304]{1,0:T(8,128)(2,1)S(1)}, u32[]{:S(2)}, u32[]{:S(2)}) collective-permute-start(bf16[16,2304]{1,0:T(8,128)(2,1)S(1)} %shard_map.284.refs_0_), channel_id=1, source_target_pairs={{0,16},{1,17},{2,18},{3,19},{4,20},{5,21},{6,22},{7,23},{8,24},{9,... | collective-permute-start | bytes 221192 | tf_op jit(solution)/shard_map/ppermute | solution.py:42
  473.7 88.6 %reduce-scatter.7.cloned.1.call-start = ((), (), s32[]{:S(2)}) async-start(), calls=%async_computation.5 | async-start | bytes 1310720 | tf_op jit(solution)/shard_map/reduce_scatter | solution.py:174
  485.5 36.6 %collective-permute-start.73 = (bf16[4,32,2432]{2,1,0:T(8,128)(2,1)}, bf16[4,32,2432]{2,1,0:T(8,128)(2,1)S(1)}, u32[]{:S(2)}, u32[]{:S(2)}) collective-permute-start(bf16[4,32,2432]{2,1,0:T(8,128)(2,1)} %get-tuple-element.316), channel_id=1, source_target_pairs={{0,2},{1,3},{2,0},{3,1},{4,6},{5,7},{6,4},{7,5},{8,10},{9,11},{10,... | collective-permute-start | bytes 1867784 | tf_op jit(solution)/shard_map/ppermute | solution.py:42
  507.0 29.6 %collective-permute-start.74 = (bf16[4,32,2432]{2,1,0:T(8,128)(2,1)}, bf16[4,32,2432]{2,1,0:T(8,128)(2,1)}, u32[]{:S(2)}, u32[]{:S(2)}) collective-permute-start(bf16[4,32,2432]{2,1,0:T(8,128)(2,1)} %get-tuple-element.315), channel_id=1, source_target_pairs={{0,4},{1,5},{2,6},{3,7},{4,0},{5,1},{6,2},{7,3},{8,12},{9,13},{10,... | collective-permute-start | bytes 1867784 | tf_op jit(solution)/shard_map/ppermute | solution.py:42
  508.2 28.4 %collective-permute-start.75 = (bf16[4,32,2432]{2,1,0:T(8,128)(2,1)}, bf16[4,32,2432]{2,1,0:T(8,128)(2,1)}, u32[]{:S(2)}, u32[]{:S(2)}) collective-permute-start(bf16[4,32,2432]{2,1,0:T(8,128)(2,1)} %get-tuple-element.314), channel_id=1, source_target_pairs={{0,6},{1,7},{2,4},{3,5},{4,2},{5,3},{6,0},{7,1},{8,14},{9,15},{10,... | collective-permute-start | bytes 1867784 | tf_op jit(solution)/shard_map/ppermute | solution.py:42
  508.5 37.0 %collective-permute-start.69 = (bf16[128,1024]{1,0:T(8,128)(2,1)S(1)}, bf16[128,1024]{1,0:T(8,128)(2,1)S(1)}, u32[]{:S(2)}, u32[]{:S(2)}) collective-permute-start(bf16[128,1024]{1,0:T(8,128)(2,1)S(1)} %get-tuple-element.296), channel_id=1, source_target_pairs={{0,8},{1,9},{2,10},{3,11},{4,12},{5,13},{6,14},{7,15},{8,0},{9,1},... | collective-permute-start | bytes 786440 | tf_op jit(solution)/shard_map/ppermute | solution.py:42
  510.9 34.6 %collective-permute-start.70 = (bf16[128,1024]{1,0:T(8,128)(2,1)S(1)}, bf16[128,1024]{1,0:T(8,128)(2,1)S(1)}, u32[]{:S(2)}, u32[]{:S(2)}) collective-permute-start(bf16[128,1024]{1,0:T(8,128)(2,1)S(1)} %get-tuple-element.297), channel_id=1, source_target_pairs={{0,16},{1,17},{2,18},{3,19},{4,20},{5,21},{6,22},{7,23},{8,24},{9,... | collective-permute-start | bytes 786440 | tf_op jit(solution)/shard_map/ppermute | solution.py:42
  522.1 23.5 %collective-permute-start.71 = (bf16[128,1024]{1,0:T(8,128)(2,1)S(1)}, bf16[128,1024]{1,0:T(8,128)(2,1)S(1)}, u32[]{:S(2)}, u32[]{:S(2)}) collective-permute-start(bf16[128,1024]{1,0:T(8,128)(2,1)S(1)} %get-tuple-element.298), channel_id=1, source_target_pairs={{0,24},{1,25},{2,26},{3,27},{4,28},{5,29},{6,30},{7,31},{8,16},{9,... | collective-permute-start | bytes 786440 | tf_op jit(solution)/shard_map/ppermute | solution.py:42
  538.9 10.4 %collective-permute-start.76 = (bf16[32,2432]{1,0:T(8,128)(2,1)S(1)}, bf16[32,2432]{1,0:T(8,128)(2,1)S(1)}, u32[]{:S(2)}, u32[]{:S(2)}) collective-permute-start(bf16[32,2432]{1,0:T(8,128)(2,1)S(1)} %get-tuple-element.311), channel_id=1, source_target_pairs={{0,8},{1,9},{2,10},{3,11},{4,12},{5,13},{6,14},{7,15},{8,0},{9,1},... | collective-permute-start | bytes 466952 | tf_op jit(solution)/shard_map/ppermute | solution.py:42
  554.5 14.7 %collective-permute-start.77 = (bf16[32,2432]{1,0:T(8,128)(2,1)}, bf16[32,2432]{1,0:T(8,128)(2,1)S(1)}, u32[]{:S(2)}, u32[]{:S(2)}) collective-permute-start(bf16[32,2432]{1,0:T(8,128)(2,1)} %get-tuple-element.310), channel_id=1, source_target_pairs={{0,16},{1,17},{2,18},{3,19},{4,20},{5,21},{6,22},{7,23},{8,24},{9,... | collective-permute-start | bytes 466952 | tf_op jit(solution)/shard_map/ppermute | solution.py:42
  556.3 12.9 %collective-permute-start.78 = (bf16[32,2432]{1,0:T(8,128)(2,1)}, bf16[32,2432]{1,0:T(8,128)(2,1)S(1)}, u32[]{:S(2)}, u32[]{:S(2)}) collective-permute-start(bf16[32,2432]{1,0:T(8,128)(2,1)} %get-tuple-element.309), channel_id=1, source_target_pairs={{0,24},{1,25},{2,26},{3,27},{4,28},{5,29},{6,30},{7,31},{8,16},{9,... | collective-permute-start | bytes 466952 | tf_op jit(solution)/shard_map/ppermute | solution.py:42
  (245 other events, 1584.1 us)
Sparse Core Ops, SparseCore 0:
  27.3 118.7 all-gather.6
  148.9 92.3 all-gather.4
  291.1 74.0 reduce-scatter.4
  377.5 56.9 reduce-scatter.8
  473.8 41.9 reduce-scatter.10
  517.9 35.6 reduce-scatter.6
